TPU v7x, 32 devices: a whole 2x2x4 slice. The times are simulated.
32 devices in a mesh: dp: 8 (over y, x, core), mp: 4 (over z).
Axes of the slice: x: 2, y: 2, z: 4, core: 2. Of those that a mesh axis runs over, the one named last changes fastest.
Arguments:
- tokens: bfloat16 [8192, 2048], P('dp'), may hold values from -6 to 6
- cotangent: bfloat16 [8192, 2048], P('dp'), may hold values from -6 to 6
- doc_lengths: int32 [8, 5], P('dp'), may hold values from 1 to 1020, as said below
- w_z: float32 [2048, 4096], P('dp', 'mp'), may hold values from -0.125 to 0.125
- w_x: float32 [2048, 4096], P('dp', 'mp'), may hold values from -0.125 to 0.125
- w_bc: float32 [2048, 256], P('dp', 'mp'), may hold values from -0.125 to 0.125
- w_dt: float32 [2048, 64], P('dp', 'mp'), may hold values from -0.125 to 0.125
- w_out: float32 [4096, 2048], P('mp', 'dp'), may hold values from -0.09375 to 0.09375
- conv_x: float32 [4, 4096], P(None, 'mp'), may hold values from -3 to 3
- conv_x_bias: float32 [4096], P('mp'), may hold values from -3 to 3
- conv_bc: float32 [4, 256], P(None, 'mp'), may hold values from -3 to 3
- conv_bc_bias: float32 [256], P('mp'), may hold values from -3 to 3
- dt_bias: float32 [64], P('mp'), may hold values from -1 to 1
- a_rate: float32 [64], P('mp'), may hold values from 0.0001 to 0.04
- d_skip: float32 [64], P('mp'), may hold values from 0.5 to 1.5
- input_norm_gain: float32 [2048], replicated, may hold values from 0.25 to 1.75
- out_gain: float32 [4096], P('mp'), may hold values from 0.25 to 1.75
Outputs:
- output: bfloat16 [8192, 2048], P('dp', 'mp')
- input_grad: bfloat16 [8192, 2048], P('dp', 'mp')
- w_z_grad: float32 [2048, 4096], P('dp', 'mp')
- w_x_grad: float32 [2048, 4096], P('dp', 'mp')
- w_bc_grad: float32 [2048, 256], P('dp', 'mp')
- w_dt_grad: float32 [2048, 64], P('dp', 'mp')
- w_out_grad: float32 [4096, 2048], P('mp', 'dp')
- conv_x_grad: float32 [4, 4096], P(None, 'mp')
- conv_x_bias_grad: float32 [4096], P('mp')
- conv_bc_grad: float32 [4, 256], P(None, 'mp')
- conv_bc_bias_grad: float32 [256], P('mp')
- dt_bias_grad: float32 [64], P('mp')
- a_rate_grad: float32 [64], P('mp')
- d_skip_grad: float32 [64], P('mp')
- in_gain_grad: float32 [2048], P('mp')
- out_gain_grad: float32 [4096], P('mp')
Inputs may be any that keep to these rules, and one draw needn't show every extreme that they name: `doc_lengths`: row s lists the 5 documents of sequence s in order; they sum to 1024. The first two together and the last two together are each shorter than 256 tokens, so the third document starts within the first 256 tokens and ends within the last 256. Some row has a document of 1 token and a third document of 1020 tokens.
All inputs are finite; a program needn't handle non-finite values.
Results may differ from a plain program's by a relative error of at most 0.02.
The roundings to bfloat16 on the way count: a program that leaves them out, or rounds other values in their place, can miss the bound.
Values may be sent and summed in bfloat16 or wider, within the bound.
A program may use at most 320 MiB of HBM per device.

v0:
```python
import jax
import jax.numpy as jnp
from jax import lax
from jax.sharding import PartitionSpec as P

INNER = 4096
HEADDIM = 64
STATE = 128
CONV = 4
BLOCK = 256


eps_norm = 1e-05
exact = lax.Precision.HIGHEST


def entering(x, axis, combine, identity):
    size, place = (lax.axis_size(axis), lax.axis_index(axis))
    everything = jax.tree.map(
        lambda part, kind: lax.all_gather(part.astype(kind), axis), x, (jnp.bfloat16, jnp.bfloat16)
    )
    start = jax.tree.map(
        lambda part, zero: jnp.broadcast_to(jnp.asarray(zero, part.dtype), part.shape), x, identity
    )

    def step(k, before):
        reached = k < place
        new = combine(
            before, jax.tree.map(lambda part, own: part[k].astype(own.dtype), everything, x)
        )
        return jax.tree.map(lambda a, b: jnp.where(reached, a, b), new, before)

    return lax.fori_loop(0, size, step, start)


def entering_2(x, axis, combine, identity):
    size, place = (lax.axis_size(axis), lax.axis_index(axis))
    everything = jax.tree.map(
        lambda part, kind: lax.all_gather(part.astype(kind), axis),
        x,
        jax.tree.map(lambda a: jnp.bfloat16 if a.dtype == jnp.float32 else a.dtype, x),
    )
    start = jax.tree.map(
        lambda part, zero: jnp.broadcast_to(jnp.asarray(zero, part.dtype), part.shape), x, identity
    )

    def step(k, before):
        at = size - 1 - k
        reached = at > place
        new = combine(
            before, jax.tree.map(lambda part, own: part[at].astype(own.dtype), everything, x)
        )
        return jax.tree.map(lambda a, b: jnp.where(reached, a, b), new, before)

    return lax.fori_loop(0, size, step, start)


def document_marks(lengths, positions):
    starts = jnp.cumsum(lengths) - lengths
    doc_ids = jnp.sum((positions[:, None] >= starts[None, :]).astype(jnp.int32), axis=1) - 1
    resets = jnp.sum((positions[:, None] == starts[None, :]).astype(jnp.float32), axis=1)
    return (doc_ids, resets)


def causal_conv(values, conv_taps, conv_shift, doc_ids):
    row_count = values.shape[0]
    summed = conv_shift[None, :] + conv_taps[CONV - 1][None, :] * values
    for lag_steps in range(1, CONV):
        shifted_in = jnp.pad(values, ((lag_steps, 0), (0, 0)))[:row_count]
        earlier_doc = jnp.pad(doc_ids, (lag_steps, 0), constant_values=-1)[:row_count]
        summed = summed + conv_taps[CONV - 1 - lag_steps][None, :] * jnp.where(
            (earlier_doc == doc_ids)[:, None], shifted_in, 0.0
        )
    return jax.nn.silu(summed)


def block_step(carried, pieces):
    x_heads, b_rows, c_rows, dt_rows, decay_rows, reset_rows = pieces
    block_rows = reset_rows.shape[0]
    segment = jnp.cumsum(reset_rows)
    order_ids = jnp.arange(block_rows)
    linked = (segment[:, None] == segment[None, :]) & (order_ids[:, None] >= order_ids[None, :])
    decay_sum = jnp.cumsum(decay_rows, axis=0).T
    log_spans = decay_sum[:, :, None] - decay_sum[:, None, :]
    kernel = jnp.where(linked[None], jnp.exp(jnp.where(linked[None], log_spans, 0.0)), 0.0)
    scores = jnp.dot(
        c_rows.astype(jnp.bfloat16),
        b_rows.T.astype(jnp.bfloat16),
        preferred_element_type=jnp.float32,
    )
    mixing = kernel * scores[None] * dt_rows.T[:, None, :]
    y_rows = jnp.einsum("hij,jhp->ihp", mixing, x_heads, precision=exact)
    inflow = jnp.where((segment == 0)[None, :], jnp.exp(decay_sum), 0.0)
    y_rows = y_rows + inflow.T[:, :, None] * jnp.einsum(
        "in,hpn->ihp", c_rows, carried, precision=exact
    )
    ending = segment[block_rows - 1]
    leaving = (
        jnp.where(
            (segment == ending)[None, :], jnp.exp(decay_sum[:, block_rows - 1 :] - decay_sum), 0.0
        )
        * dt_rows.T
    )
    fresh_part = jnp.einsum("hj,jhp,jn->hpn", leaving, x_heads, b_rows, precision=exact)
    kept_part = jnp.where(ending == 0, jnp.exp(decay_sum[:, block_rows - 1]), 0.0)
    return (kept_part[:, None, None] * carried + fresh_part, y_rows)


def local_scan(seq_x, seq_bc, seq_dt, seq_decay, resets):
    token_count, inner_width = seq_x.shape
    head_count = seq_dt.shape[1]
    blocks = token_count // BLOCK
    pieces = (
        seq_x.reshape(blocks, BLOCK, head_count, inner_width // head_count),
        seq_bc[:, :STATE].reshape(blocks, BLOCK, STATE),
        seq_bc[:, STATE:].reshape(blocks, BLOCK, STATE),
        seq_dt.reshape(blocks, BLOCK, head_count),
        seq_decay.reshape(blocks, BLOCK, head_count),
        resets.reshape(blocks, BLOCK),
    )
    zero_state = jnp.zeros((head_count, inner_width // head_count, STATE), jnp.float32)
    ending, outputs = lax.scan(block_step, zero_state, pieces)
    factor = jnp.exp(jnp.sum(seq_decay, axis=0)) * (jnp.sum(resets) == 0).astype(jnp.float32)
    return (outputs.reshape(token_count, inner_width), ending, factor)


def carry_in(c_rows, seq_decay, resets, incoming):
    decay_sum = jnp.cumsum(seq_decay, axis=0)
    inflow = jnp.where((jnp.cumsum(resets) == 0)[:, None], jnp.exp(decay_sum), 0.0)
    reached = jnp.einsum("in,hpn->ihp", c_rows, incoming, precision=exact)
    return (inflow[:, :, None] * reached).reshape(c_rows.shape[0], -1)


def forward_combine(earlier, following):
    return (earlier[0] * following[0], following[0][:, None, None] * earlier[1] + following[1])


def backward_combine(earlier, following):
    return (earlier[0] * following[0], following[1] + following[0][:, None, None] * earlier[1])


def row_total(values):
    return lax.psum(values, "mp")


def feature_share(values):
    return lax.psum_scatter(
        values.astype(jnp.bfloat16), "mp", scatter_dimension=1, tiled=True
    ).astype(jnp.float32)


def silu_slope(values):
    logistic = jax.nn.sigmoid(values)
    return logistic * (1.0 + values * (1.0 - logistic))


def per_device(
    tokens,
    cotangent,
    doc_lengths,
    w_z,
    w_x,
    w_bc,
    w_dt,
    w_out,
    conv_x,
    conv_x_bias,
    conv_bc,
    conv_bc_bias,
    dt_bias,
    a_rate,
    d_skip,
    input_norm_gain,
    out_gain,
):
    group_size = lax.axis_size("mp")
    group_rank = lax.axis_index("mp")
    length = tokens.shape[0]
    shard_rows = length // group_size
    feature_width = tokens.shape[1] // group_size
    low_weights = (
        lax.all_gather(w_z.astype(jnp.bfloat16), "dp", axis=0, tiled=True),
        lax.all_gather(w_x.astype(jnp.bfloat16), "dp", axis=0, tiled=True),
        lax.all_gather(w_bc.astype(jnp.bfloat16), "dp", axis=0, tiled=True),
        lax.all_gather(w_dt.astype(jnp.bfloat16), "dp", axis=0, tiled=True),
        lax.all_gather(w_out.astype(jnp.bfloat16), "dp", axis=1, tiled=True),
    )
    full_z, full_x, full_bc, full_dt, full_out = low_weights
    lengths = doc_lengths[0]
    doc_ids, resets_all = document_marks(lengths, jnp.arange(length, dtype=jnp.int32))
    token_rows = tokens.astype(jnp.float32)
    inverse_root = lax.rsqrt(jnp.mean(token_rows * token_rows, axis=1, keepdims=True) + eps_norm)
    normalized_input = token_rows * inverse_root
    normed = (normalized_input * input_norm_gain).astype(jnp.bfloat16)
    gate_in = jnp.dot(normed, full_z, preferred_element_type=jnp.float32)
    x_in = jnp.dot(normed, full_x, preferred_element_type=jnp.float32)
    bc_in = jnp.dot(normed, full_bc, preferred_element_type=jnp.float32)
    dt_in = jnp.dot(normed, full_dt, preferred_element_type=jnp.float32)

    def conv_here(values, conv_taps, conv_shift):
        return causal_conv(values, conv_taps, conv_shift, doc_ids)

    x_conv, x_conv_pull = jax.vjp(conv_here, x_in, conv_x, conv_x_bias)
    bc_conv, bc_conv_pull = jax.vjp(conv_here, bc_in, conv_bc, conv_bc_bias)
    step_size = jax.nn.softplus(dt_in + dt_bias)
    decay_log = -a_rate * step_size
    x_low = x_conv.astype(jnp.bfloat16)
    bc_low = bc_conv.astype(jnp.bfloat16)
    x_low_f = x_low.astype(jnp.float32)
    sent_rows = (
        lax.all_to_all(x_low, "mp", split_axis=0, concat_axis=1, tiled=True),
        lax.all_to_all(bc_low, "mp", split_axis=0, concat_axis=1, tiled=True),
        lax.all_to_all(
            step_size.astype(jnp.bfloat16), "mp", split_axis=0, concat_axis=1, tiled=True
        ),
        lax.all_to_all(
            decay_log.astype(jnp.bfloat16), "mp", split_axis=0, concat_axis=1, tiled=True
        ),
    )
    seq_x = sent_rows[0].astype(jnp.float32)
    seq_bc = sent_rows[1].astype(jnp.float32)
    seq_dt = sent_rows[2].astype(jnp.float32)
    seq_decay = sent_rows[3].astype(jnp.float32)
    positions = group_rank * shard_rows + jnp.arange(shard_rows, dtype=jnp.int32)
    _, resets = document_marks(lengths, positions)

    def scan_here(values_x, values_bc, values_dt, values_decay):
        return local_scan(values_x, values_bc, values_dt, values_decay, resets)

    (ssd_local, end_local, factor), local_pull = jax.vjp(
        scan_here, seq_x, seq_bc, seq_dt, seq_decay
    )
    carried = entering(
        (factor, end_local),
        "mp",
        forward_combine,
        (jnp.ones_like(factor), jnp.zeros_like(end_local)),
    )
    state_in = carried[1]

    def carry_here(c_rows, values_decay, incoming):
        return carry_in(c_rows, values_decay, resets, incoming)

    ssd_carry, carry_pull = jax.vjp(carry_here, seq_bc[:, STATE:], seq_decay, state_in)
    back_heads = lax.all_to_all(
        (ssd_local + ssd_carry).astype(jnp.bfloat16), "mp", split_axis=1, concat_axis=0, tiled=True
    )
    ssd_low = back_heads.astype(jnp.float32)
    skip_rows = jnp.repeat(d_skip, HEADDIM)
    mixed_rows = ssd_low + skip_rows * x_low_f
    gate_act = jax.nn.silu(gate_in)
    gated = mixed_rows * gate_act
    inverse_out = lax.rsqrt(row_total(jnp.sum(gated * gated, axis=1)) / INNER + eps_norm)[:, None]
    gated_hat = gated * inverse_out
    gated_norm = (gated_hat * out_gain).astype(jnp.bfloat16)
    branch_part = jnp.dot(gated_norm, full_out, preferred_element_type=jnp.float32)
    branch_mine = feature_share(branch_part)
    own_rows = lax.dynamic_slice_in_dim(token_rows, group_rank * feature_width, feature_width, 1)
    output = (own_rows + branch_mine).astype(jnp.bfloat16)
    w_out_grad = jnp.einsum("tc,td->cd", gated_norm, cotangent, preferred_element_type=jnp.float32)
    grad_norm = jnp.einsum("td,cd->tc", cotangent, full_out, preferred_element_type=jnp.float32)
    out_gain_grad = jnp.sum(grad_norm * gated_hat, axis=0)
    grad_hat = grad_norm * out_gain
    inner_mean = row_total(jnp.sum(grad_hat * gated_hat, axis=1)) / INNER
    grad_gated = inverse_out * (grad_hat - gated_hat * inner_mean[:, None])
    grad_mixed = grad_gated * gate_act
    grad_gate = grad_gated * mixed_rows * silu_slope(gate_in)
    head_count = d_skip.shape[0]
    d_skip_grad = jnp.sum((grad_mixed * x_low_f).reshape(length, head_count, HEADDIM), axis=(0, 2))
    grad_ssd = grad_mixed.astype(jnp.bfloat16)
    seq_grad = lax.all_to_all(grad_ssd, "mp", split_axis=0, concat_axis=1, tiled=True).astype(
        jnp.float32
    )
    grad_c_in, grad_decay_in, grad_state_in = carry_pull(seq_grad)
    returned = entering_2(
        (factor, grad_state_in),
        "mp",
        backward_combine,
        (jnp.ones_like(factor), jnp.zeros_like(grad_state_in)),
    )
    state_out_grad = returned[1]
    factor_grad = jnp.sum(state_out_grad * state_in, axis=(1, 2))
    grad_sx, grad_sbc, grad_sdt, grad_sdecay = local_pull((seq_grad, state_out_grad, factor_grad))
    grad_sbc = grad_sbc + jnp.concatenate([jnp.zeros_like(grad_c_in), grad_c_in], axis=1)
    grad_sdecay = grad_sdecay + grad_decay_in
    arrived = (
        lax.all_to_all(grad_sx.astype(jnp.bfloat16), "mp", split_axis=1, concat_axis=0, tiled=True),
        lax.all_to_all(
            grad_sbc.astype(jnp.bfloat16), "mp", split_axis=1, concat_axis=0, tiled=True
        ),
        lax.all_to_all(
            grad_sdt.astype(jnp.bfloat16), "mp", split_axis=1, concat_axis=0, tiled=True
        ),
        lax.all_to_all(
            grad_sdecay.astype(jnp.bfloat16), "mp", split_axis=1, concat_axis=0, tiled=True
        ),
    )
    grad_x_ssd = arrived[0].astype(jnp.float32)
    grad_bc = arrived[1].astype(jnp.float32)
    grad_dt_ssd = arrived[2].astype(jnp.float32)
    grad_decay = arrived[3].astype(jnp.float32)
    grad_x_conv = grad_x_ssd + skip_rows * grad_mixed
    grad_x_in, conv_x_grad, conv_x_bias_grad = x_conv_pull(grad_x_conv)
    grad_bc_in, conv_bc_grad, conv_bc_bias_grad = bc_conv_pull(grad_bc)
    grad_step = grad_dt_ssd - a_rate * grad_decay
    a_rate_grad = -jnp.sum(grad_decay * step_size, axis=0)
    grad_dt_in = grad_step * jax.nn.sigmoid(dt_in + dt_bias)
    dt_bias_grad = jnp.sum(grad_dt_in, axis=0)
    low_gate = grad_gate.astype(jnp.bfloat16)
    low_x = grad_x_in.astype(jnp.bfloat16)
    low_bc = grad_bc_in.astype(jnp.bfloat16)
    low_dt = grad_dt_in.astype(jnp.bfloat16)
    w_z_grad = jnp.einsum("td,tc->dc", normed, low_gate, preferred_element_type=jnp.float32)
    w_x_grad = jnp.einsum("td,tc->dc", normed, low_x, preferred_element_type=jnp.float32)
    w_bc_grad = jnp.einsum("td,tc->dc", normed, low_bc, preferred_element_type=jnp.float32)
    w_dt_grad = jnp.einsum("td,tc->dc", normed, low_dt, preferred_element_type=jnp.float32)
    grad_normed = jnp.einsum("tc,dc->td", low_gate, full_z, preferred_element_type=jnp.float32)
    grad_normed = grad_normed + jnp.einsum(
        "tc,dc->td", low_x, full_x, preferred_element_type=jnp.float32
    )
    grad_normed = grad_normed + jnp.einsum(
        "tc,dc->td", low_bc, full_bc, preferred_element_type=jnp.float32
    )
    grad_normed = grad_normed + jnp.einsum(
        "tc,dc->td", low_dt, full_dt, preferred_element_type=jnp.float32
    )
    gradient_complete = lax.psum(grad_normed.astype(jnp.bfloat16), "mp").astype(jnp.float32)
    gain_full = jnp.sum(gradient_complete * normalized_input, axis=0)
    gradient_normalized_input = gradient_complete * input_norm_gain
    row_square_mean = jnp.mean(gradient_normalized_input * normalized_input, axis=1, keepdims=True)
    gradient_row_block = inverse_root * (
        gradient_normalized_input - normalized_input * row_square_mean
    )
    grad_own = lax.dynamic_slice_in_dim(
        gradient_row_block, group_rank * feature_width, feature_width, 1
    )
    in_gain_grad = lax.dynamic_slice_in_dim(gain_full, group_rank * feature_width, feature_width, 0)
    cot_own = lax.dynamic_slice_in_dim(
        cotangent, group_rank * feature_width, feature_width, 1
    ).astype(jnp.float32)
    input_grad = (cot_own + grad_own).astype(jnp.bfloat16)
    summed = (
        lax.psum_scatter(
            w_z_grad.astype(jnp.bfloat16), "dp", scatter_dimension=0, tiled=True
        ).astype(jnp.float32),
        lax.psum_scatter(
            w_x_grad.astype(jnp.bfloat16), "dp", scatter_dimension=0, tiled=True
        ).astype(jnp.float32),
        lax.psum_scatter(
            w_bc_grad.astype(jnp.bfloat16), "dp", scatter_dimension=0, tiled=True
        ).astype(jnp.float32),
        lax.psum_scatter(
            w_dt_grad.astype(jnp.bfloat16), "dp", scatter_dimension=0, tiled=True
        ).astype(jnp.float32),
        lax.psum_scatter(
            w_out_grad.astype(jnp.bfloat16), "dp", scatter_dimension=1, tiled=True
        ).astype(jnp.float32),
    )
    smalls = lax.psum(
        (
            conv_x_grad,
            conv_x_bias_grad,
            conv_bc_grad,
            conv_bc_bias_grad,
            dt_bias_grad,
            a_rate_grad,
            d_skip_grad,
            in_gain_grad,
            out_gain_grad,
        ),
        "dp",
    )
    return (
        output,
        input_grad,
        summed[0],
        summed[1],
        summed[2],
        summed[3],
        summed[4],
        smalls[0],
        smalls[1],
        smalls[2],
        smalls[3],
        smalls[4],
        smalls[5],
        smalls[6],
        smalls[7],
        smalls[8],
    )


def solution(mesh):
    return jax.shard_map(
        per_device,
        mesh=mesh,
        in_specs=(
            P("dp", None),
            P("dp", None),
            P("dp", None),
            P("dp", "mp"),
            P("dp", "mp"),
            P("dp", "mp"),
            P("dp", "mp"),
            P("mp", "dp"),
            P(None, "mp"),
            P("mp"),
            P(None, "mp"),
            P("mp"),
            P("mp"),
            P("mp"),
            P("mp"),
            P(),
            P("mp"),
        ),
        out_specs=(
            P("dp", "mp"),
            P("dp", "mp"),
            P("dp", "mp"),
            P("dp", "mp"),
            P("dp", "mp"),
            P("dp", "mp"),
            P("mp", "dp"),
            P(None, "mp"),
            P("mp"),
            P(None, "mp"),
            P("mp"),
            P("mp"),
            P("mp"),
            P("mp"),
            P("mp"),
            P("mp"),
        ),
        check_vma=False,
    )
```

profile of v0, /device:TPU:0, one launch (start us, length us, event | category | flops | bytes accessed | tf_op | source)
XLA Modules:
  0.0 986.3 jit_solution(16825052762362911858)
XLA Ops:
  11.1 10.5 %all_gather.33 = bf16[2048,16]{0,1:T(8,128)(2,1)S(1)} all-gather(bf16[256,16]{0,1:T(8,128)(2,1)S(1)} %convert_element_type.371), channel_id=1, replica_groups=mesh['dp'=8,'mp'=4] {'dp'}, dimensions={0}, use_global_device_ids=true | all-gather | bytes 73728 | tf_op jit(solution)/shard_map/all_gather | solution.py:185
  27.3 4.9 all-to-all-start
  33.3 16.7 %all-gather.9.cloned.1.call-done = bf16[2048,1024]{1,0:T(8,128)(2,1)} async-done(((bf16[256,1024]{1,0:T(8,128)(2,1)}), bf16[2048,1024]{1,0:T(8,128)(2,1)}) %all-gather.9.cloned.1.call-update) | async-done | bytes 4194320 | tf_op jit(solution)/shard_map/all_gather | solution.py:183
  49.9 9.9 %fusion.105 = f32[1024,1024]{1,0:T(8,128)} fusion(bf16[2048,1024]{1,0:T(8,128)(2,1)} %all-gather.9.cloned.1.call-done, f32[2048]{0:T(1024)S(1)} %copy-done.55, f32[1024]{0:T(1024)S(1)} %add_rsqrt_fusion.1, bf16[1024,2048]{1,0:T(8,128)(2,1)} %param.21), kind=kOutput, calls=%fused_computation.247 | convolution fusion | flops 4303355904 | bytes 12595200 | tf_op jit(solution)/shard_map/dot_general | solution.py:196
  59.9 4.6 all-to-all-start.2
  64.5 12.9 %multiply_convert_fusion.3 = (bf16[1024,1024]{1,0:T(8,128)(2,1)}, f32[1024,1024]{1,0:T(8,128)}) fusion(f32[1024,1024]{1,0:T(8,128)} %fusion.105, pred[1024]{0:T(1024)(128)(4,1)S(1)} %get-tuple-element.702, f32[1024]{0:T(1024)S(1)} %bitcast.304, pred[1024]{0:T(1024)(128)(4,1)S(1)} %get-tuple-element.701, f32[1024]{0:T(1024)S(1)} %bitcast.306, ...), kind=kLoop, calls=%fused_computation.90 | loop fusion | flops 16777216 | bytes 10509312 | tf_op jit(solution)/shard_map/convert_element_type | solution.py:207
  77.5 5.2 all-to-all-start.3
  84.6 9.8 all_gather.34
  94.5 3.7 fusion.106
  104.9 25.8 %all-to-all-done.3 = bf16[4,256,1024]{2,1,0:T(8,128)(2,1)S(1)} async-done(((bf16[4,256,1024]{2,1,0:T(8,128)(2,1)}), bf16[4,256,1024]{2,1,0:T(8,128)(2,1)S(1)}, u32[]{:S(2)}, u32[]{:S(2)}) %all-to-all-start.3) | async-done | bytes 2097184 | tf_op jit(solution)/shard_map/all_to_all | solution.py:211
  130.8 3.3 all-to-all-start.1
  140.0 4.0 add_convert_fusion.2
  148.1 9.3 all-gather.2
  158.1 3.7 fusion.67
  162.0 61.4 %all-gather.15.cloned.1.call-done = bf16[256,64,128]{2,1,0:T(8,128)(2,1)} async-done(((bf16[64,64,128]{2,1,0:T(8,128)(2,1)}), bf16[256,64,128]{2,1,0:T(8,128)(2,1)}) %all-gather.15.cloned.1.call-update) | async-done | bytes 4194320 | tf_op jit(solution)/shard_map/all_gather | solution.py:20
  223.4 9.9 %while.22 = (s32[]{:T(128)}, f32[64,64,128]{2,1,0:T(8,128)S(1)}, s32[]{:T(128)}, bf16[4,64]{1,0:T(4,128)(2,1)}, bf16[4,64,64,128]{3,2,1,0:T(8,128)(2,1)}, /*index=5*/s32[]{:T(128)}, s32[]{:T(128)}) while((s32[]{:T(128)}, f32[64,64,128]{2,1,0:T(8,128)S(1)}, s32[]{:T(128)}, bf16[4,64]{1,0:T(4,128)(2,1)}, ...), condition=%wide.region_11.12_spmd.clone, body=%wide.region_10.11_spmd.clone.sunk | while | flops 2621508 | bytes 5243625 | solution.py:33
  236.2 14.6 %fusion.42 = bf16[256,64,64]{0,2,1:T(8,128)(2,1)} fusion(f32[256,64,64]{0,2,1:T(8,128)S(1)} %fusion.88, f32[256,64,64]{0,2,1:T(8,128)S(1)} %copy-done.11, bf16[256,64,64]{0,2,1:T(8,128)(2,1)S(1)} %bitcast.269, f32[64,256]{1,0:T(8,128)S(1)} %bitcast.294, f32[256,256]{1,0:T(8,128)S(1)} %fusion.89, f32[64,256]{1,0:T(8,128)S(1)} %copy-done.31, ...), kind=kOutput, calls=%fused_computation.70 | convolution fusion | flops 3247439872 | bytes 13107200 | tf_op jit(solution)/shard_map/jvp()/while/body/eval_jaxpr/hij,jhp->ihp/dot_general | solution.py:92
  250.8 4.0 copy.181
  254.8 4.5 all-to-all-start.4
  261.2 46.7 %all-to-all-done.4 = bf16[256,4,1024]{2,0,1:T(8,128)(2,1)} async-done(((bf16[256,4,1024]{2,0,1:T(8,128)(2,1)}), bf16[256,4,1024]{2,0,1:T(8,128)(2,1)}, u32[]{:S(2)}, u32[]{:S(2)}) %all-to-all-start.4) | async-done | bytes 2097184 | tf_op jit(solution)/shard_map/all_to_all | solution.py:245
  307.9 13.0 %multiply_reduce_fusion.10 = (f32[1024]{0:T(1024)S(1)}, f32[1024,1024]{1,0:T(8,128)}, f32[1024,1024]{1,0:T(8,128)}) fusion(bf16[1024,1024]{1,0:T(8,128)(2,1)} %get-tuple-element.677, f32[1024]{0:T(1024)S(1)} %mul.695, bf16[256,4,1024]{2,0,1:T(8,128)(2,1)} %all-to-all-done.4, bf16[2048,1024]{1,0:T(8,128)(2,1)} %all-gather.11.cloned.1.call-done, ...), kind=kOutput, calls=%fused_computation.84 | convolution fusion | flops 4314889216 | bytes 20992000 | tf_op jit(solution)/shard_map/dot_general | solution.py:195
  320.9 9.8 psum.84
  330.7 12.0 %multiply_reduce_fusion.4 = (f32[1024]{0:T(1024)}, f32[1024]{0:T(1024)S(1)}, f32[1024,1024]{1,0:T(8,128)}) fusion(f32[1024,1024]{1,0:T(8,128)} %get-tuple-element.672, f32[1024]{0:T(1024)S(1)} %add_rsqrt_fusion, f32[1024]{0:T(1024)S(1)} %copy-done.71, bf16[1024,2048]{1,0:T(8,128)(2,1)} %param.22, bf16[1024,2048]{1,0:T(8,128)(2,1)} %all-gather.13.cloned.1.call-done), kind=kOutput, calls=%fused_computation.71 | convolution fusion | flops 4301256704 | bytes 16793600 | tf_op jit(solution)/shard_map/td,cd->tc/dot_general | solution.py:261
  342.7 8.9 psum.85
  351.7 9.3 fusion.34
  361.3 47.4 %all_to_all.139 = bf16[4,256,1024]{2,1,0:T(8,128)(2,1)} all-to-all(bf16[4,256,1024]{2,1,0:T(8,128)(2,1)S(1)} %bitcast.272), channel_id=1, replica_groups=mesh['dp'=8,'mp'=4] {'mp'}, dimensions={0} | all-to-all | bytes 4194304 | tf_op jit(solution)/shard_map/all_to_all | solution.py:271
  408.7 4.0 copy.182
  412.6 4.7 fusion.59
  417.5 10.3 %convolution_convert_fusion = bf16[1024,2048]{1,0:T(8,128)(2,1)} fusion(bf16[1024,2048]{1,0:T(8,128)(2,1)} %param.22, f32[1024,1024]{1,0:T(8,128)} %get-tuple-element.672, f32[1024]{0:T(1024)S(1)} %copy-done.71, f32[1024]{0:T(1024)S(1)} %add_rsqrt_fusion), kind=kOutput, calls=%fused_computation.94 | convolution fusion | flops 4300210176 | bytes 12591104 | tf_op jit(solution)/shard_map/tc,td->cd/dot_general | solution.py:260
  427.8 9.7 convolution_convert_fusion.2
  440.1 5.4 copy.184
  446.2 10.0 %convolution_convert_fusion.3 = bf16[1024,2048]{1,0:T(8,128)(2,1)} fusion(bf16[1024,2048]{1,0:T(8,128)(2,1)} %all-gather.13.cloned.1.call-done, f32[1024,1024]{1,0:T(8,128)} %get-tuple-element.672, f32[1024]{0:T(1024)S(1)} %copy-done.71, f32[1024]{0:T(1024)S(1)} %add_rsqrt_fusion), kind=kOutput, calls=%fused_computation.97 | convolution fusion | flops 4300210176 | bytes 12591104 | tf_op jit(solution)/shard_map/dot_general | solution.py:256
  456.2 13.7 %fusion.10 = (f32[64,256]{1,0:T(8,128)S(1)}, f32[64,256]{1,0:T(8,128)S(1)}, f32[64,256]{1,0:T(8,128)S(1)}, bf16[256,256]{1,0:T(8,128)(2,1)S(1)}) fusion(f32[64,256]{1,0:T(8,128)S(1)} %bitcast.295, f32[256,256]{1,0:T(8,128)S(1)} %fusion.89, f32[64,256]{1,0:T(8,128)S(1)} %copy-done.31, pred[256,256]{1,0:T(8,128)(4,1)S(1)} %fusion.78, ...), kind=kOutput, calls=%fused_computation.18 | convolution fusion | flops 599670784 | bytes 4980736 | tf_op jit(solution)/shard_map/transpose(jvp())/while/body/eval_jaxpr/hij,jhp->ihp/dot_general | solution.py:92
  475.9 5.8 copy.185
  482.2 6.3 fusion.61
  491.5 5.9 all-gather.17.cloned.1.call-done
  497.3 17.1 %while.23 = (s32[]{:T(128)}, f32[64,64,128]{2,1,0:T(8,128)}, s32[]{:T(128)}, bf16[4,64,64,128]{3,2,1,0:T(8,128)(2,1)}, bf16[4,64]{1,0:T(4,128)(2,1)}, /*index=5*/s32[]{:T(128)}, s32[]{:T(128)}, s32[]{:T(128)}, s32[]{:T(128)}) while((s32[]{:T(128)}, f32[64,64,128]{2,1,0:T(8,128)}, s32[]{:T(128)}, ...), condition=%wide.region_18.19_spmd.clone, body=%wide.region_17.18_spmd.clone.sunk | while | flops 2621512 | bytes 5243687 | solution.py:55
  501.6 3.6 fusion.151
  505.9 4.0 fusion.151
  510.6 3.9 fusion.151
  514.4 6.1 fusion.39
  532.7 3.3 all-to-all-start.9
  536.0 6.2 fusion.62
  542.9 5.0 all-to-all-start.8
  549.6 4.0 all-to-all-done.8
  553.6 3.3 all-to-all-start.7
  557.0 14.5 %fusion.40 = bf16[256,64,64]{0,2,1:T(8,128)(2,1)} fusion(f32[256,64,64]{0,2,1:T(8,128)} %get-tuple-element.713, bf16[64,64,256]{2,1,0:T(8,128)(2,1)S(1)} %bitcast.263, f32[64,256]{1,0:T(8,128)} %bitcast.293, f32[256,256]{1,0:T(8,128)} %copy-done.35, f32[64,256]{1,0:T(8,128)} %copy-done.30, pred[256,256]{1,0:T(8,128)(4,1)} %copy-done.38, f32[256,64]{0,1:T(8,128)} %copy.179), kind=kOutput, calls=%fused_computation.67 | convolution fusion | flops 3245342720 | bytes 8912896 | tf_op jit(solution)/shard_map/transpose(jvp())/while/body/eval_jaxpr/hij,jhp->ihp/dot_general | solution.py:92
  571.4 4.0 copy.183
  575.4 5.0 all-to-all-start.6
  580.7 10.8 %fusion.114 = f32[1024,2048]{1,0:T(8,128)} fusion(bf16[1024,1024]{1,0:T(8,128)(2,1)} %get-tuple-element.679, bf16[2048,1024]{1,0:T(8,128)(2,1)} %all-gather.11.cloned.1.call-done), kind=kOutput, calls=%fused_computation.252 | convolution fusion | flops 4294967296 | bytes 14680064 | tf_op jit(solution)/shard_map/tc,dc->td/dot_general | solution.py:317
  598.3 4.5 fusion.116
  602.8 54.4 %all-to-all-done.6 = bf16[256,4,1024]{2,0,1:T(8,128)(2,1)S(1)} async-done(((bf16[256,4,1024]{2,0,1:T(8,128)(2,1)}), bf16[256,4,1024]{2,0,1:T(8,128)(2,1)S(1)}, u32[]{:S(2)}, u32[]{:S(2)}) %all-to-all-start.6) | async-done | bytes 2097184 | tf_op jit(solution)/shard_map/all_to_all | solution.py:287
  657.2 12.6 %multiply_reduce_fusion.8 = (f32[1024]{0:T(1024)S(1)}, f32[1024]{0:T(1024)S(1)}, f32[1024]{0:T(1024)S(1)}, f32[1024]{0:T(1024)S(1)}, f32[1024]{0:T(1024)S(1)}, /*index=5*/f32[1024,1024]{1,0:T(8,128)S(1)}) fusion(f32[1024,1024]{1,0:T(8,128)} %fusion.105, pred[1024]{0:T(1024)(128)(4,1)S(1)} %copy-done.44, pred[1024]{0:T(1024)(128)(4,1)S(1)} %copy-done.40, ...), kind=kLoop, calls=%fused_computation.75 | loop fusion | flops 25160704 | bytes 18902016 | tf_op jit(solution)/shard_map/transpose(jvp())/reduce_sum | solution.py:71
  673.4 9.2 fusion.115
  682.7 7.0 add_convert_fusion
  690.0 9.0 convolution_convert_fusion.1
  699.1 6.5 convert_element_type.368
  713.2 15.3 %reduce-scatter.15.cloned.1.call-done = bf16[256,16]{0,1:T(8,128)(2,1)} async-done(((bf16[2048,16]{0,1:T(8,128)(2,1)}), bf16[256,16]{0,1:T(8,128)(2,1)}) %reduce-scatter.15.cloned.1.call-update) | async-done | bytes 8208 | tf_op jit(solution)/shard_map/reduce_scatter | solution.py:352
  729.8 35.8 %reduce-scatter.13.cloned.1.call-done = bf16[256,64]{0,1:T(8,128)(2,1)} async-done(((bf16[2048,64]{0,1:T(8,128)(2,1)}), bf16[256,64]{0,1:T(8,128)(2,1)}) %reduce-scatter.13.cloned.1.call-update) | async-done | bytes 32784 | tf_op jit(solution)/shard_map/reduce_scatter | solution.py:349
  767.0 156.1 %all-reduce.31.cloned.1.call-done = bf16[1024,2048]{1,0:T(8,128)(2,1)} async-done(((bf16[1024,2048]{1,0:T(8,128)(2,1)}), bf16[1024,2048]{1,0:T(8,128)(2,1)}) %all-reduce.31.cloned.1.call-update) | async-done | bytes 4194320 | tf_op jit(solution)/shard_map/psum | solution.py:327
  923.1 9.5 fusion.11
  932.7 25.0 %all-reduce.28 = (f32[4,1024]{1,0:T(4,128)}, f32[1024]{0:T(1024)}, f32[4,64]{1,0:T(4,128)}, f32[64]{0:T(128)}, f32[16]{0:T(128)}, /*index=5*/f32[16]{0:T(128)}, f32[16]{0:T(128)}, f32[512]{0:T(512)}, f32[1024]{0:T(1024)}) all-reduce(f32[4,1024]{1,0:T(4,128)S(1)} %pad_add_fusion, ...), channel_id=1, replica_groups=mesh['dp'=8,'mp'=4] {'dp'}, use_global_device_ids=true, to_apply=%region_43.44 | all-reduce | flops 7024 | bytes 56192 | tf_op jit(solution)/shard_map/psum | solution.py:359
  957.7 3.9 fusion.53
  961.6 15.2 %reduce-scatter.11.cloned.1.call-done = bf16[256,1024]{1,0:T(8,128)(2,1)} async-done(((bf16[2048,1024]{1,0:T(8,128)(2,1)}), bf16[256,1024]{1,0:T(8,128)(2,1)}) %reduce-scatter.11.cloned.1.call-update) | async-done | bytes 524304 | tf_op jit(solution)/shard_map/reduce_scatter | solution.py:346
  (331 shorter events, 99.5 us)
Async XLA Ops:
  7.2 17.6 %copy-start.76 = (f32[16]{0:T(128)S(1)}, f32[16]{0:T(128)}, u32[]{:S(2)}) copy-start(f32[16]{0:T(128)} %param.33) | copy-start | bytes 196
  7.2 17.6 %copy-start.55 = (f32[2048]{0:T(1024)S(1)}, f32[2048]{0:T(1024)}, u32[]{:S(2)}) copy-start(f32[2048]{0:T(1024)} %param.36) | copy-start | bytes 24580
  7.2 42.7 %all-gather.9.cloned.1.call-start = ((), (), s32[]{:S(2)}) async-start(), calls=%async_computation.16 | async-start | bytes 4718592 | tf_op jit(solution)/shard_map/all_gather | solution.py:183
  9.4 15.4 %copy-start = (bf16[1024,2048]{1,0:T(8,128)(2,1)S(1)}, bf16[1024,2048]{1,0:T(8,128)(2,1)}, u32[]{:S(2)}) copy-start(bf16[1024,2048]{1,0:T(8,128)(2,1)} %param.21) | copy-start | bytes 12582916
  27.3 32.6 %all-to-all-start = ((bf16[4,256,16]{1,2,0:T(8,128)(2,1)}), bf16[4,256,16]{1,2,0:T(8,128)(2,1)S(1)}, u32[]{:S(2)}, u32[]{:S(2)}) async-start(bf16[4,256,16]{1,2,0:T(8,128)(2,1)} %bitcast.247), calls=%async_computation | async-start | bytes 65536 | tf_op jit(solution)/shard_map/all_to_all | solution.py:216
  33.2 65.0 %copy-start.39 = (pred[1024]{0:T(1024)(128)(4,1)}, pred[1024]{0:T(1024)(128)(4,1)S(1)}, u32[]{:S(2)}) copy-start(pred[1024]{0:T(1024)(128)(4,1)S(1)} %get-tuple-element.700) | copy-start | bytes 3076
  33.2 65.0 %copy-start.41 = (pred[1024]{0:T(1024)(128)(4,1)}, pred[1024]{0:T(1024)(128)(4,1)S(1)}, u32[]{:S(2)}) copy-start(pred[1024]{0:T(1024)(128)(4,1)S(1)} %get-tuple-element.701) | copy-start | bytes 3076
  33.2 65.0 %copy-start.43 = (pred[1024]{0:T(1024)(128)(4,1)}, pred[1024]{0:T(1024)(128)(4,1)S(1)}, u32[]{:S(2)}) copy-start(pred[1024]{0:T(1024)(128)(4,1)S(1)} %get-tuple-element.702) | copy-start | bytes 3076
  33.2 31.3 %copy-start.45 = (f32[1,1024]{1,0:T(1,128)}, f32[1,1024]{1,0:T(1,128)S(1)}, u32[]{:S(2)}) copy-start(f32[1,1024]{1,0:T(1,128)S(1)} %get-tuple-element.696) | copy-start | bytes 12292
  33.2 31.3 %copy-start.47 = (f32[1,1024]{1,0:T(1,128)}, f32[1,1024]{1,0:T(1,128)S(1)}, u32[]{:S(2)}) copy-start(f32[1,1024]{1,0:T(1,128)S(1)} %get-tuple-element.697) | copy-start | bytes 12292
  33.2 31.2 %copy-start.49 = (f32[1,1024]{1,0:T(1,128)}, f32[1,1024]{1,0:T(1,128)S(1)}, u32[]{:S(2)}) copy-start(f32[1,1024]{1,0:T(1,128)S(1)} %get-tuple-element.698) | copy-start | bytes 12292
  33.2 31.2 %copy-start.51 = (f32[1,1024]{1,0:T(1,128)}, f32[1,1024]{1,0:T(1,128)S(1)}, u32[]{:S(2)}) copy-start(f32[1,1024]{1,0:T(1,128)S(1)} %get-tuple-element.699) | copy-start | bytes 12292
  33.3 31.2 %copy-start.69 = (f32[1024]{0:T(1024)S(1)}, f32[1024]{0:T(1024)}, u32[]{:S(2)}) copy-start(f32[1024]{0:T(1024)} %param.30) | copy-start | bytes 12292
  59.9 42.0 %copy-start.26 = (bf16[4,256,16]{1,2,0:T(8,128)(2,1)}, bf16[4,256,16]{1,2,0:T(8,128)(2,1)S(1)}, u32[]{:S(2)}) copy-start(bf16[4,256,16]{1,2,0:T(8,128)(2,1)S(1)} %all-to-all-done) | copy-start | bytes 98308
  59.9 17.6 %all-to-all-start.2 = ((bf16[4,256,16]{1,2,0:T(8,128)(2,1)}), bf16[4,256,16]{1,2,0:T(8,128)(2,1)S(1)}, u32[]{:S(2)}, u32[]{:S(2)}) async-start(bf16[4,256,16]{1,2,0:T(8,128)(2,1)} %bitcast.246), calls=%async_computation.2 | async-start | bytes 65536 | tf_op jit(solution)/shard_map/all_to_all | solution.py:213
  77.5 16.9 %copy-start.72 = (f32[4,64]{1,0:T(4,128)S(1)}, f32[4,64]{1,0:T(4,128)}, u32[]{:S(2)}) copy-start(f32[4,64]{1,0:T(4,128)} %param.31) | copy-start | bytes 3076
  77.5 53.3 %all-to-all-start.3 = ((bf16[4,256,1024]{2,1,0:T(8,128)(2,1)}), bf16[4,256,1024]{2,1,0:T(8,128)(2,1)S(1)}, u32[]{:S(2)}, u32[]{:S(2)}) async-start(bf16[4,256,1024]{2,1,0:T(8,128)(2,1)} %bitcast.22), calls=%async_computation.3 | async-start | bytes 4194304 | tf_op jit(solution)/shard_map/all_to_all | solution.py:211
  84.0 20.1 %copy-start.60 = (pred[256]{0:T(512)(128)(4,1)}, pred[256]{0:T(512)(128)(4,1)S(1)}, u32[]{:S(2)}) copy-start(pred[256]{0:T(512)(128)(4,1)S(1)} %get-tuple-element.673) | copy-start | bytes 772
  101.9 33.0 %copy-start.56 = (pred[256]{0:T(512)(128)(4,1)}, pred[256]{0:T(512)(128)(4,1)S(1)}, u32[]{:S(2)}) copy-start(pred[256]{0:T(512)(128)(4,1)S(1)} %broadcast_compare_fusion) | copy-start | bytes 772
  103.0 41.1 %copy-start.16 = (f32[64,256]{0,1:T(8,128)}, f32[64,256]{0,1:T(8,128)S(1)}, u32[]{:S(2)}) copy-start(f32[64,256]{0,1:T(8,128)S(1)} %copy.174) | copy-start | bytes 196612
  103.6 27.2 %copy-start.18 = (f32[256,64]{1,0:T(8,128)}, f32[256,64]{1,0:T(8,128)S(1)}, u32[]{:S(2)}) copy-start(f32[256,64]{1,0:T(8,128)S(1)} %copy.171) | copy-start | bytes 196612
  104.1 30.8 %copy-start.58 = (f32[64]{0:T(128)}, f32[64]{0:T(128)S(1)}, u32[]{:S(2)}) copy-start(f32[64]{0:T(128)S(1)} %slice_bitcast_fusion.11) | copy-start | bytes 772
  130.8 9.2 all-to-all-start.1
  134.1 89.3 %all-gather.15.cloned.1.call-start = ((), (), s32[]{:S(2)}) async-start(), calls=%async_computation.26 | async-start | bytes 5242880 | tf_op jit(solution)/shard_map/all_gather | solution.py:20
  134.9 9.2 copy-start.25
  137.9 9.3 copy-start.7
  144.0 117.1 %all-gather.11.cloned.1.call-start = ((), (), s32[]{:S(2)}) async-start(), calls=%async_computation.17 | async-start | bytes 4718592 | tf_op jit(solution)/shard_map/all_gather | solution.py:182
  145.0 185.7 %all-gather.13.cloned.1.call-start = ((), (), s32[]{:S(2)}) async-start(), calls=%async_computation.18 | async-start | bytes 4718592 | tf_op jit(solution)/shard_map/all_gather | solution.py:186
  147.3 308.9 %copy-start.38 = (pred[256,256]{1,0:T(8,128)(4,1)}, pred[256,256]{1,0:T(8,128)(4,1)S(1)}, u32[]{:S(2)}) copy-start(pred[256,256]{1,0:T(8,128)(4,1)S(1)} %fusion.78) | copy-start | bytes 196612
  162.0 294.2 %copy-start.35 = (f32[256,256]{1,0:T(8,128)}, f32[256,256]{1,0:T(8,128)S(1)}, u32[]{:S(2)}) copy-start(f32[256,256]{1,0:T(8,128)S(1)} %fusion.89) | copy-start | bytes 786436
  223.4 11.9 %copy-start.33 = (f32[4,256,16]{1,2,0:T(8,128)S(1)}, f32[4,256,16]{1,2,0:T(8,128)}, u32[]{:S(2)}) copy-start(f32[4,256,16]{1,2,0:T(8,128)} %copy-done.32) | copy-start | bytes 196612
  235.2 15.6 %copy-start.13 = (f32[256,64,64]{0,2,1:T(8,128)}, f32[256,64,64]{0,2,1:T(8,128)S(1)}, u32[]{:S(2)}) copy-start(f32[256,64,64]{0,2,1:T(8,128)S(1)} %fusion.88) | copy-start | bytes 12582916
  254.8 53.1 %all-to-all-start.4 = ((bf16[256,4,1024]{2,0,1:T(8,128)(2,1)}), bf16[256,4,1024]{2,0,1:T(8,128)(2,1)}, u32[]{:S(2)}, u32[]{:S(2)}) async-start(bf16[256,4,1024]{2,0,1:T(8,128)(2,1)} %copy.181), calls=%async_computation.4 | async-start | bytes 4194304 | tf_op jit(solution)/shard_map/all_to_all | solution.py:245
  259.3 238.0 %all-gather.17.cloned.1.call-start = ((), (), s32[]{:S(2)}) async-start(), calls=%async_computation.27 | async-start | bytes 5242880 | tf_op jit(solution)/shard_map/all_gather | solution.py:39
  259.9 70.8 %copy-start.71 = (f32[1024]{0:T(1024)S(1)}, f32[1024]{0:T(1024)}, u32[]{:S(2)}) copy-start(f32[1024]{0:T(1024)} %param.37) | copy-start | bytes 12292
  361.0 47.7 %copy-start.3 = (f32[1024,1024]{1,0:T(8,128)}, f32[1024,1024]{1,0:T(8,128)S(1)}, u32[]{:S(2)}) copy-start(f32[1024,1024]{1,0:T(8,128)S(1)} %get-tuple-element.666) | copy-start | bytes 12582916
  417.4 288.4 %reduce-scatter.17.cloned.1.call-start = ((), (), s32[]{:S(2)}) async-start(), calls=%async_computation.25 | async-start | bytes 4718592 | tf_op jit(solution)/shard_map/reduce_scatter | solution.py:355
  427.8 280.1 %reduce-scatter.9.cloned.1.call-start = ((), (), s32[]{:S(2)}) async-start(), calls=%async_computation.21 | async-start | bytes 4718592 | tf_op jit(solution)/shard_map/reduce_scatter | solution.py:343
  437.6 272.4 %reduce-scatter.7.cloned.1.call-start = ((), (), s32[]{:S(2)}) async-start(), calls=%async_computation.19 | async-start | bytes 5242880 | tf_op jit(solution)/shard_map/reduce_scatter | solution.py:147
  456.2 14.1 %copy-start.4 = (bf16[256,4,1024]{0,2,1:T(8,128)(2,1)S(1)}, bf16[256,4,1024]{0,2,1:T(8,128)(2,1)}, u32[]{:S(2)}) copy-start(bf16[256,4,1024]{0,2,1:T(8,128)(2,1)} %copy.182) | copy-start | bytes 6291460
  456.2 14.1 %copy-start.12 = (f32[256,64,64]{0,2,1:T(8,128)S(1)}, f32[256,64,64]{0,2,1:T(8,128)}, u32[]{:S(2)}) copy-start(f32[256,64,64]{0,2,1:T(8,128)} %fusion.67) | copy-start | bytes 12582916
  456.2 14.1 %copy-start.14 = (f32[256,64,64]{0,2,1:T(8,128)S(1)}, f32[256,64,64]{0,2,1:T(8,128)}, u32[]{:S(2)}) copy-start(f32[256,64,64]{0,2,1:T(8,128)} %copy-done.13) | copy-start | bytes 12582916
  524.0 33.0 %copy-start.5 = (bf16[256,4,1024]{0,2,1:T(8,128)(2,1)S(1)}, bf16[256,4,1024]{0,2,1:T(8,128)(2,1)}, u32[]{:S(2)}) copy-start(bf16[256,4,1024]{0,2,1:T(8,128)(2,1)} %copy.182) | copy-start | bytes 6291460
  525.6 16.6 %copy-start.34 = (bf16[256,64]{1,0:T(8,128)(2,1)S(1)}, bf16[256,64]{1,0:T(8,128)(2,1)}, u32[]{:S(2)}) copy-start(bf16[256,64]{1,0:T(8,128)(2,1)} %get-tuple-element.686) | copy-start | bytes 98308
  532.7 10.2 %all-to-all-start.9 = ((bf16[256,4,16]{0,2,1:T(8,128)(2,1)}), bf16[256,4,16]{0,2,1:T(8,128)(2,1)S(1)}, u32[]{:S(2)}, u32[]{:S(2)}) async-start(bf16[256,4,16]{0,2,1:T(8,128)(2,1)} %bitcast.65), calls=%async_computation.10 | async-start | bytes 65536 | tf_op jit(solution)/shard_map/all_to_all | solution.py:294
  542.9 10.7 %all-to-all-start.8 = ((bf16[256,4,16]{0,2,1:T(8,128)(2,1)}), bf16[256,4,16]{0,2,1:T(8,128)(2,1)S(1)}, u32[]{:S(2)}, u32[]{:S(2)}) async-start(bf16[256,4,16]{0,2,1:T(8,128)(2,1)} %bitcast.56), calls=%async_computation.9 | async-start | bytes 65536 | tf_op jit(solution)/shard_map/all_to_all | solution.py:291
  553.6 21.8 %all-to-all-start.7 = ((bf16[256,4,64]{0,2,1:T(8,128)(2,1)}), bf16[256,4,64]{0,2,1:T(8,128)(2,1)S(1)}, u32[]{:S(2)}, u32[]{:S(2)}) async-start(bf16[256,4,64]{0,2,1:T(8,128)(2,1)} %bitcast.52), calls=%async_computation.8 | async-start | bytes 262144 | tf_op jit(solution)/shard_map/all_to_all | solution.py:288
  575.4 81.8 %all-to-all-start.6 = ((bf16[256,4,1024]{2,0,1:T(8,128)(2,1)}), bf16[256,4,1024]{2,0,1:T(8,128)(2,1)S(1)}, u32[]{:S(2)}, u32[]{:S(2)}) async-start(bf16[256,4,1024]{2,0,1:T(8,128)(2,1)} %copy.183), calls=%async_computation.7 | async-start | bytes 4194304 | tf_op jit(solution)/shard_map/all_to_all | solution.py:287
  580.4 11.1 %copy-start.36 = (f32[1024,16]{0,1:T(8,128)S(1)}, f32[1024,16]{0,1:T(8,128)}, u32[]{:S(2)}) copy-start(f32[1024,16]{0,1:T(8,128)} %get-tuple-element.709) | copy-start | bytes 196612
  580.4 11.1 %copy-start.73 = (f32[16]{0:T(128)S(1)}, f32[16]{0:T(128)}, u32[]{:S(2)}) copy-start(f32[16]{0:T(128)} %param.34) | copy-start | bytes 196
  580.4 148.1 %reduce-scatter.15.cloned.1.call-start = ((), (), s32[]{:S(2)}) async-start(), calls=%async_computation.24 | async-start | bytes 73728 | tf_op jit(solution)/shard_map/reduce_scatter | solution.py:352
  580.7 11.1 %copy-start.1 = (bf16[1024,2048]{1,0:T(8,128)(2,1)S(1)}, bf16[1024,2048]{1,0:T(8,128)(2,1)}, u32[]{:S(2)}) copy-start(bf16[1024,2048]{1,0:T(8,128)(2,1)} %param.21) | copy-start | bytes 12582916
  593.7 171.9 %reduce-scatter.13.cloned.1.call-start = ((), (), s32[]{:S(2)}) async-start(), calls=%async_computation.23 | async-start | bytes 294912 | tf_op jit(solution)/shard_map/reduce_scatter | solution.py:349
  598.0 325.1 %all-reduce.31.cloned.1.call-start = ((), (), s32[]{:S(2)}) async-start(), calls=%async_computation.20 | async-start | bytes 8388608 | tf_op jit(solution)/shard_map/psum | solution.py:327
  657.2 12.6 %copy-start.48 = (f32[1,1024]{1,0:T(1,128)S(1)}, f32[1,1024]{1,0:T(1,128)}, u32[]{:S(2)}) copy-start(f32[1,1024]{1,0:T(1,128)} %copy-done.47) | copy-start | bytes 12292
  657.2 12.6 %copy-start.50 = (f32[1,1024]{1,0:T(1,128)S(1)}, f32[1,1024]{1,0:T(1,128)}, u32[]{:S(2)}) copy-start(f32[1,1024]{1,0:T(1,128)} %copy-done.49) | copy-start | bytes 12292
  657.2 12.6 %copy-start.52 = (f32[1,1024]{1,0:T(1,128)S(1)}, f32[1,1024]{1,0:T(1,128)}, u32[]{:S(2)}) copy-start(f32[1,1024]{1,0:T(1,128)} %copy-done.51) | copy-start | bytes 12292
  671.1 11.5 %slice-start = ((s8[8388608]{0:T(1024)(128)(4,1)}), s8[4194304]{0:T(1024)(128)(4,1)S(1)}, s32[]{:S(2)}) async-start(s8[8388608]{0:T(1024)(128)(4,1)} %bitcast.257), calls=%async_computation.28 | async-start | bytes 8388608
  671.1 11.5 %slice-start.2 = ((s8[8388608]{0:T(1024)(128)(4,1)}), s8[4194304]{0:T(1024)(128)(4,1)S(1)}, s32[]{:S(2)}) async-start(s8[8388608]{0:T(1024)(128)(4,1)} %bitcast.274), calls=%async_computation.30 | async-start | bytes 8388608
  673.4 9.2 slice-start.1
  673.4 9.2 slice-start.3
  673.4 9.2 copy-start.29
  689.7 287.1 %reduce-scatter.11.cloned.1.call-start = ((), (), s32[]{:S(2)}) async-start(), calls=%async_computation.22 | async-start | bytes 4718592 | tf_op jit(solution)/shard_map/reduce_scatter | solution.py:346
  767.0 165.7 %copy-start.70 = (f32[1024]{0:T(1024)S(1)}, f32[1024]{0:T(1024)}, u32[]{:S(2)}) copy-start(f32[1024]{0:T(1024)} %get-tuple-element.616) | copy-start | bytes 12292
  (39 other events, 147.1 us)
Sparse Core Ops, SparseCore 0:
  10.5 39.4 all-gather.8
  144.2 79.1 all-gather.14
  225.8 35.2 all-gather.10
  263.5 37.4 all-gather.12
  417.5 79.7 all-gather.16
  500.5 49.8 reduce-scatter.16
  554.1 51.3 reduce-scatter.8
  607.8 86.9 reduce-scatter.6
  698.6 29.8 reduce-scatter.14
  731.9 33.6 reduce-scatter.12
  768.1 154.9 all-reduce.30
  926.3 50.4 reduce-scatter.10
where the time goes:
time: 997 us; the launch traced here: 986 us
  waiting for transfers between devices  441 us (44%)
  matrix products  194 us (19%)
  other arithmetic  132 us (13%)
  blocking collectives  121 us (12%)
  starting transfers between devices  41.3 us (4%)
  local copies, waits for them, and re-layouts  40.4 us (4%)
  between operations  17.4 us (2%)
    psum x1, waiting for transfers between devices, per_device(): lax.psum(grad_normed.astype(jnp.bfloat16), 'mp').astype(jnp.float32)  156 us
    all_gather x1, waiting for transfers between devices, entering(): lax.all_gather(part.astype(kind), axis)  61.4 us
    all_to_all x1, waiting for transfers between devices, per_device(): lax.all_to_all(grad_sx.astype(jnp.bfloat16), 'mp', split_axis=1, concat_a...  54.4 us
    all_to_all x1, blocking collectives, per_device(): lax.all_to_all(grad_ssd, 'mp', split_axis=0, concat_axis=1, tiled=True)  47.4 us
    all_to_all x1, waiting for transfers between devices, per_device(): lax.all_to_all((ssd_local + ssd_carry).astype(jnp.bfloat16), 'mp', split_...  46.7 us
    dot_general x3, matrix products, block_step(): y_rows = jnp.einsum('hij,jhp->ihp', mixing, x_heads, precision=exact)  42.8 us
    reduce_scatter x1, waiting for transfers between devices, per_device(): lax.psum_scatter(w_bc_grad.astype(jnp.bfloat16), 'dp', scatter_dimension=...  35.8 us
    all_to_all x1, waiting for transfers between devices, per_device(): lax.all_to_all(x_low, 'mp', split_axis=0, concat_axis=1, tiled=True)  25.8 us
  transfers between devices with their start and end apart: 21, of which 13 were waited for; matrix products, arithmetic and copies ran while one was open for 33% of the time, Pallas kernels for 0%

commit v1 on v0

v1 whole, which is shorter than its diff:
```python
import functools

import jax
import jax.numpy as jnp
from jax import lax
from jax.experimental import pallas as pl
from jax.experimental.pallas import tpu as pltpu
from jax.sharding import PartitionSpec as P

HEADDIM = 64
STATE = 128
CONV = 4
BLOCK = 256
DOCS = 5
LANES = 128
EPS = 1e-05
f32 = jnp.float32
bf16 = jnp.bfloat16
VMEM_LIMIT = 62 * 2**20


def mm(a, b):
    return jnp.dot(a, b, preferred_element_type=f32)


def mm_nt(a, b):
    return lax.dot_general(a, b, (((1,), (1,)), ((), ())), preferred_element_type=f32)


def mm_tn(a, b):
    return lax.dot_general(a, b, (((0,), (0,)), ((), ())), preferred_element_type=f32)


def halves(v):
    high = v.astype(bf16)
    return high, (v - high.astype(f32)).astype(bf16)


def expand(v, spread):
    high, rest = halves(v)
    return mm(high, spread) + mm(rest, spread)


def gather_heads(v, spread):
    high, rest = halves(v)
    return mm_nt(high, spread) + mm_nt(rest, spread)


def logistic(v):
    return 1.0 / (1.0 + jnp.exp(-v))


def tiles(total, size):
    return [(at, min(size, total - at)) for at in range(0, total, size)]


def fold(v):
    return jnp.sum(v.reshape(v.shape[0] // 8, 8, v.shape[1]), axis=0)


def doc_of(starts, place):
    count = (place >= starts[0]).astype(jnp.int32)
    for k in range(1, DOCS):
        count = count + (place >= starts[k]).astype(jnp.int32)
    return count


def fill_spread(spread):
    rows, columns = spread.shape
    head = lax.broadcasted_iota(jnp.int32, (rows, columns), 0)
    channel = lax.broadcasted_iota(jnp.int32, (rows, columns), 1)
    low = head * HEADDIM
    spread[...] = jnp.where((channel >= low) & (channel < low + HEADDIM), 1.0, 0.0).astype(bf16)


def fill_positions(starts, pos, rpos):
    length = pos.shape[0]

    def body(i, carry):
        at = pl.multiple_of(i * BLOCK, BLOCK)
        place = lax.broadcasted_iota(jnp.int32, (BLOCK, LANES), 0) + at
        begin = jnp.zeros_like(place)
        end = jnp.full_like(place, length)
        for k in range(DOCS):
            begin = jnp.maximum(begin, jnp.where(place >= starts[k], starts[k], 0))
            end = jnp.minimum(end, jnp.where(place < starts[k], starts[k], length))
        pos[pl.ds(at, BLOCK), :] = place - begin
        if rpos is not None:
            rpos[pl.ds(at, BLOCK), :] = end - 1 - place
        return carry

    lax.fori_loop(0, length // BLOCK, body, 0)


def normalize(tok, gain, normed, stat):
    step = 64

    def body(i, carry):
        rows = pl.ds(pl.multiple_of(i * step, step), step)
        v = tok[rows, :].astype(f32)
        inverse = lax.rsqrt(jnp.mean(v * v, axis=1, keepdims=True) + EPS)
        normed[rows, :] = (v * inverse * gain[...]).astype(bf16)
        stat[rows, :] = jnp.broadcast_to(inverse, (step, LANES))
        return carry

    lax.fori_loop(0, tok.shape[0] // step, body, 0)


def project_x(normed, wxd, xin, dtin):
    length, width = normed.shape[0], xin.shape[1]
    xin[pl.ds(0, 8), :] = jnp.zeros((8, width), f32)
    rows = 512

    def body(i, carry):
        at = pl.multiple_of(i * rows, rows)
        left = normed[pl.ds(at, rows), :]
        for c, w in tiles(width, 512):
            xin[pl.ds(at + 8, rows), c : c + w] = mm(left, wxd[:, c : c + w])
        dtin[pl.ds(at, rows), :] = mm(left, wxd[:, width : width + LANES])
        return carry

    lax.fori_loop(0, length // rows, body, 0)


def convolve(xin, taps, pos, slope, x_low, bc_low):
    width, inner = xin.shape[1], x_low.shape[1]

    def tile(b, c, out, at):
        rows = pl.ds(pl.multiple_of(b * BLOCK, BLOCK), BLOCK)
        x = xin[pl.ds(pl.multiple_of(b * BLOCK, BLOCK), BLOCK + 8), pl.ds(c, LANES)]
        place = pos[rows, :]
        tap = taps[:, pl.ds(c, LANES)]
        pre = tap[CONV : CONV + 1] + tap[CONV - 1 : CONV] * x[8:]
        for lag in range(1, CONV):
            earlier = pltpu.roll(x, lag, 0)[8:]
            pre = pre + tap[CONV - 1 - lag : CONV - lag] * jnp.where(place >= lag, earlier, 0.0)
        sg = logistic(pre)
        slope[rows, pl.ds(c, LANES)] = sg * (1.0 + pre * (1.0 - sg))
        out[rows, pl.ds(at, LANES)] = (pre * sg).astype(bf16)

    blocks = x_low.shape[0] // BLOCK
    xcols, bcols = inner // LANES, (width - inner) // LANES

    def x_body(i, carry):
        c = pl.multiple_of((i % xcols) * LANES, LANES)
        tile(i // xcols, c, x_low, c)
        return carry

    def bc_body(i, carry):
        c = pl.multiple_of((i % bcols) * LANES, LANES)
        tile(i // bcols, inner + c, bc_low, c)
        return carry

    lax.fori_loop(0, blocks * xcols, x_body, 0)
    lax.fori_loop(0, blocks * bcols, bc_body, 0)


def steps(dtin, dpar, step, sgdt, step_low, decay_low):
    def body(i, carry):
        rows = pl.ds(pl.multiple_of(i * BLOCK, BLOCK), BLOCK)
        v = dtin[rows, :] + dpar[0:1, :]
        soft = jnp.maximum(v, 0.0) + jnp.log1p(jnp.exp(-jnp.abs(v)))
        step[rows, :] = soft
        sgdt[rows, :] = logistic(v)
        step_low[rows, :] = soft.astype(bf16)
        decay_low[rows, :] = (-dpar[1:2, :] * soft).astype(bf16)
        return carry

    lax.fori_loop(0, dtin.shape[0] // BLOCK, body, 0)


def block_marks(starts, b):
    at = b * BLOCK
    column = doc_of(starts, lax.broadcasted_iota(jnp.int32, (BLOCK, 1), 0) + at)
    row = doc_of(starts, lax.broadcasted_iota(jnp.int32, (1, BLOCK), 1) + at)
    before = doc_of(starts, at - 1)
    last = doc_of(starts, at + BLOCK - 1)
    return column, row, before, last


def block_decays(b, starts, decay_low, step_low, spread):
    rows = pl.ds(pl.multiple_of(b * BLOCK, BLOCK), BLOCK)
    column, row, before, last = block_marks(starts, b)
    i0 = lax.broadcasted_iota(jnp.int32, (BLOCK, BLOCK), 0)
    i1 = lax.broadcasted_iota(jnp.int32, (BLOCK, BLOCK), 1)
    lower = jnp.where(i0 >= i1, 1.0, 0.0).astype(bf16)
    cum = mm(lower, decay_low[rows, :])
    step_e = mm(step_low[rows, :], spread[...])
    cum_e = expand(jnp.exp(cum), spread[...])
    kept_e = jnp.where(before == last, cum_e[BLOCK - 1 : BLOCK], 0.0)
    in_e = jnp.where(column == before, cum_e, 0.0)
    out_e = expand(jnp.exp(cum[BLOCK - 1 : BLOCK] - cum), spread[...])
    out_e = jnp.where(column == last, out_e, 0.0)
    return cum, step_e, kept_e, in_e, out_e, column, row


def scan_forward(starts, x_low, bc_low, step_low, decay_low, ssd, states, spread, state, xs, yin, cbm):
    length, inner = x_low.shape
    state[...] = jnp.zeros_like(state)

    def body(b, carry):
        rows = pl.ds(pl.multiple_of(b * BLOCK, BLOCK), BLOCK)
        cum, step_e, kept_e, in_e, out_e, column, row = block_decays(
            b, starts, decay_low, step_low, spread
        )
        bm, cm = bc_low[rows, :STATE], bc_low[rows, STATE:]
        i0 = lax.broadcasted_iota(jnp.int32, (BLOCK, BLOCK), 0)
        i1 = lax.broadcasted_iota(jnp.int32, (BLOCK, BLOCK), 1)
        cbm[...] = jnp.where((column == row) & (i0 >= i1), mm_nt(cm, bm), 0.0)
        stepped = x_low[rows, :].astype(f32) * step_e
        xs[...] = stepped.astype(bf16)
        entering = state[...].astype(bf16)
        states[b] = entering
        yin[...] = in_e * mm(cm, entering)
        state[...] = kept_e * state[...] + mm_tn(bm, (stepped * out_e).astype(bf16))
        cum_t = cum.T
        first = lax.broadcasted_iota(jnp.int32, (BLOCK, LANES), 1) < HEADDIM
        for j in range(inner // LANES):
            cols = slice(j * LANES, (j + 1) * LANES)
            pair = xs[:, cols]
            part = []
            for h in (2 * j, 2 * j + 1):
                span = jnp.minimum(cum[:, h : h + 1] - cum_t[h : h + 1, :], 0.0)
                part.append(mm((jnp.exp(span) * cbm[...]).astype(bf16), pair))
            y = jnp.where(first, part[0], part[1]) + yin[:, cols]
            ssd[rows, cols] = y.astype(bf16)
        return carry

    lax.fori_loop(0, length // BLOCK, body, 0)


def project_rows(left, right, out, rows=512, columns=512):
    def body(i, carry):
        at = pl.ds(pl.multiple_of(i * rows, rows), rows)
        part = left[at, :]
        for c, w in tiles(out.shape[1], columns):
            out[at, c : c + w] = mm(part, right[:, c : c + w]).astype(out.dtype)
        return carry

    lax.fori_loop(0, out.shape[0] // rows, body, 0)


def back_rows(left, right, out, rows=512, columns=512):
    def body(i, carry):
        at = pl.ds(pl.multiple_of(i * rows, rows), rows)
        part = left[at, :]
        for c, w in tiles(out.shape[1], columns):
            out[at, c : c + w] = mm_nt(part, right[c : c + w, :]).astype(out.dtype)
        return carry

    lax.fori_loop(0, out.shape[0] // rows, body, 0)


def weight_rows(left, right, out, rows=256, columns=512):
    def body(i, carry):
        at = pl.ds(pl.multiple_of(i * rows, rows), rows)
        part = left[:, at]
        for c, w in tiles(out.shape[1], columns):
            out[at, c : c + w] = mm_tn(part, right[:, c : c + w]).astype(out.dtype)
        return carry

    lax.fori_loop(0, out.shape[0] // rows, body, 0)


def gate_sums(gate, ssd, x_low, gnorm, crow, stat):
    step, inner = 64, gate.shape[1]

    def body(i, carry):
        rows = pl.ds(pl.multiple_of(i * step, step), step)
        squares = jnp.zeros((step, 256), f32)
        crosses = jnp.zeros((step, 256), f32)
        for c in range(0, inner, 256):
            cols = slice(c, c + 256)
            g = gate[rows, cols]
            mixed = ssd[rows, cols].astype(f32) + crow[1:2, cols] * x_low[rows, cols].astype(f32)
            gated = mixed * (g * logistic(g))
            squares = squares + gated * gated
            crosses = crosses + gnorm[rows, cols] * crow[0:1, cols] * gated
        lane = lax.broadcasted_iota(jnp.int32, (step, LANES), 1)
        s1 = jnp.sum(squares, axis=1, keepdims=True)
        s2 = jnp.sum(crosses, axis=1, keepdims=True)
        stat[rows, :] = jnp.where(lane == 0, s1, jnp.where(lane == 1, s2, 0.0))
        return carry

    lax.fori_loop(0, gate.shape[0] // step, body, 0)


def forward_kernel(
    starts, tok, gain, wxd, wz, taps, dpar,
    normed, inverse, xin, slope, gate, x_low, bc_low, step, sgdt, step_low, decay_low, ssd, states,
    pos, spread, dtin, state, xs, yin, cbm,
):
    fill_spread(spread)
    fill_positions(starts, pos, None)
    normalize(tok, gain, normed, inverse)
    project_x(normed, wxd, xin, dtin)
    convolve(xin, taps, pos, slope, x_low, bc_low)
    steps(dtin, dpar, step, sgdt, step_low, decay_low)
    scan_forward(starts, x_low, bc_low, step_low, decay_low, ssd, states, spread, state, xs, yin, cbm)
    project_rows(normed, wz, gate)


def gate_kernel(cot, wout, gate, ssd, x_low, crow, gnorm, stat):
    back_rows(cot, wout, gnorm)
    gate_sums(gate, ssd, x_low, gnorm, crow, stat)


def gate_backward(gate, ssd, x_low, gnorm, crow, stat, width, gn, low_gate, gs, sums):
    step, inner = 64, gate.shape[1]
    sums[...] = jnp.zeros_like(sums)

    def body(i, carry):
        rows = pl.ds(pl.multiple_of(i * step, step), step)
        inverse = lax.rsqrt(stat[rows, 0:1] / width + EPS)
        mean = inverse * stat[rows, 1:2] / width
        for c in range(0, inner, 256):
            cols = slice(c, c + 256)
            g = gate[rows, cols]
            x = x_low[rows, cols].astype(f32)
            mixed = ssd[rows, cols].astype(f32) + crow[1:2, cols] * x
            sg = logistic(g)
            act = g * sg
            hat = mixed * act * inverse
            gn[rows, cols] = (hat * crow[0:1, cols]).astype(bf16)
            gnorm_here = gnorm[rows, cols]
            grad = inverse * (gnorm_here * crow[0:1, cols] - hat * mean)
            grad_mixed = grad * act
            low_gate[rows, cols] = (grad * mixed * (sg * (1.0 + g * (1.0 - sg)))).astype(bf16)
            gs[rows, cols] = grad_mixed.astype(bf16)
            sums[0:8, cols] += fold(gnorm_here * hat)
            sums[8:16, cols] += fold(grad_mixed * x)
        return carry

    lax.fori_loop(0, gate.shape[0] // step, body, 0)


def middle_kernel(
    cot, wout, normed, gate, x_low, ssd, gnorm, crow, stat,
    branch, dwout, dwz, low_gate, gs, sums,
    gn, *, width,
):
    gate_backward(gate, ssd, x_low, gnorm, crow, stat, width, gn, low_gate, gs, sums)
    project_rows(gn, wout, branch)
    weight_rows(gn, cot, dwout)
    weight_rows(normed, low_gate, dwz)


def scan_backward(
    starts, x_low, bc_low, step_low, decay_low, ssd, states, gs, slope, crow, step, sgdt, dpar,
    gpre, low_xd, dsums, spread, dstate, xs, gx, cbm, acc,
):
    length, inner = x_low.shape
    width = gpre.shape[1]
    blocks = length // BLOCK
    dstate[...] = jnp.zeros_like(dstate)
    dsums[...] = jnp.zeros_like(dsums)
    gpre[pl.ds(length, 8), :] = jnp.zeros((8, width), f32)

    def body(i, carry):
        b = blocks - 1 - i
        rows = pl.ds(pl.multiple_of(b * BLOCK, BLOCK), BLOCK)
        cum, step_e, kept_e, in_e, out_e, column, row = block_decays(
            b, starts, decay_low, step_low, spread
        )
        bm, cm = bc_low[rows, :STATE], bc_low[rows, STATE:]
        i0 = lax.broadcasted_iota(jnp.int32, (BLOCK, BLOCK), 0)
        i1 = lax.broadcasted_iota(jnp.int32, (BLOCK, BLOCK), 1)
        linked = (column == row) & (i0 <= i1)
        cbm[...] = jnp.where(linked, mm_nt(bm, cm), 0.0)
        x = x_low[rows, :].astype(f32)
        stepped = x * step_e
        xs[...] = stepped.astype(bf16)
        cum_t = cum.T
        first = lax.broadcasted_iota(jnp.int32, (BLOCK, LANES), 1) < HEADDIM
        acc[...] = jnp.zeros_like(acc)
        for j in range(inner // LANES):
            cols = slice(j * LANES, (j + 1) * LANES)
            xpair, gpair = xs[:, cols], gs[rows, cols]
            none = jnp.zeros_like(xpair)
            part, total = [], None
            for k in range(2):
                h = 2 * j + k
                kernel = jnp.exp(jnp.minimum(cum_t[h : h + 1, :] - cum[:, h : h + 1], 0.0))
                part.append(mm((kernel * cbm[...]).astype(bf16), gpair))
                own = jnp.where(first, xpair, none) if k == 0 else jnp.where(first, none, xpair)
                here = kernel * mm_nt(own, gpair)
                total = here if total is None else total + here
            acc[...] += total
            gx[:, cols] = jnp.where(first, part[0], part[1])
        dstate_low = dstate[...].astype(bf16)
        entering = states[b]
        leaving = states[jnp.minimum(b + 1, blocks - 1)]
        end = jnp.sum(dstate[...] * leaving.astype(f32), axis=0, keepdims=True)
        g = gs[rows, :].astype(f32)
        g_in = (in_e * g).astype(bf16)
        raw = gx[...] + out_e * mm(bm, dstate_low)
        grad_x = (step_e * raw).astype(bf16).astype(f32)
        gpre[rows, :inner] = (grad_x + crow[1:2, :] * g) * slope[rows, :inner]
        pairs = jnp.where(linked, acc[...], 0.0).astype(bf16)
        db = mm(pairs, cm) + mm_nt((stepped * out_e).astype(bf16), dstate_low)
        dc = mm_tn(pairs, bm) + mm_nt(g_in, entering)
        gpre[rows, inner : inner + STATE] = db * slope[rows, inner : inner + STATE]
        gpre[rows, inner + STATE :] = dc * slope[rows, inner + STATE :]
        raw_x = x * raw
        grad_step = gather_heads(raw_x, spread[...]).astype(bf16).astype(f32)
        dcum = gather_heads(g * ssd[rows, :].astype(f32) - step_e * raw_x, spread[...])
        tail = gather_heads(jnp.broadcast_to(end, (8, inner)), spread[...])[0:1]
        upper = jnp.where(i0 <= i1, 1.0, 0.0).astype(bf16)
        high, rest = halves(dcum)
        later = mm(upper, high) + mm(upper, rest) + tail
        grad_decay = later.astype(bf16).astype(f32)
        total_step = grad_step - dpar[1:2, :] * grad_decay
        grad_dt = total_step * sgdt[rows, :]
        low_xd[rows, width:] = grad_dt.astype(bf16)
        dsums[0:8, :] += fold(grad_dt)
        dsums[8:16, :] -= fold(grad_decay * step[rows, :])
        dstate[...] = kept_e * dstate[...] + mm_tn(cm, g_in)
        return carry

    lax.fori_loop(0, blocks, body, 0)


def convolve_back(xin, gpre, taps, pos, rpos, low_xd, csums):
    width = gpre.shape[1]
    columns = width // LANES
    csums[...] = jnp.zeros_like(csums)

    def body(i, carry):
        at = pl.multiple_of((i // columns) * BLOCK, BLOCK)
        cols = pl.ds(pl.multiple_of((i % columns) * LANES, LANES), LANES)
        rows = pl.ds(at, BLOCK)
        x = xin[pl.ds(at, BLOCK + 8), cols]
        g = gpre[pl.ds(at, BLOCK + 8), cols]
        here = g[:BLOCK]
        place, ahead = pos[rows, :], rpos[rows, :]
        tap = taps[:, cols]
        grad = tap[CONV - 1 : CONV] * here
        csums[pl.ds(8 * CONV, 8), cols] += fold(here)
        csums[pl.ds(8 * (CONV - 1), 8), cols] += fold(here * x[8:])
        for lag in range(1, CONV):
            k = CONV - 1 - lag
            later = pltpu.roll(g, BLOCK + 8 - lag, 0)[:BLOCK]
            earlier = pltpu.roll(x, lag, 0)[8:]
            grad = grad + tap[k : k + 1] * jnp.where(ahead >= lag, later, 0.0)
            csums[pl.ds(8 * k, 8), cols] += fold(here * jnp.where(place >= lag, earlier, 0.0))
        low_xd[rows, cols] = grad.astype(bf16)
        return carry

    lax.fori_loop(0, (xin.shape[0] - 8) // BLOCK * columns, body, 0)


def backward_kernel(
    starts, xin, slope, x_low, bc_low, step, sgdt, step_low, decay_low, ssd, states, gs, taps, crow, dpar,
    low_xd, csums, dsums,
    pos, rpos, spread, gpre, dstate, xs, gx, cbm, acc,
):
    fill_spread(spread)
    fill_positions(starts, pos, rpos)
    scan_backward(
        starts, x_low, bc_low, step_low, decay_low, ssd, states, gs, slope, crow, step, sgdt, dpar,
        gpre, low_xd, dsums, spread, dstate, xs, gx, cbm, acc,
    )
    convolve_back(xin, gpre, taps, pos, rpos, low_xd, csums)


def last_kernel(tok, inverse, gain, normed, low_gate, low_xd, wz, wxd, dwxd, gfull, rowdot):
    weight_rows(normed, low_xd, dwxd)
    rows = 256

    def body(i, carry):
        at = pl.ds(pl.multiple_of(i * rows, rows), rows)
        total = jnp.zeros((rows, 1), f32)
        for c, w in tiles(gfull.shape[1], 512):
            cols = slice(c, c + w)
            part = mm_nt(low_gate[at, :], wz[cols, :]) + mm_nt(low_xd[at, :], wxd[cols, :])
            gfull[at, cols] = part.astype(bf16)
            total = total + jnp.sum(part * gain[:, cols] * tok[at, cols].astype(f32), axis=1, keepdims=True)
        rowdot[at, :] = total * inverse[at, :]
        return carry

    lax.fori_loop(0, gfull.shape[0] // rows, body, 0)


def call(kernel, outs, scratch, smem, *operands):
    whole = pl.BlockSpec(memory_space=pltpu.VMEM)
    scalar = pl.BlockSpec(memory_space=pltpu.SMEM)
    return pl.pallas_call(
        kernel,
        out_shape=[jax.ShapeDtypeStruct(shape, kind) for shape, kind in outs],
        in_specs=[scalar if i < smem else whole for i in range(len(operands))],
        out_specs=[whole] * len(outs),
        scratch_shapes=[pltpu.VMEM(shape, kind) for shape, kind in scratch],
        compiler_params=pltpu.CompilerParams(vmem_limit_bytes=VMEM_LIMIT),
    )(*operands)


def per_device(
    tokens, cotangent, doc_lengths, w_z, w_x, w_bc, w_dt, w_out, conv_x, conv_x_bias, conv_bc,
    conv_bc_bias, dt_bias, a_rate, d_skip, input_norm_gain, out_gain,
):
    group = lax.axis_size("mp")
    rank = lax.axis_index("mp")
    T, D = tokens.shape
    inner, heads = w_x.shape[1], w_dt.shape[1]
    pair = 2 * STATE
    width = inner + pair
    wide = width + LANES
    own = D // group

    lengths = doc_lengths[0]
    starts = jnp.cumsum(lengths) - lengths
    packed = jnp.concatenate([w_bc, conv_bc, conv_bc_bias[None, :]], axis=0)
    packed = lax.all_gather(packed, "mp", axis=1, tiled=True)
    shard = w_bc.shape[0]
    w_bc_all, taps_bc = packed[:shard], packed[shard:]
    wxd = jnp.concatenate(
        [w_x.astype(bf16), w_bc_all.astype(bf16), w_dt.astype(bf16), jnp.zeros((shard, LANES - heads), bf16)],
        axis=1,
    )
    wxd = lax.all_gather(wxd, "dp", axis=0, tiled=True)
    wz = lax.all_gather(w_z.astype(bf16), "dp", axis=0, tiled=True)
    wout = lax.all_gather(w_out.astype(bf16), "dp", axis=1, tiled=True)
    taps = jnp.concatenate([jnp.concatenate([conv_x, conv_x_bias[None, :]], axis=0), taps_bc], axis=1)
    taps = jnp.pad(taps, ((0, 8 - CONV - 1), (0, 0)))
    crow = jnp.pad(jnp.stack([out_gain, jnp.repeat(d_skip, HEADDIM)]), ((0, 6), (0, 0)))
    dpar = jnp.pad(jnp.stack([dt_bias, a_rate]), ((0, 6), (0, LANES - heads)))
    gain = input_norm_gain[None, :]

    blocks = T // BLOCK
    (
        normed, inverse, xin, slope, gate, x_low, bc_low, step, sgdt, step_low, decay_low, ssd, states,
    ) = call(
        forward_kernel,
        [
            ((T, D), bf16), ((T, LANES), f32), ((T + 8, width), f32), ((T, width), f32), ((T, inner), f32),
            ((T, inner), bf16), ((T, pair), bf16), ((T, LANES), f32), ((T, LANES), f32),
            ((T, LANES), bf16), ((T, LANES), bf16), ((T, inner), bf16), ((blocks, STATE, inner), bf16),
        ],
        [
            ((T, LANES), jnp.int32), ((LANES, inner), bf16), ((T, LANES), f32), ((STATE, inner), f32),
            ((BLOCK, inner), bf16), ((BLOCK, inner), f32), ((BLOCK, BLOCK), f32),
        ],
        1, starts, tokens, gain, wxd, wz, taps, dpar,
    )
    gnorm, stat = call(
        gate_kernel,
        [((T, inner), f32), ((T, LANES), f32)],
        [],
        0, cotangent, wout, gate, ssd, x_low, crow,
    )
    stat = jnp.pad(lax.psum(stat[:, :8], "mp"), ((0, 0), (0, LANES - 8)))
    branch, dwout, dwz, low_gate, gs, sums = call(
        functools.partial(middle_kernel, width=inner * group),
        [
            ((T, D), bf16), ((inner, D), bf16), ((D, inner), bf16), ((T, inner), bf16), ((T, inner), bf16),
            ((16, inner), f32),
        ],
        [((T, inner), bf16)],
        0, cotangent, wout, normed, gate, x_low, ssd, gnorm, crow, stat,
    )
    low_xd, csums, dsums = call(
        backward_kernel,
        [((T, wide), bf16), ((8 * CONV + 8, width), f32), ((16, LANES), f32)],
        [
            ((T, LANES), jnp.int32), ((T, LANES), jnp.int32), ((LANES, inner), bf16), ((T + 8, width), f32),
            ((STATE, inner), f32), ((BLOCK, inner), bf16), ((BLOCK, inner), f32), ((BLOCK, BLOCK), f32),
            ((BLOCK, BLOCK), f32),
        ],
        1, starts, xin, slope, x_low, bc_low, step, sgdt, step_low, decay_low, ssd, states, gs, taps, crow,
        dpar,
    )
    dwxd, gfull, rowdot = call(
        last_kernel,
        [((D, wide), bf16), ((T, D), bf16), ((T, LANES), f32)],
        [],
        0, tokens, inverse, gain, normed, low_gate, low_xd, wz, wxd,
    )

    def scatter(v, axis, dim):
        return lax.psum_scatter(v, axis, scatter_dimension=dim, tiled=True)

    token_own = lax.dynamic_slice_in_dim(tokens, rank * own, own, 1).astype(f32)
    output = (token_own + scatter(branch, "mp", 1).astype(f32)).astype(bf16)
    w_out_grad = scatter(dwout, "dp", 1).astype(f32)
    w_z_grad = scatter(dwz, "dp", 0).astype(f32)
    dwxd_own = scatter(dwxd, "dp", 0)
    w_x_grad = dwxd_own[:, :inner].astype(f32)
    w_dt_grad = dwxd_own[:, width : width + heads].astype(f32)
    w_bc_grad = scatter(dwxd_own[:, inner:width], "mp", 1).astype(f32)

    g_own = scatter(gfull, "mp", 1).astype(f32)
    gain_own = lax.dynamic_slice_in_dim(input_norm_gain, rank * own, own, 0)
    row_mean = (lax.psum(rowdot[:, 0], "mp") / D)[:, None]
    inv = inverse[:, :1]
    hat = token_own * inv
    cot_own = lax.dynamic_slice_in_dim(cotangent, rank * own, own, 1).astype(f32)
    input_grad = (cot_own + inv * (g_own * gain_own - hat * row_mean)).astype(bf16)
    in_gain = jnp.sum(g_own * hat, axis=0)

    csums = jnp.sum(csums.reshape(CONV + 1, 8, width), axis=1)
    sums = jnp.sum(sums.reshape(2, 8, inner), axis=1)
    dsums = jnp.sum(dsums.reshape(2, 8, LANES), axis=1)[:, :heads]
    csums_bc = scatter(csums[:, inner:], "mp", 1)
    conv_grad, conv_bc_grad, sums, dsums, in_gain = lax.psum(
        (csums[:, :inner], csums_bc, sums, dsums, in_gain), "dp"
    )
    d_skip_grad = jnp.sum(sums[1].reshape(heads, HEADDIM), axis=1)
    return (
        output, input_grad, w_z_grad, w_x_grad, w_bc_grad, w_dt_grad, w_out_grad,
        conv_grad[:CONV], conv_grad[CONV], conv_bc_grad[:CONV], conv_bc_grad[CONV],
        dsums[0], dsums[1], d_skip_grad, in_gain, sums[0],
    )


def solution(mesh):
    row, block, column = P("dp", None), P("dp", "mp"), P("mp")
    return jax.shard_map(
        per_device,
        mesh=mesh,
        in_specs=(
            row, row, row, block, block, block, block, P("mp", "dp"), P(None, "mp"), column,
            P(None, "mp"), column, column, column, column, P(), column,
        ),
        out_specs=(
            block, block, block, block, block, block, P("mp", "dp"), P(None, "mp"), column,
            P(None, "mp"), column, column, column, column, column, column,
        ),
        check_vma=False,
    )
```

time: 997 us -> 634 us (0.64)
  matrix products: 194 us -> 0 us
  Pallas kernels: 0 us -> 158 us
  other arithmetic: 132 us -> 19.1 us
  waiting for transfers between devices: 441 us -> 348 us
  starting transfers between devices: 41.3 us -> 0.4 us
  blocking collectives: 121 us -> 80.8 us
  local copies, waits for them, and re-layouts: 40.4 us -> 12.9 us
    reduce_scatter x6 -> x5, waiting for transfers between devices: 66.3 us -> 265 us  [scatter(): return lax.psum_scatter(v, axis, scatter_dimension=dim, tiled=True)]
    dot_general x29 -> x0, matrix products: 194 us -> none  [the longest x3 42.8 us: block_step(): y_rows = jnp.einsum('hij,jhp->ihp', mixing, x_heads, precision=exact)]
    pallas_call x0 -> x5, Pallas kernels: none -> 158 us  [call(): pl.pallas_call(kernel, out_shape=[jax.ShapeDtypeStruct(shape, kind) for s...]
    psum x1 -> x0, waiting for transfers between devices: 156 us -> none  [per_device(): lax.psum(grad_normed.astype(jnp.bfloat16), 'mp').astype(jnp.float32)]
    all_to_all x9 -> x0, waiting for transfers between devices: 133 us -> none  [the longest x1 54.4 us: per_device(): lax.all_to_all(grad_sx.astype(jnp.bfloat16), 'mp', split_axis=1, concat_a...]
    all_to_all x1 -> x0, blocking collectives: 47.4 us -> none  [per_device(): lax.all_to_all(grad_ssd, 'mp', split_axis=0, concat_axis=1, tiled=True)]
    convert_element_type x28 -> x8, other arithmetic: 53.3 us -> 10.3 us  [the longest x1 2.18 us: per_device(): wz = lax.all_gather(w_z.astype(bf16), 'dp', axis=0, tiled=True)]
    all_to_all x9 -> x0, starting transfers between devices: 39.2 us -> none  [the longest x1 5.23 us: per_device(): lax.all_to_all(x_low, 'mp', split_axis=0, concat_axis=1, tiled=True)]
  transfers between devices with their start and end apart: 21 -> 10, of which waited for: 13 -> 8; matrix products, arithmetic and copies ran while one was open for 33% -> 4% of each run, Pallas kernels for 0% -> 11%
where the time goes in v1:
time: 634 us; the launch traced here: 633 us
  waiting for transfers between devices  348 us (55%)
  Pallas kernels  158 us (25%)
  blocking collectives  80.8 us (13%)
  other arithmetic  19.1 us (3%)
  between operations  14.5 us (2%)
  local copies, waits for them, and re-layouts  12.9 us (2%)
    reduce_scatter x5, waiting for transfers between devices, scatter(): return lax.psum_scatter(v, axis, scatter_dimension=dim, tiled=True)  265 us
    pallas_call x5, Pallas kernels, call(): pl.pallas_call(kernel, out_shape=[jax.ShapeDtypeStruct(shape, kind) for s...  158 us
    all_gather x1, waiting for transfers between devices, per_device(): wxd = lax.all_gather(wxd, 'dp', axis=0, tiled=True)  45.8 us
    psum x1, blocking collectives, per_device(): stat = jnp.pad(lax.psum(stat[:, :8], 'mp'), ((0, 0), (0, LANES - 8)))  30.9 us
    psum x1, blocking collectives, per_device(): lax.psum((csums[:, :inner], csums_bc, sums, dsums, in_gain), 'dp')  25.1 us
    all_gather x1, waiting for transfers between devices, per_device(): wz = lax.all_gather(w_z.astype(bf16), 'dp', axis=0, tiled=True)  18.6 us
    unnamed x12, waiting for transfers between devices  18.4 us
    all_gather x1, blocking collectives, per_device(): packed = lax.all_gather(packed, 'mp', axis=1, tiled=True)  16.2 us
  transfers between devices with their start and end apart: 10, of which 8 were waited for; matrix products, arithmetic and copies ran while one was open for 4% of the time, Pallas kernels for 11%

profile of v1, /device:TPU:0, one launch (start us, length us, event | category | flops | bytes accessed | tf_op | source)
XLA Modules:
  0.0 633.2 jit_solution(7225906579809921552)
XLA Ops:
  7.3 2.2 convert_element_type.58
  9.5 0.1 copy.48
  9.6 0.1 copy.49
  9.7 0.1 pad_maximum_fusion
  9.8 16.2 %all_gather.13 = f32[261,256]{0,1:T(8,128)S(1)} all-gather(f32[261,64]{0,1:T(8,128)S(1)} %pad_maximum_fusion), channel_id=1, replica_groups=mesh['dp'=8,'mp'=4] {'mp'}, dimensions={1}, use_global_device_ids=true | all-gather | bytes 334080 | tf_op jit(solution)/shard_map/all_gather | solution.py:513
  26.1 0.1 copy.59
  26.2 0.1 convert_element_type.56
  26.3 0.1 copy.51
  26.5 1.0 concatenate.13
  27.6 0.0 all-gather.4.cloned.1.call-start
  27.6 0.8 convert_element_type.55
  28.6 0.1 copy.60
  28.6 0.1 broadcast_in_dim.21
  28.7 0.1 stack_reshape.3
  28.8 0.2 reduce-window.9
  29.0 0.6 select_maximum_fusion.3.dpar
  29.6 0.6 select_maximum_fusion.2.crow
  30.2 0.5 bitcast_subtract_fusion.starts
  30.7 0.6 select_maximum_fusion.taps
  31.4 18.6 %all-gather.8.cloned.1.call-done.wz = bf16[2048,1024]{1,0:T(8,128)(2,1)} async-done(((bf16[256,1024]{1,0:T(8,128)(2,1)}), bf16[2048,1024]{1,0:T(8,128)(2,1)}) %all-gather.8.cloned.1.call-update) | async-done | bytes 4194320 | tf_op jit(solution)/shard_map/all_gather | solution.py:521
  50.0 45.8 %all-gather.6.cloned.1.call-done.wxd = bf16[2048,1408]{1,0:T(8,128)(2,1)} async-done(((bf16[256,1408]{1,0:T(8,128)(2,1)}), bf16[2048,1408]{1,0:T(8,128)(2,1)}) %all-gather.6.cloned.1.call-update) | async-done | bytes 5767184 | tf_op jit(solution)/shard_map/all_gather | solution.py:520
  95.8 41.0 %shard_map.288 = (bf16[1024,2048]{1,0:T(8,128)(2,1)}, f32[1024,128]{1,0:T(8,128)}, f32[1032,1280]{1,0:T(8,128)}, f32[1024,1280]{1,0:T(8,128)}, f32[1024,1024]{1,...) custom-call(s32[5]{0:T(128)} %bitcast_subtract_fusion.starts, ...), custom_call_target="tpu_custom_call" | custom-call | tf_op jit(solution)/shard_map/pallas_call | solution.py:487
  136.8 16.0 %shard_map.289 = (f32[1024,1024]{1,0:T(8,128)}, f32[1024,128]{1,0:T(8,128)}) custom-call(bf16[1024,2048]{1,0:T(8,128)(2,1)} %cot.3, bf16[1024,2048]{1,0:T(8,128)(2,1)} %all-gather.4.cloned.1.call-done.wout, f32[1024,1024]{1,0:T(8,128)} %get-tuple-element.44.gate, bf16[1024,1024]{1,0:T(8,128)(2,1)} %get-tuple-element.46.ssd, ...), custom_call_target="tpu_custom_call" | custom-call | tf_op jit(solution)/shard_map/pallas_call | solution.py:487
  152.8 30.9 %psum.49 = f32[1024,8]{1,0:T(8,128)S(1)} all-reduce(f32[1024,8]{1,0:T(8,128)} %bitcast.31), channel_id=1, replica_groups=mesh['dp'=8,'mp'=4] {'mp'}, use_global_device_ids=true, to_apply=%region_1.2 | all-reduce | flops 8192 | bytes 65536 | tf_op jit(solution)/shard_map/psum | solution.py:551
  183.7 0.8 pad.19.stat
  184.5 34.4 %shard_map.290 = (bf16[1024,2048]{1,0:T(8,128)(2,1)}, bf16[1024,2048]{1,0:T(8,128)(2,1)}, bf16[2048,1024]{1,0:T(8,128)(2,1)}, bf16[1024,1024]{1,0:T(8,128)(2,1)}...) custom-call(bf16[1024,2048]{1,0:T(8,128)(2,1)} %cot.3, bf16[1024,2048]{1,0:T(8,128)(2,1)} %all-gather.4.cloned.1.call-done.wout, ...), custom_call_target="tpu_custom_call" | custom-call | tf_op jit(solution)/shard_map/pallas_call | solution.py:487
  219.0 35.9 %shard_map.291 = (bf16[1024,1408]{1,0:T(8,128)(2,1)}, f32[40,1280]{1,0:T(8,128)}, f32[16,128]{1,0:T(8,128)}) custom-call(s32[5]{0:T(128)} %bitcast_subtract_fusion.starts, f32[1032,1280]{1,0:T(8,128)} %get-tuple-element.52.xin, f32[1024,1280]{1,0:T(8,128)} %get-tuple-element.53.slope, bf16[1024,1024]{1,0:T(8,128)(2,1)} %get-tuple-element.45.x_low, ...), custom_call_target="tpu_custom_call" | custom-call | tf_op jit(solution)/shard_map/pallas_call | solution.py:487
  254.9 1.0 bitcast_reduce_fusion
  255.9 0.8 copy.57
  256.8 0.5 reduce-scatter.16.cloned.1.call-update
  257.3 0.5 reduce-scatter.20.cloned.1.call-update
  257.9 30.4 %shard_map.292 = (bf16[2048,1408]{1,0:T(8,128)(2,1)}, bf16[1024,2048]{1,0:T(8,128)(2,1)}, f32[1024,128]{1,0:T(8,128)}) custom-call(bf16[1024,2048]{1,0:T(8,128)(2,1)} %tok.3, f32[1024,128]{1,0:T(8,128)} %get-tuple-element.50.inverse, f32[1,2048]{1,0:T(1,128)} %bitcast.35, bf16[1024,2048]{1,0:T(8,128)(2,1)} %get-tuple-element.43.normed, ...), custom_call_target="tpu_custom_call" | custom-call | tf_op jit(solution)/shard_map/pallas_call | solution.py:487
  288.4 0.7 reduce-scatter.12.cloned.1.call-update
  289.2 0.6 reduce-scatter.18.cloned.1.call-update
  289.9 0.8 dynamic_slice.11
  290.6 0.2 slice_reduce_fusion
  290.9 8.6 %psum.50 = f32[1024]{0:T(1024)S(1)} all-reduce(f32[1024]{0:T(1024)S(1)} %slice_reduce_fusion), channel_id=1, replica_groups=mesh['dp'=8,'mp'=4] {'mp'}, use_global_device_ids=true, to_apply=%region_4.5 | all-reduce | flops 1024 | bytes 8192 | tf_op jit(solution)/shard_map/psum | solution.py:593
  299.5 0.2 slice_reduce_fusion.1
  299.8 0.8 copy.58
  300.6 26.1 %reduce-scatter.16.cloned.1.call-done = bf16[256,1024]{1,0:T(8,128)(2,1)} async-done(((bf16[2048,1024]{1,0:T(8,128)(2,1)}), bf16[256,1024]{1,0:T(8,128)(2,1)}) %reduce-scatter.16.cloned.1.call-update) | async-done | bytes 524304 | tf_op jit(solution)/shard_map/reduce_scatter | solution.py:580
  326.7 2.1 convert_element_type.64
  328.9 52.4 %reduce-scatter.20.cloned.1.call-done = bf16[1024,256]{1,0:T(8,128)(2,1)} async-done(((bf16[1024,2048]{1,0:T(8,128)(2,1)}), bf16[1024,256]{1,0:T(8,128)(2,1)}) %reduce-scatter.20.cloned.1.call-update) | async-done | bytes 524304 | tf_op jit(solution)/shard_map/reduce_scatter | solution.py:580
  381.3 2.1 convert_element_type.68
  383.4 77.1 %reduce-scatter.14.cloned.1.call-done = bf16[1024,512]{1,0:T(8,128)(2,1)} async-done(((bf16[1024,2048]{1,0:T(8,128)(2,1)}), bf16[1024,512]{1,0:T(8,128)(2,1)}) %reduce-scatter.14.cloned.1.call-update) | async-done | bytes 1048592 | tf_op jit(solution)/shard_map/reduce_scatter | solution.py:580
  460.5 79.6 %reduce-scatter.12.cloned.1.call-done = bf16[1024,512]{1,0:T(8,128)(2,1)} async-done(((bf16[1024,2048]{1,0:T(8,128)(2,1)}), bf16[1024,512]{1,0:T(8,128)(2,1)}) %reduce-scatter.12.cloned.1.call-update) | async-done | bytes 1048592 | tf_op jit(solution)/shard_map/reduce_scatter | solution.py:580
  540.1 4.5 fusion.6
  544.6 25.1 %all-reduce.4 = (f32[5,1024]{1,0:T(8,128)S(1)}, f32[5,64]{1,0:T(8,128)S(1)}, f32[2,16]{1,0:T(2,128)S(1)}, f32[2,1024]{1,0:T(2,128)S(1)}, f32[512]{0:T(512)}) all-reduce(f32[5,1024]{1,0:T(8,128)S(1)} %slice-done, f32[5,64]{1,0:T(8,128)S(1)} %copy.58, f32[2,16]{1,0:T(2,128)S(1)} %bitcast.40, ...), channel_id=1, replica_groups=mesh['dp'=8,'mp'=4] {'dp'}, use_global_device_ids=true, to_apply=%region_10.11 | all-reduce | flops 8032 | bytes 64256 | tf_op jit(solution)/shard_map/psum | solution.py:604
  569.7 0.6 slice.83
  570.3 0.6 slice.84
  570.9 0.6 fusion.7
  571.5 0.1 reshape_squeeze.3
  571.5 0.6 reduce_sum.48
  572.2 0.6 slice.70
  572.8 0.5 slice_bitcast_fusion
  573.3 0.5 slice_bitcast_fusion.2
  573.8 29.7 %reduce-scatter.18.cloned.1.call-done = bf16[256,1408]{1,0:T(8,128)(2,1)} async-done(((bf16[2048,1408]{1,0:T(8,128)(2,1)}), bf16[256,1408]{1,0:T(8,128)(2,1)}) %reduce-scatter.18.cloned.1.call-update) | async-done | bytes 720912 | tf_op jit(solution)/shard_map/reduce_scatter | solution.py:580
  603.5 0.9 slice.80
  604.4 0.8 copy.55
  605.2 0.9 slice_convert_fusion.1
  606.0 0.7 copy.54
  606.7 2.1 slice_convert_fusion
  608.9 15.9 %reduce-scatter.22.cloned.1.call-done = bf16[64,256]{1,0:T(8,128)(2,1)} async-done(((bf16[256,256]{1,0:T(8,128)(2,1)}), bf16[64,256]{1,0:T(8,128)(2,1)}) %reduce-scatter.22.cloned.1.call-update) | async-done | bytes 32784
  624.8 0.9 copy.56
  625.7 0.7 copy.53
  (63 shorter events, 0.7 us)
Async XLA Ops:
  7.2 2.3 copy-start.12
  7.2 2.4 copy-start.13
  7.2 2.5 copy-start.5
  7.2 19.0 %copy-start.1 = (f32[256,1024]{1,0:T(8,128)S(1)}, f32[256,1024]{1,0:T(8,128)}, u32[]{:S(2)}) copy-start(f32[256,1024]{1,0:T(8,128)} %param.21) | copy-start | bytes 3145732
  7.2 42.8 %all-gather.8.cloned.1.call-start = ((), (), s32[]{:S(2)}) async-start(), calls=%async_computation.9 | async-start | bytes 4718592 | tf_op jit(solution)/shard_map/all_gather | solution.py:521
  9.4 16.8 %copy-start.8 = (f32[256,16]{0,1:T(8,128)S(1)}, f32[256,16]{0,1:T(8,128)}, u32[]{:S(2)}) copy-start(f32[256,16]{0,1:T(8,128)} %param.23) | copy-start | bytes 49156
  9.5 86.3 %all-gather.6.cloned.1.call-start = ((), (), s32[]{:S(2)}) async-start(), calls=%async_computation.8 | async-start | bytes 6488064 | tf_op jit(solution)/shard_map/all_gather | solution.py:520
  26.1 1.6 copy-start.2
  26.4 2.2 copy-start.14
  26.4 2.4 copy-start.17
  26.4 2.5 copy-start.15
  26.5 2.5 copy-start.16
  26.5 3.1 copy-start.10
  26.5 4.3 copy-start.7
  26.5 4.2 copy-start.11
  27.6 109.3 %all-gather.4.cloned.1.call-start = ((), (), s32[]{:S(2)}) async-start(), calls=%async_computation.7 | async-start | bytes 4718592 | tf_op jit(solution)/shard_map/all_gather | solution.py:522
  28.5 271.3 %reduce-scatter.24.cloned.1.call-start = ((), (), s32[]{:S(2)}) async-start(), calls=%async_computation.16 | async-start | bytes 163840
  255.9 34.8 %copy-start.4 = (f32[5,1280]{1,0:T(8,128)}, f32[5,1280]{1,0:T(8,128)S(1)}, u32[]{:S(2)}) copy-start(f32[5,1280]{1,0:T(8,128)S(1)} %bitcast_reduce_fusion) | copy-start | bytes 76804
  256.7 70.0 %reduce-scatter.16.cloned.1.call-start = ((), (), s32[]{:S(2)}) async-start(), calls=%async_computation.12 | async-start | bytes 4718592 | tf_op jit(solution)/shard_map/reduce_scatter | solution.py:580
  257.3 124.0 %reduce-scatter.20.cloned.1.call-start = ((), (), s32[]{:S(2)}) async-start(), calls=%async_computation.14 | async-start | bytes 4718592 | tf_op jit(solution)/shard_map/reduce_scatter | solution.py:580
  257.9 202.6 %reduce-scatter.14.cloned.1.call-start = ((), (), s32[]{:S(2)}) async-start(), calls=%async_computation.11 | async-start | bytes 5242880 | tf_op jit(solution)/shard_map/reduce_scatter | solution.py:580
  288.3 251.7 %reduce-scatter.12.cloned.1.call-start = ((), (), s32[]{:S(2)}) async-start(), calls=%async_computation.10 | async-start | bytes 5242880 | tf_op jit(solution)/shard_map/reduce_scatter | solution.py:580
  289.1 314.4 %reduce-scatter.18.cloned.1.call-start = ((), (), s32[]{:S(2)}) async-start(), calls=%async_computation.13 | async-start | bytes 6488064 | tf_op jit(solution)/shard_map/reduce_scatter | solution.py:580
  289.1 1.5 copy-start.3
  289.1 10.3 %copy-start.9 = (f32[16,128]{1,0:T(8,128)S(1)}, f32[16,128]{1,0:T(8,128)}, u32[]{:S(2)}) copy-start(f32[16,128]{1,0:T(8,128)} %get-tuple-element.68) | copy-start | bytes 24580
  289.2 10.3 %copy-start.6 = (f32[16,1024]{1,0:T(8,128)S(1)}, f32[16,1024]{1,0:T(8,128)}, u32[]{:S(2)}) copy-start(f32[16,1024]{1,0:T(8,128)} %get-tuple-element.69) | copy-start | bytes 196612
  289.2 10.3 %copy-start = (f32[1024,128]{1,0:T(8,128)S(1)}, f32[1024,128]{1,0:T(8,128)}, u32[]{:S(2)}) copy-start(f32[1024,128]{1,0:T(8,128)} %get-tuple-element.50.inverse) | copy-start | bytes 1572868
  289.8 335.0 %reduce-scatter.22.cloned.1.call-start = ((), (), s32[]{:S(2)}) async-start(), calls=%async_computation.15 | async-start | bytes 163840
  383.4 161.2 %slice-start = ((f32[5,1280]{1,0:T(8,128)}), f32[5,1024]{1,0:T(8,128)S(1)}, s32[]{:S(2)}) async-start(f32[5,1280]{1,0:T(8,128)} %copy-done.4), calls=%async_computation.17 | async-start | bytes 65536 | tf_op jit(solution)/shard_map/slice | solution.py:605
Sparse Core Ops, SparseCore 0:
  10.5 39.4 all-gather.7
  52.5 43.3 all-gather.5
  97.7 37.4 all-gather.3
  256.8 16.7 reduce-scatter.23
  277.2 49.4 reduce-scatter.15
  329.9 51.2 reduce-scatter.19
  383.7 76.7 reduce-scatter.13
  462.8 77.2 reduce-scatter.11
  543.9 59.5 reduce-scatter.17
  605.6 19.1 reduce-scatter.21

commit v2 on v1

--- a/solution.py
+++ b/solution.py
@@ -135,7 +135,7 @@
             earlier = pltpu.roll(x, lag, 0)[8:]
             pre = pre + tap[CONV - 1 - lag : CONV - lag] * jnp.where(place >= lag, earlier, 0.0)
         sg = logistic(pre)
-        slope[rows, pl.ds(c, LANES)] = sg * (1.0 + pre * (1.0 - sg))
+        slope[rows, pl.ds(c, LANES)] = (sg * (1.0 + pre * (1.0 - sg))).astype(bf16)
         out[rows, pl.ds(at, LANES)] = (pre * sg).astype(bf16)
 
     blocks = x_low.shape[0] // BLOCK
@@ -347,7 +347,7 @@
 
 def scan_backward(
     starts, x_low, bc_low, step_low, decay_low, ssd, states, gs, slope, crow, step, sgdt, dpar,
-    gpre, low_xd, dsums, spread, dstate, xs, gx, cbm, acc,
+    gpre, low_xd, dsums, spread, dstate, xs, gx, cbm, acc, tick=None,
 ):
     length, inner = x_low.shape
     width = gpre.shape[1]
@@ -415,6 +415,8 @@
         dsums[0:8, :] += fold(grad_dt)
         dsums[8:16, :] -= fold(grad_decay * step[rows, :])
         dstate[...] = kept_e * dstate[...] + mm_tn(cm, g_in)
+        if tick is not None:
+            tick(i)
         return carry
 
     lax.fori_loop(0, blocks, body, 0)
@@ -481,16 +483,537 @@
     lax.fori_loop(0, gfull.shape[0] // rows, body, 0)
 
 
-def call(kernel, outs, scratch, smem, *operands):
-    whole = pl.BlockSpec(memory_space=pltpu.VMEM)
-    scalar = pl.BlockSpec(memory_space=pltpu.SMEM)
+MESH = pl.DeviceIdType.MESH
+
+
+def remote(source, target, send, receive, **where):
+    return pltpu.make_async_remote_copy(
+        src_ref=source, dst_ref=target, send_sem=send, recv_sem=receive, device_id=where, device_id_type=MESH
+    )
+
+
+def add_into(target, source, rows=64):
+    def body(i, carry):
+        at = pl.ds(pl.multiple_of(i * rows, rows), rows)
+        target[at, :] = (target[at, :].astype(f32) + source[at, :].astype(f32)).astype(target.dtype)
+        return carry
+
+    lax.fori_loop(0, target.shape[0] // rows, body, 0)
+
+
+class Ring:
+    def __init__(self):
+        self.me = lax.axis_index("dp")
+        self.core = self.me % 2
+        chip = self.me // 2
+        y = chip // 2
+        self.pos = 2 * y + (chip + y) % 2
+        self.partner = self.me + 1 - 2 * self.core
+        self.right = self.at(self.pos + 1)
+        self.left = self.at(self.pos + 3)
+        self.across = self.at(self.pos + 2)
+
+    def at(self, pos):
+        pos = pos % 4
+        y = pos // 2
+        return (2 * y + (pos + y) % 2) * 2 + self.core
+
+
+def greet(ring, everyone):
+    barrier = pltpu.get_barrier_semaphore()
+    n, z = lax.axis_size("mp"), lax.axis_index("mp")
+    if everyone:
+        size = lax.axis_size("dp")
+        close = [(ring.me + i) % size for i in range(1, size)]
+    else:
+        close = [ring.partner, ring.right, ring.left]
+    for other in close:
+        pl.semaphore_signal(barrier, inc=1, device_id={"dp": other}, device_id_type=MESH)
+    for i in range(1, n):
+        pl.semaphore_signal(barrier, inc=1, device_id={"mp": (z + i) % n}, device_id_type=MESH)
+    pl.semaphore_wait(barrier, len(close) + n - 1)
+
+
+class Scatter:
+    def __init__(self, ring, shard, cores, parts, wholes, sems):
+        self.ring, self.shard = ring, shard
+        self.cores, self.parts, self.wholes = cores, parts, wholes
+        self.core_send, self.core_recv, self.ring_send, self.ring_recv = sems
+        self.half = cores.shape[1] // 2
+
+    def upper(self, r):
+        return self.shard(r).at[pl.ds(0, self.half), :]
+
+    def lower(self, r):
+        return self.shard(r).at[pl.ds(self.half, self.half), :]
+
+    def core_copy(self, chip):
+        ring = self.ring
+        return remote(
+            self.shard(2 * chip + 1 - ring.core), self.cores.at[chip],
+            self.core_send.at[chip], self.core_recv.at[chip], dp=ring.partner,
+        )
+
+    def ring_copy(self, k):
+        ring = self.ring
+        source = (self.upper(ring.across), self.lower(ring.across), self.shard(ring.right), self.shard(ring.left))[k]
+        target = (self.parts.at[0], self.parts.at[1], self.wholes.at[0], self.wholes.at[1])[k]
+        return remote(
+            source, target, self.ring_send.at[k], self.ring_recv.at[k], dp=(ring.right, ring.left)[k % 2]
+        )
+
+    def start(self, chip):
+        self.core_copy(chip).start()
+
+    def first(self):
+        def body(chip, carry):
+            self.core_copy(chip).wait_recv()
+            add_into(self.shard(2 * chip + self.ring.core), self.cores.at[chip])
+            return carry
+
+        lax.fori_loop(0, 4, body, 0)
+        self.ring_copy(0).start()
+        self.ring_copy(1).start()
+
+    def second(self):
+        self.ring_copy(0).wait_recv()
+        add_into(self.upper(self.ring.right), self.parts.at[0])
+        self.ring_copy(2).start()
+        self.ring_copy(1).wait_recv()
+        add_into(self.lower(self.ring.left), self.parts.at[1])
+        self.ring_copy(3).start()
+
+    def finish(self, out, rows=64):
+        self.ring_copy(2).wait_recv()
+        self.ring_copy(3).wait_recv()
+        own = self.shard(self.ring.me)
+
+        def body(i, carry):
+            at = pl.ds(pl.multiple_of(i * rows, rows), rows)
+            out[at, :] = own[at, :].astype(f32) + self.wholes[0, at, :].astype(f32) + self.wholes[1, at, :].astype(f32)
+            return carry
+
+        lax.fori_loop(0, out.shape[0] // rows, body, 0)
+
+        def done(chip, carry):
+            self.core_copy(chip).wait_send()
+            return carry
+
+        lax.fori_loop(0, 4, done, 0)
+        for k in range(4):
+            self.ring_copy(k).wait_send()
+
+
+class Line:
+    def __init__(self, part, slots, sems, total):
+        self.part, self.slots, self.total = part, slots, total
+        self.send, self.recv = sems
+        self.n, self.z = lax.axis_size("mp"), lax.axis_index("mp")
+        self.blocks = part.shape[0] // BLOCK
+        self.own = part.shape[1] // self.n
+        self.place = (self.z, self.n - 1 - self.z)
+        self.count = self.blocks * (self.n - 1)
+
+    def rows(self, t):
+        return pl.ds(pl.multiple_of(t * BLOCK, BLOCK), BLOCK)
+
+    def columns(self, q):
+        return pl.ds(pl.multiple_of(q * self.own, self.own), self.own)
+
+    def copy(self, side, k):
+        d = k // self.blocks
+        q = self.n - 1 - d if side == 0 else d
+        source = self.part.at[self.rows(k - d * self.blocks), self.columns(q)]
+        return remote(
+            source, self.slots.at[side, k], self.send.at[side, k], self.recv.at[side, k],
+            mp=self.z + 1 if side == 0 else self.z - 1,
+        ), source
+
+    def inject(self, k):
+        for side in range(2):
+            @pl.when(self.place[side] == 0)
+            def _():
+                self.copy(side, k)[0].start()
+
+    def forward(self, k, hop):
+        for side in range(2):
+            @pl.when(self.place[side] == hop)
+            def _():
+                copy, source = self.copy(side, k)
+                copy.wait_recv()
+                add_into(source, self.slots.at[side, k])
+                copy.start()
+
+    def finish(self, t):
+        self.total[...] = self.part[self.rows(t), self.columns(self.z)].astype(f32)
+        for side in range(2):
+            @pl.when(self.place[side] >= 1)
+            def _():
+                k = (self.n - 1 - self.place[side]) * self.blocks + t
+                self.copy(side, k)[0].wait_recv()
+                self.total[...] += self.slots[side, k].astype(f32)
+
+    def drain(self):
+        def body(k, carry):
+            for side in range(2):
+                @pl.when(self.place[side] + k // self.blocks <= self.n - 2)
+                def _():
+                    self.copy(side, k)[0].wait_send()
+            return carry
+
+        lax.fori_loop(0, self.count, body, 0)
+
+    def order(self, i):
+        z = self.z
+        far = jnp.where(z < 2, 3 - i, i)
+        near = z + 1 - 2 * (z % 2)
+        return jnp.where(i < 2, far, jnp.where(i == 2, near, z))
+
+
+class Loads:
+    def __init__(self, sems):
+        self.sems, self.pairs = sems, []
+
+    def start(self, source, target):
+        i = len(self.pairs)
+        copy = pltpu.make_async_copy(source, target, self.sems.at[i])
+        copy.start()
+        self.pairs.append(copy)
+        return copy
+
+
+def output_kernel(
+    starts, tok, gn, wout, cot, x_low, ssd, states, gs, slope, xin, bc_low, step, sgdt, step_low, decay_low,
+    taps, crow, dpar,
+    out, dwout, low_xd, csums, dsums,
+    v_gn, v_wout, v_cot, v_x, v_ssd, v_states, v_gs, v_slope, v_xin,
+    part, slots, cores, parts, wholes,
+    pos, rpos, spread, gpre, dstate, xs, gx, cbm, acc,
+    load_sems, cot_sems, line_send, line_recv, core_send, core_recv, ring_send, ring_recv,
+):
+    ring = Ring()
+    loads = Loads(load_sems)
+    n = lax.axis_size("mp")
+    z = lax.axis_index("mp")
+    own = part.shape[1] // n
+    load_gn = loads.start(gn, v_gn)
+    load_wout = loads.start(wout, v_wout)
+    later = [
+        loads.start(source, target)
+        for source, target in (
+            (x_low, v_x), (ssd, v_ssd), (states, v_states), (gs, v_gs), (slope, v_slope), (xin, v_xin),
+        )
+    ]
+    greet(ring, False)
+    total = gx.at[:, pl.ds(0, own)]
+    line = Line(part, slots, (line_send, line_recv), total)
+    chunk = v_cot.shape[2]
+    shard = dwout.shape[1]
+
+    def cot_copy(j):
+        return pltpu.make_async_copy(
+            cot.at[:, pl.ds(pl.multiple_of(j * chunk, chunk), chunk)], v_cot.at[j % 2], cot_sems.at[j % 2]
+        )
+
+    cot_copy(0).start()
+    fill_spread(spread)
+    fill_positions(starts, pos, rpos)
+    load_gn.wait()
+    load_wout.wait()
+
+    def quarter(i, carry):
+        q = line.order(i)
+        columns = line.columns(q)
+        for r in range(0, part.shape[0], 512):
+            part[r : r + 512, columns] = mm(v_gn[r : r + 512, :], v_wout[:, columns]).astype(bf16)
+
+        @pl.when(i == 0)
+        def _():
+            line.inject(0)
+            line.inject(1)
+
+        line.inject(i + 2)
+        return carry
+
+    lax.fori_loop(0, n, quarter, 0)
+
+    grads = v_wout
+    scatter = Scatter(
+        ring, lambda r: grads.at[:, pl.ds(pl.multiple_of(r * shard, shard), shard)], cores, parts, wholes,
+        (core_send, core_recv, ring_send, ring_recv),
+    )
+
+    def weight(j, carry):
+        @pl.when(j < 3)
+        def _():
+            cot_copy(j + 1).start()
+
+        cot_copy(j).wait()
+        columns = pl.ds(pl.multiple_of(j * chunk, chunk), chunk)
+        for r in range(0, grads.shape[0], 256):
+            grads[r : r + 256, columns] = mm_tn(v_gn[:, r : r + 256], v_cot[j % 2]).astype(bf16)
+        scatter.start(j)
+
+        @pl.when(j == 2)
+        def _():
+            line.forward(0, 1)
+            line.inject(6)
+
+        return carry
+
+    lax.fori_loop(0, 4, weight, 0)
+    v_tok = v_cot.at[0]
+    load_tok = loads.start(tok.at[:, pl.ds(pl.multiple_of(z * own, own), own)], v_tok)
+    for copy in later[:5]:
+        copy.wait()
+
+    def scan_tick(i):
+        @pl.when(i == 0)
+        def _():
+            scatter.first()
+
+        @pl.when(i == 1)
+        def _():
+            scatter.second()
+
+        line.forward(i + 1, 1)
+        line.forward(i, 2)
+        line.inject(i + 7)
+
+    scan_backward(
+        starts, v_x, bc_low, step_low, decay_low, v_ssd, v_states, v_gs, v_slope, crow, step, sgdt, dpar,
+        gpre, low_xd, dsums, spread, dstate, xs, gx, cbm, acc, scan_tick,
+    )
+    line.inject(11)
+    line.forward(5, 1)
+    scatter.finish(dwout)
+    later[5].wait()
+    convolve_back(v_xin, gpre, taps, pos, rpos, low_xd, csums)
+    line.forward(6, 1)
+    line.forward(7, 1)
+    load_tok.wait()
+
+    def last(t, carry):
+        line.finish(t)
+        out[line.rows(t), :] = (v_tok[line.rows(t), :].astype(f32) + total[...]).astype(bf16)
+        return carry
+
+    lax.fori_loop(0, line.blocks, last, 0)
+    line.drain()
+
+
+def input_kernel(
+    tok, inverse, gain, normed, low_gate, low_xd, wz, wxd, cot, csums, sums, dsums,
+    grad, dwz, dwxd, smalls,
+    v_tok, v_normed, v_gate, v_xd, v_wz, v_wxd, v_cot,
+    part, slots, total, z_grads, z_cores, z_parts, z_wholes, x_grads, x_cores, x_parts, x_wholes,
+    rowacc, rows_own, rows_in, colacc, dp_in, bc_in, gain_in,
+    load_sems, line_send, line_recv, z_core_send, z_core_recv, z_ring_send, z_ring_recv,
+    x_core_send, x_core_recv, x_ring_send, x_ring_recv,
+    rows_send, rows_recv, dp_send, dp_recv, mp_send, mp_recv,
+):
+    ring = Ring()
+    loads = Loads(load_sems)
+    n = lax.axis_size("mp")
+    z = lax.axis_index("mp")
+    size = lax.axis_size("dp")
+    length, features = part.shape
+    inner = v_gate.shape[1]
+    width = smalls.shape[1]
+    first = [
+        loads.start(source, target)
+        for source, target in ((low_gate, v_gate), (wz, v_wz), (low_xd, v_xd), (wxd, v_wxd), (tok, v_tok))
+    ]
+    own = features // n
+    own_columns = pl.ds(pl.multiple_of(z * own, own), own)
+    later = [
+        loads.start(source, target)
+        for source, target in ((normed, v_normed), (cot.at[:, own_columns], v_cot))
+    ]
+    greet(ring, True)
+    line = Line(part, slots, (line_send, line_recv), total)
+    rowacc[...] = jnp.zeros_like(rowacc)
+    for copy in first:
+        copy.wait()
+
+    def quarter(i, carry):
+        columns = line.columns(line.order(i))
+        for r in range(0, length, 256):
+            rows = slice(r, r + 256)
+            here = mm_nt(v_gate[rows, :], v_wz[columns, :]) + mm_nt(v_xd[rows, :], v_wxd[columns, :])
+            part[rows, columns] = here.astype(bf16)
+            along = here * (v_tok[rows, columns].astype(f32) * inverse[rows, :1])
+            folded = fold(along)
+            if r == 0:
+                colacc[:, columns] = folded
+            else:
+                colacc[:, columns] += folded
+            along = along * gain[:, columns]
+            sum_lanes = along[:, :LANES]
+            for c in range(LANES, own, LANES):
+                sum_lanes = sum_lanes + along[:, c : c + LANES]
+            rowacc[rows, :] += sum_lanes
+
+        @pl.when(i == 0)
+        def _():
+            line.inject(0)
+            line.inject(1)
+
+        line.inject(i + 2)
+        return carry
+
+    lax.fori_loop(0, n, quarter, 0)
+    line.forward(0, 1)
+
+    for b in range(length // BLOCK):
+        columns = slice(b * BLOCK, (b + 1) * BLOCK)
+        line_sum = jnp.sum(rowacc[columns, :].T, axis=0, keepdims=True)
+        rows_own[:, columns] = jnp.broadcast_to(line_sum, (8, BLOCK))
+
+    def rows_copy(i):
+        return remote(
+            rows_own, rows_in.at[i - 1], rows_send.at[i - 1], rows_recv.at[i - 1], mp=(z + i) % n
+        )
+
+    def dp_copy(i):
+        return remote(
+            smalls, dp_in.at[i - 1], dp_send.at[i - 1], dp_recv.at[i - 1], dp=(ring.me + i) % size
+        )
+
+    def bc_copy(i):
+        return remote(
+            smalls.at[pl.ds(0, 8), pl.ds(inner, width - inner)], bc_in.at[i - 1],
+            mp_send.at[i - 1], mp_recv.at[i - 1], mp=(z + i) % n,
+        )
+
+    def gain_copy(i):
+        return remote(
+            smalls.at[pl.ds(8, 8), pl.ds(0, inner)], gain_in.at[i - 1],
+            mp_send.at[n + i - 2], mp_recv.at[n + i - 2], mp=(z + i) % n,
+        )
+
+    smalls[...] = jnp.zeros_like(smalls)
+    for k in range(CONV + 1):
+        smalls[k : k + 1, :] = jnp.sum(csums[8 * k : 8 * k + 8, :], axis=0, keepdims=True)
+    for k in range(2):
+        smalls[CONV + 1 + k : CONV + 2 + k, :inner] = jnp.sum(sums[8 * k : 8 * k + 8, :], axis=0, keepdims=True)
+        smalls[7:8, k * LANES : (k + 1) * LANES] = jnp.sum(dsums[8 * k : 8 * k + 8, :], axis=0, keepdims=True)
+    for k in range(features // inner):
+        smalls[8 + k : 9 + k, :inner] = jnp.sum(colacc[:, k * inner : (k + 1) * inner], axis=0, keepdims=True)
+    for i in range(1, n):
+        rows_copy(i).start()
+    for i in range(1, size):
+        dp_copy(i).start()
+
+    later[0].wait()
+    shard = dwz.shape[0]
+    z_scatter = Scatter(
+        ring, lambda r: z_grads.at[pl.ds(pl.multiple_of(r * shard, shard), shard), :], z_cores, z_parts, z_wholes,
+        (z_core_send, z_core_recv, z_ring_send, z_ring_recv),
+    )
+    x_scatter = Scatter(
+        ring, lambda r: x_grads.at[pl.ds(pl.multiple_of(r * shard, shard), shard), :], x_cores, x_parts, x_wholes,
+        (x_core_send, x_core_recv, x_ring_send, x_ring_recv),
+    )
+
+    def weight(j, right, grads):
+        for c in range(0, 2 * shard, shard):
+            rows = pl.ds(pl.multiple_of(j * 2 * shard + c, shard), shard)
+            left = v_normed[:, rows]
+            for at, w in tiles(grads.shape[1], 512):
+                grads[rows, at : at + w] = mm_tn(left, right[:, at : at + w]).astype(bf16)
+
+    def z_weight(j, carry):
+        weight(j, v_gate, z_grads)
+        z_scatter.start(j)
+
+        @pl.when(j % 2 == 1)
+        def _():
+            line.inject(6 + j // 2)
+            line.forward(1 + j // 2, 1)
+
+        return carry
+
+    lax.fori_loop(0, 4, z_weight, 0)
+    line.forward(0, 2)
+
+    def x_weight(j, carry):
+        weight(j, v_xd, x_grads)
+        x_scatter.start(j)
+
+        @pl.when(j == 1)
+        def _():
+            z_scatter.first()
+
+        @pl.when(j % 2 == 1)
+        def _():
+            line.inject(8 + j // 2)
+            line.forward(3 + j // 2, 1)
+            line.forward(1 + j // 2, 2)
+
+        return carry
+
+    lax.fori_loop(0, 4, x_weight, 0)
+    z_scatter.second()
+    line.inject(10)
+    line.inject(11)
+    x_scatter.first()
+
+    for i in range(1, size):
+        dp_copy(i).wait()
+    smalls[...] += functools.reduce(lambda a, b: a + b, [dp_in[i] for i in range(size - 1)])
+    for i in range(1, n):
+        bc_copy(i).start()
+        gain_copy(i).start()
+    line.forward(5, 1)
+    line.forward(3, 2)
+    z_scatter.finish(dwz)
+    for i in range(1, n):
+        rows_copy(i).wait()
+    rows_own[...] += functools.reduce(lambda a, b: a + b, [rows_in[i] for i in range(n - 1)])
+    x_scatter.second()
+    line.forward(6, 1)
+    line.forward(7, 1)
+    for i in range(1, n):
+        bc_copy(i).wait()
+        gain_copy(i).wait()
+    smalls[0:8, inner:] += functools.reduce(lambda a, b: a + b, [bc_in[i] for i in range(n - 1)])
+    smalls[8:16, :inner] += functools.reduce(lambda a, b: a + b, [gain_in[i] for i in range(n - 1)])
+    x_scatter.finish(dwxd)
+    later[1].wait()
+
+    def last(t, carry):
+        line.finish(t)
+        rows = line.rows(t)
+        mean = jnp.broadcast_to(rows_own[0:1, rows] / features, (LANES, BLOCK)).T
+        for c in range(0, own, LANES):
+            columns = pl.ds(pl.multiple_of(z * own + c, LANES), LANES)
+            hat = v_tok[rows, columns].astype(f32) * inverse[rows, :]
+            change = inverse[rows, :] * (total[:, c : c + LANES] * gain[:, columns] - hat * mean)
+            grad[rows, c : c + LANES] = (v_cot[rows, c : c + LANES].astype(f32) + change).astype(bf16)
+        return carry
+
+    lax.fori_loop(0, line.blocks, last, 0)
+    line.drain()
+
+
+def gate_back_kernel(gate, ssd, x_low, gnorm, crow, stat, gn, low_gate, gs, sums, *, width):
+    gate_backward(gate, ssd, x_low, gnorm, crow, stat, width, gn, low_gate, gs, sums)
+
+
+def call(kernel, outs, scratch, smem, *operands, places=None, sems=(), collective=None):
+    spaces = {"s": pltpu.SMEM, "v": pltpu.VMEM, "a": pl.ANY}
+    if places is None:
+        places = "s" * smem + "v" * (len(operands) - smem)
+    extra = {} if collective is None else dict(collective_id=collective, has_side_effects=True)
     return pl.pallas_call(
         kernel,
         out_shape=[jax.ShapeDtypeStruct(shape, kind) for shape, kind in outs],
-        in_specs=[scalar if i < smem else whole for i in range(len(operands))],
-        out_specs=[whole] * len(outs),
-        scratch_shapes=[pltpu.VMEM(shape, kind) for shape, kind in scratch],
-        compiler_params=pltpu.CompilerParams(vmem_limit_bytes=VMEM_LIMIT),
+        in_specs=[pl.BlockSpec(memory_space=spaces[c]) for c in places],
+        out_specs=[pl.BlockSpec(memory_space=pltpu.VMEM)] * len(outs),
+        scratch_shapes=[pltpu.VMEM(shape, kind) for shape, kind in scratch]
+        + [pltpu.SemaphoreType.DMA(shape) for shape in sems],
+        compiler_params=pltpu.CompilerParams(vmem_limit_bytes=VMEM_LIMIT, **extra),
     )(*operands)
 
 
@@ -532,7 +1055,7 @@
     ) = call(
         forward_kernel,
         [
-            ((T, D), bf16), ((T, LANES), f32), ((T + 8, width), f32), ((T, width), f32), ((T, inner), f32),
+            ((T, D), bf16), ((T, LANES), f32), ((T + 8, width), f32), ((T, width), bf16), ((T, inner), f32),
             ((T, inner), bf16), ((T, pair), bf16), ((T, LANES), f32), ((T, LANES), f32),
             ((T, LANES), bf16), ((T, LANES), bf16), ((T, inner), bf16), ((blocks, STATE, inner), bf16),
         ],
@@ -549,6 +1072,69 @@
         0, cotangent, wout, gate, ssd, x_low, crow,
     )
     stat = jnp.pad(lax.psum(stat[:, :8], "mp"), ((0, 0), (0, LANES - 8)))
+    if lax.axis_size("dp") == 8 and group == 4:
+        gn, low_gate, gs, sums = call(
+            functools.partial(gate_back_kernel, width=inner * group),
+            [((T, inner), bf16), ((T, inner), bf16), ((T, inner), bf16), ((16, inner), f32)],
+            [],
+            0, gate, ssd, x_low, gnorm, crow, stat,
+        )
+        columns = D // lax.axis_size("dp")
+        messages = blocks * (group - 1)
+        output, w_out_grad, low_xd, csums, dsums = call(
+            output_kernel,
+            [
+                ((T, own), bf16), ((inner, columns), f32), ((T, wide), bf16), ((8 * CONV + 8, width), f32),
+                ((16, LANES), f32),
+            ],
+            [
+                ((T, inner), bf16), ((inner, D), bf16), ((2, T, 2 * columns), bf16), ((T, inner), bf16),
+                ((T, inner), bf16), ((blocks, STATE, inner), bf16), ((T, inner), bf16), ((T, width), bf16),
+                ((T + 8, width), f32),
+                ((T, D), bf16), ((2, messages, BLOCK, own), bf16),
+                ((4, inner, columns), bf16), ((2, inner // 2, columns), bf16), ((2, inner, columns), bf16),
+                ((T, LANES), jnp.int32), ((T, LANES), jnp.int32), ((LANES, inner), bf16), ((T + 8, width), f32),
+                ((STATE, inner), f32), ((BLOCK, inner), bf16), ((BLOCK, inner), f32), ((BLOCK, BLOCK), f32),
+                ((BLOCK, BLOCK), f32),
+            ],
+            0, starts, tokens, gn, wout, cotangent, x_low, ssd, states, gs, slope, xin, bc_low, step, sgdt,
+            step_low, decay_low, taps, crow, dpar,
+            places="s" + "a" * 10 + "v" * 8,
+            sems=[(9,), (2,), (2, messages), (2, messages), (4,), (4,), (4,), (4,)],
+            collective=1,
+        )
+        size = lax.axis_size("dp")
+        input_grad, w_z_grad, dwxd_own, smalls = call(
+            input_kernel,
+            [((T, own), bf16), ((shard, inner), f32), ((shard, wide), f32), ((16, width), f32)],
+            [
+                ((T, D), bf16), ((T, D), bf16), ((T, inner), bf16), ((T, wide), bf16), ((D, inner), bf16),
+                ((D, wide), bf16), ((T, own), bf16),
+                ((T, D), bf16), ((2, messages, BLOCK, own), bf16), ((BLOCK, own), f32),
+                ((D, inner), bf16), ((4, shard, inner), bf16), ((2, shard // 2, inner), bf16), ((2, shard, inner), bf16),
+                ((D, wide), bf16), ((4, shard, wide), bf16), ((2, shard // 2, wide), bf16), ((2, shard, wide), bf16),
+                ((T, LANES), f32), ((8, T), f32), ((group - 1, 8, T), f32), ((8, D), f32),
+                ((size - 1, 16, width), f32), ((group - 1, 8, pair), f32), ((group - 1, 8, inner), f32),
+            ],
+            0, tokens, inverse, gain, normed, low_gate, low_xd, wz, wxd, cotangent, csums, sums, dsums,
+            places="avvaaaaaavvv",
+            sems=[
+                (7,), (2, messages), (2, messages), (4,), (4,), (4,), (4,), (4,), (4,), (4,), (4,),
+                (group - 1,), (group - 1,), (size - 1,), (size - 1,), (2 * group - 2,), (2 * group - 2,),
+            ],
+            collective=2,
+        )
+        bc = lax.dynamic_slice_in_dim(smalls[: CONV + 1, inner:], rank * (pair // group), pair // group, 1)
+        in_gain = lax.dynamic_slice_in_dim(smalls[8 : 8 + D // inner, :inner].reshape(D), rank * own, own, 0)
+        w_bc_grad = lax.psum_scatter(
+            dwxd_own[:, inner:width].astype(bf16), "mp", scatter_dimension=1, tiled=True
+        ).astype(f32)
+        return (
+            output, input_grad, w_z_grad, dwxd_own[:, :inner], w_bc_grad, dwxd_own[:, width : width + heads],
+            w_out_grad, smalls[:CONV, :inner], smalls[CONV, :inner], bc[:CONV], bc[CONV],
+            smalls[7, :heads], smalls[7, LANES : LANES + heads],
+            jnp.sum(smalls[6, :inner].reshape(heads, HEADDIM), axis=1), in_gain, smalls[5, :inner],
+        )
     branch, dwout, dwz, low_gate, gs, sums = call(
         functools.partial(middle_kernel, width=inner * group),
         [

time: 634 us -> 396 us (0.62)
  waiting for transfers between devices: 348 us -> 72.4 us
  Pallas kernels: 158 us -> 230 us
  blocking collectives: 80.8 us -> 47.1 us
  local copies, waits for them, and re-layouts: 12.9 us -> 24 us
  other arithmetic: 19.1 us -> 8.43 us
    reduce_scatter x5 -> x0, waiting for transfers between devices: 265 us -> none  [scatter(): return lax.psum_scatter(v, axis, scatter_dimension=dim, tiled=True)]
    pallas_call x5, Pallas kernels: 158 us -> 230 us  [call(): pl.pallas_call(kernel, out_shape=[jax.ShapeDtypeStruct(shape, kind) for s...]
    psum x2 -> x0, blocking collectives: 33.7 us -> none  [the longest x1 25.1 us: per_device(): lax.psum((csums[:, :inner], csums_bc, sums, dsums, in_gain), 'dp')]
    convert_element_type x4 -> x0, other arithmetic: 7.19 us -> none  [the longest x1 2.13 us: per_device(): w_z_grad = scatter(dwz, 'dp', 0).astype(f32)]
    unnamed x12 -> x5, waiting for transfers between devices: 18.4 us -> 11.3 us
  transfers between devices with their start and end apart: 10 -> 4, of which waited for: 8 -> 3; matrix products, arithmetic and copies ran while one was open for 4% -> 4% of each run, Pallas kernels for 11% -> 10%
where the time goes in v2:
time: 396 us
  Pallas kernels  230 us (58%)
  waiting for transfers between devices  72.4 us (18%)
  blocking collectives  47.1 us (12%)
  local copies, waits for them, and re-layouts  24 us (6%)
  between operations  13.9 us (4%)
  other arithmetic  8.43 us (2%)
    pallas_call x5, Pallas kernels, call(): pl.pallas_call(kernel, out_shape=[jax.ShapeDtypeStruct(shape, kind) for s...  230 us
    all_gather x1, waiting for transfers between devices, per_device(): wxd = lax.all_gather(wxd, 'dp', axis=0, tiled=True)  45.8 us
    psum x1, blocking collectives, per_device(): stat = jnp.pad(lax.psum(stat[:, :8], 'mp'), ((0, 0), (0, LANES - 8)))  30.9 us
    all_gather x1, blocking collectives, per_device(): packed = lax.all_gather(packed, 'mp', axis=1, tiled=True)  16.2 us
    all_gather x1, waiting for transfers between devices, per_device(): wz = lax.all_gather(w_z.astype(bf16), 'dp', axis=0, tiled=True)  15.3 us
    unnamed x5, waiting for transfers between devices  11.3 us
    unnamed x37, local copies, waits for them, and re-layouts  10.1 us
  transfers between devices with their start and end apart: 4, of which 3 were waited for; matrix products, arithmetic and copies ran while one was open for 4% of the time, Pallas kernels for 10%

profile of v2, /device:TPU:0, one launch (start us, length us, event | category | flops | bytes accessed | tf_op | source)
XLA Modules:
  0.0 395.7 jit_solution(5103521911541816279)
XLA Ops:
  7.2 0.0 copy-start.5
  7.2 0.0 copy-start
  7.2 0.0 all-gather.6.cloned.1.call-start
  7.2 2.2 convert_element_type.27
  9.4 0.0 copy-start.6
  9.4 0.0 copy-start.4
  9.5 0.0 copy-start.7
  9.5 0.0 all-gather.6.cloned.1.call-update
  9.5 0.0 all-gather.4.cloned.1.call-start
  9.5 0.8 copy.37
  10.3 0.7 copy.38
  11.1 0.9 pad_maximum_fusion
  12.0 16.2 %all_gather.12 = f32[261,256]{0,1:T(8,128)S(1)} all-gather(f32[261,64]{0,1:T(8,128)S(1)} %pad_maximum_fusion), channel_id=1, replica_groups=mesh['dp'=8,'mp'=4] {'mp'}, dimensions={1}, use_global_device_ids=true | all-gather | bytes 334080 | tf_op jit(solution)/shard_map/all_gather | solution.py:1036
  28.2 0.1 copy.46
  28.3 1.3 convert_element_type.25
  29.6 0.0 copy-done.5
  29.7 0.1 copy.40
  29.8 1.0 concatenate.13
  30.8 0.0 all-gather.4.cloned.1.call-update
  30.8 0.0 all-gather.8.cloned.1.call-start
  30.9 0.9 convert_element_type.28
  31.8 0.0 all-gather.8.cloned.1.call-update
  31.8 0.0 reduce-scatter.4.cloned.1.call-start
  31.8 0.1 copy.47
  31.9 0.1 broadcast_in_dim.19
  32.0 0.1 stack_reshape.3
  32.1 0.2 reduce-window.9
  32.3 0.6 select_maximum_fusion.3.dpar
  32.9 0.6 select_maximum_fusion.2.crow
  33.5 0.5 bitcast_subtract_fusion.starts
  34.0 0.6 select_maximum_fusion.taps
  34.7 15.3 %all-gather.6.cloned.1.call-done.wz = bf16[2048,1024]{1,0:T(8,128)(2,1)} async-done(((bf16[256,1024]{1,0:T(8,128)(2,1)}), bf16[2048,1024]{1,0:T(8,128)(2,1)}) %all-gather.6.cloned.1.call-update) | async-done | bytes 4194320 | tf_op jit(solution)/shard_map/all_gather | solution.py:1044
  49.9 45.8 %all-gather.4.cloned.1.call-done.wxd = bf16[2048,1408]{1,0:T(8,128)(2,1)} async-done(((bf16[256,1408]{1,0:T(8,128)(2,1)}), bf16[2048,1408]{1,0:T(8,128)(2,1)}) %all-gather.4.cloned.1.call-update) | async-done | bytes 5767184 | tf_op jit(solution)/shard_map/all_gather | solution.py:1043
  95.8 40.5 %shard_map.288 = (bf16[1024,2048]{1,0:T(8,128)(2,1)}, f32[1024,128]{1,0:T(8,128)}, f32[1032,1280]{1,0:T(8,128)}, bf16[1024,1280]{1,0:T(8,128)(2,1)}, f32[1024,10...) custom-call(s32[5]{0:T(128)} %bitcast_subtract_fusion.starts, ...), custom_call_target="tpu_custom_call" | custom-call | tf_op jit(solution)/shard_map/pallas_call | solution.py:1009
  136.2 16.1 %shard_map.289 = (f32[1024,1024]{1,0:T(8,128)}, f32[1024,128]{1,0:T(8,128)}) custom-call(bf16[1024,2048]{1,0:T(8,128)(2,1)} %cot.5, bf16[1024,2048]{1,0:T(8,128)(2,1)} %all-gather.8.cloned.1.call-done.wout, f32[1024,1024]{1,0:T(8,128)} %get-tuple-element.44.gate, bf16[1024,1024]{1,0:T(8,128)(2,1)} %get-tuple-element.45.ssd, ...), custom_call_target="tpu_custom_call" | custom-call | tf_op jit(solution)/shard_map/pallas_call | solution.py:1009
  152.3 30.9 %psum.7 = f32[1024,8]{1,0:T(8,128)S(1)} all-reduce(f32[1024,8]{1,0:T(8,128)} %bitcast.27), channel_id=1, replica_groups=mesh['dp'=8,'mp'=4] {'mp'}, use_global_device_ids=true, to_apply=%region_1.2 | all-reduce | flops 8192 | bytes 65536 | tf_op jit(solution)/shard_map/psum | solution.py:1074
  183.2 0.9 pad.19.stat
  184.0 12.3 %shard_map.290 = (bf16[1024,1024]{1,0:T(8,128)(2,1)}, bf16[1024,1024]{1,0:T(8,128)(2,1)}, bf16[1024,1024]{1,0:T(8,128)(2,1)}, f32[16,1024]{1,0:T(8,128)}) custom-call(f32[1024,1024]{1,0:T(8,128)} %get-tuple-element.44.gate, bf16[1024,1024]{1,0:T(8,128)(2,1)} %get-tuple-element.45.ssd, bf16[1024,1024]{1,0:T(8,128)(2,1)} %get-tuple-element.46.x_low, ...), custom_call_target="tpu_custom_call" | custom-call | tf_op jit(solution)/shard_map/pallas_call | solution.py:1009
  196.4 75.1 %shard_map.291 = (bf16[1024,512]{1,0:T(8,128)(2,1)}, f32[1024,256]{1,0:T(8,128)}, bf16[1024,1408]{1,0:T(8,128)(2,1)}, f32[40,1280]{1,0:T(8,128)}, f32[16,128]{1,0:T(8,128)}) custom-call(s32[5]{0:T(128)} %bitcast_subtract_fusion.starts, bf16[1024,2048]{1,0:T(8,128)(2,1)} %tok.5, bf16[1024,1024]{1,0:T(8,128)(2,1)} %get-tuple-element.49.gn, ...), custom_call_target="tpu_custom_call" | custom-call | tf_op jit(solution)/shard_map/pallas_call | solution.py:1009
  271.4 85.7 %shard_map.292 = (bf16[1024,512]{1,0:T(8,128)(2,1)}, f32[256,1024]{1,0:T(8,128)}, f32[256,1408]{1,0:T(8,128)}, f32[16,1280]{1,0:T(8,128)}) custom-call(bf16[1024,2048]{1,0:T(8,128)(2,1)} %tok.5, f32[1024,128]{1,0:T(8,128)} %get-tuple-element.60.inverse, f32[1,2048]{1,0:T(1,128)} %bitcast.30, bf16[1024,2048]{1,0:T(8,128)(2,1)} %get-tuple-element.61.normed, ...), custom_call_target="tpu_custom_call" | custom-call | tf_op jit(solution)/shard_map/pallas_call | solution.py:1009
  357.2 0.9 slice_bitcast_fusion
  358.1 0.7 slice.58
  358.8 1.5 fusion
  360.3 1.0 slice.75
  361.2 0.8 copy.44
  362.0 0.0 reduce-scatter.4.cloned.1.call-update
  362.0 0.1 constant_dynamic-slice_fusion
  362.1 0.5 slice_bitcast_fusion.3
  362.6 2.4 slice.53
  365.0 0.9 slice.55
  365.9 0.6 slice.59
  366.5 1.4 slice.56
  367.9 0.7 copy.43
  368.5 0.1 reshape_squeeze.3
  368.6 0.6 reduce_sum.9
  369.2 0.7 dynamic_slice.7
  369.9 1.2 slice_bitcast_fusion.1
  371.1 11.3 %reduce-scatter.4.cloned.1.call-done = bf16[64,256]{1,0:T(8,128)(2,1)} async-done(((bf16[256,256]{1,0:T(8,128)(2,1)}), bf16[64,256]{1,0:T(8,128)(2,1)}) %reduce-scatter.4.cloned.1.call-update) | async-done | bytes 32784
  382.4 0.9 copy.45
  383.2 0.7 copy.42
  384.0 1.0 copy.55
  384.9 2.3 copy.56
  387.2 1.0 copy.57
  388.2 1.0 copy.58
  (24 shorter events, 0.1 us)
Async XLA Ops:
  7.2 22.5 %copy-start.5 = (f32[256,16]{0,1:T(8,128)S(1)}, f32[256,16]{0,1:T(8,128)}, u32[]{:S(2)}) copy-start(f32[256,16]{0,1:T(8,128)} %param.23) | copy-start | bytes 49156
  7.2 23.7 %copy-start = (f32[1024,256]{1,0:T(8,128)S(1)}, f32[1024,256]{1,0:T(8,128)}, u32[]{:S(2)}) copy-start(f32[1024,256]{1,0:T(8,128)} %param.24) | copy-start | bytes 3145732
  7.2 42.7 %all-gather.6.cloned.1.call-start = ((), (), s32[]{:S(2)}) async-start(), calls=%async_computation.2 | async-start | bytes 4718592 | tf_op jit(solution)/shard_map/all_gather | solution.py:1044
  9.4 22.5 %copy-start.8 = (f32[16]{0:T(128)S(1)}, f32[16]{0:T(128)}, u32[]{:S(2)}) copy-start(f32[16]{0:T(128)} %param.31) | copy-start | bytes 196
  9.4 22.7 %copy-start.11 = (s32[1,5]{1,0:T(1,128)S(1)}, s32[1,5]{1,0:T(1,128)}, u32[]{:S(2)}) copy-start(s32[1,5]{1,0:T(1,128)} %param.19) | copy-start | bytes 64
  9.4 22.8 %copy-start.9 = (f32[16]{0:T(128)S(1)}, f32[16]{0:T(128)}, u32[]{:S(2)}) copy-start(f32[16]{0:T(128)} %param.30) | copy-start | bytes 196
  9.4 22.8 %copy-start.10 = (f32[16]{0:T(128)S(1)}, f32[16]{0:T(128)}, u32[]{:S(2)}) copy-start(f32[16]{0:T(128)} %param.29) | copy-start | bytes 196
  9.4 23.5 %copy-start.6 = (f32[1024]{0:T(1024)S(1)}, f32[1024]{0:T(1024)}, u32[]{:S(2)}) copy-start(f32[1024]{0:T(1024)} %param.33) | copy-start | bytes 12292
  9.4 24.6 %copy-start.4 = (f32[4,1024]{1,0:T(4,128)S(1)}, f32[4,1024]{1,0:T(4,128)}, u32[]{:S(2)}) copy-start(f32[4,1024]{1,0:T(4,128)} %param.25) | copy-start | bytes 49156
  9.5 24.6 %copy-start.7 = (f32[1024]{0:T(1024)S(1)}, f32[1024]{0:T(1024)}, u32[]{:S(2)}) copy-start(f32[1024]{0:T(1024)} %param.26) | copy-start | bytes 12292
  9.5 86.3 %all-gather.4.cloned.1.call-start = ((), (), s32[]{:S(2)}) async-start(), calls=%async_computation.1 | async-start | bytes 6488064 | tf_op jit(solution)/shard_map/all_gather | solution.py:1043
  30.8 105.4 %all-gather.8.cloned.1.call-start = ((), (), s32[]{:S(2)}) async-start(), calls=%async_computation.3 | async-start | bytes 4718592 | tf_op jit(solution)/shard_map/all_gather | solution.py:1045
  31.8 350.6 %reduce-scatter.4.cloned.1.call-start = ((), (), s32[]{:S(2)}) async-start(), calls=%async_computation.4 | async-start | bytes 163840
  357.1 26.8 %copy-start.2 = (bf16[1024,512]{1,0:T(8,128)(2,1)S(1)}, bf16[1024,512]{1,0:T(8,128)(2,1)}, u32[]{:S(2)}) copy-start(bf16[1024,512]{1,0:T(8,128)(2,1)} %get-tuple-element.125) | copy-start | bytes 3145732
  357.2 30.0 %copy-start.3 = (f32[256,1024]{1,0:T(8,128)S(1)}, f32[256,1024]{1,0:T(8,128)}, u32[]{:S(2)}) copy-start(f32[256,1024]{1,0:T(8,128)} %get-tuple-element.127) | copy-start | bytes 3145732
  362.6 25.6 %copy-start.1 = (f32[1024,256]{1,0:T(8,128)S(1)}, f32[1024,256]{1,0:T(8,128)}, u32[]{:S(2)}) copy-start(f32[1024,256]{1,0:T(8,128)} %get-tuple-element.131) | copy-start | bytes 3145732
Sparse Core Ops, SparseCore 0:
  10.5 39.4 all-gather.5
  52.4 43.3 all-gather.3
  97.6 37.4 all-gather.7
  362.1 20.1 reduce-scatter.3

commit v3 on v2

--- a/solution.py
+++ b/solution.py
@@ -194,7 +194,9 @@
     return cum, step_e, kept_e, in_e, out_e, column, row
 
 
-def scan_forward(starts, x_low, bc_low, step_low, decay_low, ssd, states, spread, state, xs, yin, cbm):
+def scan_forward(
+    starts, x_low, bc_low, step_low, decay_low, ssd, states, spread, state, xs, yin, cbm, tick=None
+):
     length, inner = x_low.shape
     state[...] = jnp.zeros_like(state)
 
@@ -224,6 +226,8 @@
                 part.append(mm((jnp.exp(span) * cbm[...]).astype(bf16), pair))
             y = jnp.where(first, part[0], part[1]) + yin[:, cols]
             ssd[rows, cols] = y.astype(bf16)
+        if tick is not None:
+            tick(b)
         return carry
 
     lax.fori_loop(0, length // BLOCK, body, 0)
@@ -682,8 +686,275 @@
         return copy
 
 
+class Gather:
+    def __init__(self, ring, shard, rows, sems):
+        self.ring, self.shard, self.half = ring, shard, rows // 2
+        self.ring_send, self.ring_recv, self.core_send, self.core_recv = sems
+        self.other = 1 - 2 * ring.core
+
+    def ring_copy(self, k, source):
+        ring = self.ring
+        piece = self.shard(source)
+        if k >= 2:
+            piece = piece.at[pl.ds((k - 2) * self.half, self.half), :]
+        return remote(
+            piece, piece, self.ring_send.at[k], self.ring_recv.at[k], dp=(ring.right, ring.left)[k % 2]
+        )
+
+    def core_copy(self, k, source):
+        return remote(
+            self.shard(source), self.shard(source), self.core_send.at[k], self.core_recv.at[k], dp=self.ring.partner
+        )
+
+    def start(self):
+        me = self.ring.me
+        self.ring_copy(0, me).start()
+        self.ring_copy(1, me).start()
+        self.core_copy(0, me).start()
+
+    def second(self):
+        left, right = self.ring.left, self.ring.right
+        self.ring_copy(0, left).wait_recv()
+        self.ring_copy(2, left).start()
+        self.core_copy(1, left).start()
+        self.ring_copy(1, right).wait_recv()
+        self.ring_copy(3, right).start()
+        self.core_copy(2, right).start()
+
+    def third(self):
+        across = self.ring.across
+        self.ring_copy(2, across).wait_recv()
+        self.ring_copy(3, across).wait_recv()
+        self.core_copy(3, across).start()
+
+    def arrived(self, k):
+        ring = self.ring
+        source = (ring.me, ring.left, ring.right, ring.across)[k] + self.other
+        self.core_copy(k, source).wait_recv()
+
+    def drain(self):
+        ring = self.ring
+        for k, source in enumerate((ring.me, ring.me, ring.left, ring.right)):
+            self.ring_copy(k, source).wait_send()
+        for k, source in enumerate((ring.me, ring.left, ring.right, ring.across)):
+            self.core_copy(k, source).wait_send()
+
+
+def cast_into(target, source, rows=64):
+    def body(i, carry):
+        at = pl.ds(pl.multiple_of(i * rows, rows), rows)
+        target[at, :] = source[at, :].astype(target.dtype)
+        return carry
+
+    lax.fori_loop(0, target.shape[0] // rows, body, 0)
+
+
+def gather_kernel(
+    lengths, tok, cot, w_x, w_z, w_out, w_bc, w_dt, conv_x, conv_x_bias, conv_bc, conv_bc_bias, dt_bias, a_rate,
+    d_skip, gain, out_gain,
+    normed_o, xin_o, slope_o, x_low_o, ssd_o, states_o, wxd_o, wz_o, wout_o, gn_o, low_gate_o, gs_o,
+    bc_low, step, sgdt, step_low, decay_low, inverse, sums, taps, crow, dpar,
+    v_tc, stage_a, stage_b, normed, xin, slope, x_low, ssd, states, wxd, wz, wout, gate, gnorm,
+    bc_slots, tap_slots, row_slots, wide, stat, turned,
+    pos, spread, dtin, state, xs, yin, cbm,
+    load_sems, store_sems, ring_send, ring_recv, core_send, core_recv, mp_send, mp_recv,
+):
+    ring = Ring()
+    n, z = lax.axis_size("mp"), lax.axis_index("mp")
+    length, features = normed.shape
+    inner, width = gate.shape[1], xin.shape[1]
+    shard, column_shard = stage_a.shape[0], stage_b.shape[1]
+    heads, per = w_dt.shape[1], w_bc.shape[1]
+    loads, stores = Loads(load_sems), Loads(store_sems)
+    load_x = loads.start(w_x, stage_a)
+    load_tok = loads.start(tok, v_tc)
+    load_out = loads.start(w_out, stage_b)
+    starts = [jnp.int32(0)]
+    for k in range(DOCS - 1):
+        starts.append(starts[-1] + lengths[0, k])
+
+    wide[...] = jnp.zeros_like(wide)
+    wide[:, :per] = w_bc[...]
+    bc_slots[0] = wide[...].astype(bf16)
+    tap_slots[0] = jnp.zeros_like(tap_slots[0])
+    tap_slots[0, :CONV, :per] = conv_bc[...]
+    tap_slots[0, CONV : CONV + 1, :per] = conv_bc_bias[...]
+    wide[...] = jnp.zeros_like(wide)
+    wide[:, :heads] = w_dt[...]
+    own_rows = pl.ds(pl.multiple_of(ring.me * shard, shard), shard)
+    wxd[own_rows, width:] = wide[...].astype(bf16)
+    dpar[...] = jnp.zeros_like(dpar)
+    dpar[0:1, :heads] = dt_bias[...]
+    dpar[1:2, :heads] = a_rate[...]
+    dpar[2:3, :heads] = d_skip[...]
+
+    greet(ring, False)
+
+    def exchange(k, i):
+        slots = (bc_slots, tap_slots, row_slots)[k]
+        at = k * (n - 1) + i - 1
+        return remote(slots.at[0], slots.at[i], mp_send.at[at], mp_recv.at[at], mp=(z + i) % n)
+
+    def rows_of(ref, low, high):
+        def shard_of(r):
+            return ref.at[pl.ds(pl.multiple_of(r * shard, shard), shard), pl.ds(low, high - low)]
+
+        return shard_of
+
+    def columns_of(r):
+        return wout.at[:, pl.ds(pl.multiple_of(r * column_shard, column_shard), column_shard)]
+
+    sems = [tuple(group.at[k] for group in (ring_send, ring_recv, core_send, core_recv)) for k in range(4)]
+    get_x = Gather(ring, rows_of(wxd, 0, inner), shard, sems[0])
+    get_bd = Gather(ring, rows_of(wxd, inner, wxd.shape[1]), shard, sems[1])
+    get_z = Gather(ring, rows_of(wz, 0, inner), shard, sems[2])
+    get_out = Gather(ring, columns_of, inner, sems[3])
+
+    load_x.wait()
+    cast_into(get_x.shard(ring.me), stage_a)
+    get_x.start()
+    for k in range(2):
+        for i in range(1, n):
+            exchange(k, i).start()
+    load_z = loads.start(w_z, stage_a)
+    fill_spread(spread)
+    fill_positions(starts, pos, None)
+    crow[0:1, :] = out_gain[...]
+    crow[1:2, :] = expand(dpar[...], spread[...])[2:3]
+    load_tok.wait()
+    normalize(tok=v_tc, gain=gain, normed=normed, stat=inverse)
+    load_cot = loads.start(cot, v_tc)
+    store_normed = stores.start(normed, normed_o)
+    for k in range(2):
+        for i in range(1, n):
+            exchange(k, i).wait()
+    first = lax.broadcasted_iota(jnp.int32, (shard, LANES), 1) < per
+    for j in range((width - inner) // LANES):
+        low, high = (z - 2 * j + n) % n, (z - 2 * j - 1 + n) % n
+        columns = slice(inner + j * LANES, inner + (j + 1) * LANES)
+        pair = jnp.where(first, bc_slots[low].astype(f32), pltpu.roll(bc_slots[high].astype(f32), per, 1))
+        wxd[own_rows, columns] = pair.astype(bf16)
+        taps[:, columns] = jnp.where(first[:8], tap_slots[low], pltpu.roll(tap_slots[high], per, 1))
+    get_bd.start()
+    taps[:, :inner] = jnp.zeros((8, inner), f32)
+    taps[:CONV, :inner] = conv_x[...]
+    taps[CONV : CONV + 1, :inner] = conv_x_bias[...]
+    load_z.wait()
+    cast_into(get_z.shard(ring.me), stage_a)
+    load_out.wait()
+    cast_into(get_out.shard(ring.me), stage_b)
+    xin[pl.ds(0, 8), :] = jnp.zeros((8, width), f32)
+
+    def project_chip(k, source):
+        get_x.arrived(k)
+        get_bd.arrived(k)
+        part = pl.ds(pl.multiple_of((source // 2) * 2 * shard, 2 * shard), 2 * shard)
+
+        def body(i, carry):
+            at = pl.multiple_of(i * 512, 512)
+            left = normed[pl.ds(at, 512), part]
+            for c, w in tiles(wxd.shape[1], 512):
+                here = mm(left, wxd[part, c : c + w])
+                w_x_part = min(w, width - c)
+                if k == 0:
+                    xin[pl.ds(at + 8, 512), c : c + w_x_part] = here[:, :w_x_part]
+                else:
+                    xin[pl.ds(at + 8, 512), c : c + w_x_part] += here[:, :w_x_part]
+                if w_x_part < w:
+                    if k == 0:
+                        dtin[pl.ds(at, 512), :] = here[:, w_x_part:]
+                    else:
+                        dtin[pl.ds(at, 512), :] += here[:, w_x_part:]
+            return carry
+
+        lax.fori_loop(0, length // 512, body, 0)
+
+    project_chip(0, ring.me)
+    get_x.second()
+    get_bd.second()
+    get_z.start()
+    project_chip(1, ring.left)
+    project_chip(2, ring.right)
+    get_x.third()
+    get_bd.third()
+    project_chip(3, ring.across)
+    for source, target in ((xin, xin_o), (wxd, wxd_o)):
+        stores.start(source, target)
+    steps(dtin, dpar, step, sgdt, step_low, decay_low)
+    convolve(xin, taps, pos, slope, x_low, bc_low)
+    get_z.second()
+    get_out.start()
+    for source, target in ((slope, slope_o), (x_low, x_low_o)):
+        stores.start(source, target)
+
+    def scan_tick(b):
+        @pl.when(b == 1)
+        def _():
+            get_z.third()
+
+    scan_forward(
+        starts, x_low, bc_low, step_low, decay_low, ssd, states, spread, state, xs, yin, cbm, scan_tick
+    )
+    for source, target in ((ssd, ssd_o), (states, states_o)):
+        stores.start(source, target)
+    get_out.second()
+    for k in range(4):
+        get_z.arrived(k)
+    project_rows(normed, wz, gate)
+    stores.start(wz, wz_o)
+    load_cot.wait()
+
+    def back_chip(k, source):
+        get_out.arrived(k)
+        part = pl.ds(pl.multiple_of((source // 2) * 2 * column_shard, 2 * column_shard), 2 * column_shard)
+
+        def body(i, carry):
+            at = pl.ds(pl.multiple_of(i * 512, 512), 512)
+            left = v_tc[at, part]
+            for c, w in tiles(inner, 512):
+                here = mm_nt(left, wout[c : c + w, part])
+                if k == 0:
+                    gnorm[at, c : c + w] = here
+                else:
+                    gnorm[at, c : c + w] += here
+            return carry
+
+        lax.fori_loop(0, length // 512, body, 0)
+
+    back_chip(0, ring.me)
+    back_chip(1, ring.left)
+    back_chip(2, ring.right)
+    get_out.third()
+    back_chip(3, ring.across)
+    stores.start(wout, wout_o)
+    gate_sums(gate, ssd, x_low, gnorm, crow, stat)
+    for b in range(length // BLOCK):
+        columns = slice(b * BLOCK, (b + 1) * BLOCK)
+        row_slots[0, :, columns] = stat[columns, :].T[:8]
+    for i in range(1, n):
+        exchange(2, i).start()
+    store_normed.wait()
+    turned[...] = jnp.zeros_like(turned)
+    for i in range(1, n):
+        exchange(2, i).wait()
+    for b in range(length // BLOCK):
+        columns = slice(b * BLOCK, (b + 1) * BLOCK)
+        turned[0:8, :] = functools.reduce(lambda p, q: p + q, [row_slots[i, :, columns] for i in range(n)])
+        stat[columns, :] = turned[...].T
+    gn = v_tc.at[:, pl.ds(0, inner)]
+    low_gate = v_tc.at[:, pl.ds(inner, inner)]
+    gs = normed.at[:, pl.ds(0, inner)]
+    gate_backward(gate, ssd, x_low, gnorm, crow, stat, inner * n, gn, low_gate, gs, sums)
+    for source, target in ((gn, gn_o), (low_gate, low_gate_o), (gs, gs_o)):
+        stores.start(source, target)
+    for each in (get_x, get_bd, get_z, get_out):
+        each.drain()
+    for copy in stores.pairs[1:]:
+        copy.wait()
+
+
 def output_kernel(
-    starts, tok, gn, wout, cot, x_low, ssd, states, gs, slope, xin, bc_low, step, sgdt, step_low, decay_low,
+    lengths, tok, gn, wout, cot, x_low, ssd, states, gs, slope, xin, bc_low, step, sgdt, step_low, decay_low,
     taps, crow, dpar,
     out, dwout, low_xd, csums, dsums,
     v_gn, v_wout, v_cot, v_x, v_ssd, v_states, v_gs, v_slope, v_xin,
@@ -692,6 +963,9 @@
     load_sems, cot_sems, line_send, line_recv, core_send, core_recv, ring_send, ring_recv,
 ):
     ring = Ring()
+    starts = [jnp.int32(0)]
+    for k in range(DOCS - 1):
+        starts.append(starts[-1] + lengths[0, k])
     loads = Loads(load_sems)
     n = lax.axis_size("mp")
     z = lax.axis_index("mp")
@@ -804,13 +1078,14 @@
 
 def input_kernel(
     tok, inverse, gain, normed, low_gate, low_xd, wz, wxd, cot, csums, sums, dsums,
-    grad, dwz, dwxd, smalls,
+    grad, dwz, dwx, dwbc, dwdt, conv_x, conv_x_bias, conv_bc, conv_bc_bias, dt_bias, a_rate, d_skip, in_gain, out_gain,
+    dwxd, smalls, spread, bc_own, bc_slots,
     v_tok, v_normed, v_gate, v_xd, v_wz, v_wxd, v_cot,
     part, slots, total, z_grads, z_cores, z_parts, z_wholes, x_grads, x_cores, x_parts, x_wholes,
     rowacc, rows_own, rows_in, colacc, dp_in, bc_in, gain_in,
     load_sems, line_send, line_recv, z_core_send, z_core_recv, z_ring_send, z_ring_recv,
     x_core_send, x_core_recv, x_ring_send, x_ring_recv,
-    rows_send, rows_recv, dp_send, dp_recv, mp_send, mp_recv,
+    rows_send, rows_recv, dp_send, dp_recv, mp_send, mp_recv, bc_send, bc_recv,
 ):
     ring = Ring()
     loads = Loads(load_sems)
@@ -820,6 +1095,7 @@
     length, features = part.shape
     inner = v_gate.shape[1]
     width = smalls.shape[1]
+    heads, per = dwdt.shape[1], dwbc.shape[1]
     first = [
         loads.start(source, target)
         for source, target in ((low_gate, v_gate), (wz, v_wz), (low_xd, v_xd), (wxd, v_wxd), (tok, v_tok))
@@ -980,6 +1256,43 @@
     smalls[0:8, inner:] += functools.reduce(lambda a, b: a + b, [bc_in[i] for i in range(n - 1)])
     smalls[8:16, :inner] += functools.reduce(lambda a, b: a + b, [gain_in[i] for i in range(n - 1)])
     x_scatter.finish(dwxd)
+    share = LANES // per
+
+    def mine(v):
+        turns = [v] + [pltpu.roll(v, LANES - k * per, 1) for k in range(1, share)]
+        which = jnp.full(v.shape, z % share, jnp.int32)
+        return functools.reduce(lambda a, k: jnp.where(which == k, turns[k], a), range(1, share), turns[0])
+
+    for j in range((width - inner) // LANES):
+        bc_own[j] = dwxd[:, inner + j * LANES : inner + (j + 1) * LANES].astype(bf16)
+
+    def weight_copy(i):
+        other = (z + i) % n
+        return remote(
+            bc_own.at[other // share], bc_slots.at[i - 1], bc_send.at[i - 1], bc_recv.at[i - 1], mp=other
+        )
+
+    for i in range(1, n):
+        weight_copy(i).start()
+    cast_into(dwx, dwxd.at[:, pl.ds(0, inner)])
+    dwdt[...] = dwxd[:, width : width + heads]
+    lanes = pl.ds(pl.multiple_of(inner + (z // share) * LANES, LANES), LANES)
+    conv_x[...] = smalls[:CONV, :inner]
+    conv_x_bias[...] = smalls[CONV : CONV + 1, :inner]
+    taps = mine(smalls[:8, lanes])
+    conv_bc[...] = taps[:CONV, :per]
+    conv_bc_bias[...] = taps[CONV : CONV + 1, :per]
+    out_gain[...] = smalls[5:6, :inner]
+    fill_spread(spread)
+    d_skip[...] = gather_heads(smalls[0:8, :inner], spread[...])[6:7, :heads]
+    dt_bias[...] = smalls[7:8, :heads]
+    a_rate[...] = smalls[7:8, LANES : LANES + heads]
+    fits = inner // own
+    in_gain[...] = smalls[pl.ds(8 + z // fits, 1), pl.ds(pl.multiple_of((z % fits) * own, own), own)]
+    for i in range(1, n):
+        weight_copy(i).wait()
+    here = functools.reduce(lambda a, b: a + b, [bc_slots[i].astype(f32) for i in range(n - 1)], dwxd[:, lanes])
+    dwbc[...] = mine(here)[:, :per]
     later[1].wait()
 
     def last(t, carry):
@@ -997,11 +1310,7 @@
     line.drain()
 
 
-def gate_back_kernel(gate, ssd, x_low, gnorm, crow, stat, gn, low_gate, gs, sums, *, width):
-    gate_backward(gate, ssd, x_low, gnorm, crow, stat, width, gn, low_gate, gs, sums)
-
-
-def call(kernel, outs, scratch, smem, *operands, places=None, sems=(), collective=None):
+def call(kernel, outs, scratch, smem, *operands, places=None, sems=(), collective=None, far=0):
     spaces = {"s": pltpu.SMEM, "v": pltpu.VMEM, "a": pl.ANY}
     if places is None:
         places = "s" * smem + "v" * (len(operands) - smem)
@@ -1010,14 +1319,14 @@
         kernel,
         out_shape=[jax.ShapeDtypeStruct(shape, kind) for shape, kind in outs],
         in_specs=[pl.BlockSpec(memory_space=spaces[c]) for c in places],
-        out_specs=[pl.BlockSpec(memory_space=pltpu.VMEM)] * len(outs),
+        out_specs=[pl.BlockSpec(memory_space=pl.ANY if i < far else pltpu.VMEM) for i in range(len(outs))],
         scratch_shapes=[pltpu.VMEM(shape, kind) for shape, kind in scratch]
         + [pltpu.SemaphoreType.DMA(shape) for shape in sems],
         compiler_params=pltpu.CompilerParams(vmem_limit_bytes=VMEM_LIMIT, **extra),
     )(*operands)
 
 
-def per_device(
+def per_device_any(
     tokens, cotangent, doc_lengths, w_z, w_x, w_bc, w_dt, w_out, conv_x, conv_x_bias, conv_bc,
     conv_bc_bias, dt_bias, a_rate, d_skip, input_norm_gain, out_gain,
 ):
@@ -1072,69 +1381,6 @@
         0, cotangent, wout, gate, ssd, x_low, crow,
     )
     stat = jnp.pad(lax.psum(stat[:, :8], "mp"), ((0, 0), (0, LANES - 8)))
-    if lax.axis_size("dp") == 8 and group == 4:
-        gn, low_gate, gs, sums = call(
-            functools.partial(gate_back_kernel, width=inner * group),
-            [((T, inner), bf16), ((T, inner), bf16), ((T, inner), bf16), ((16, inner), f32)],
-            [],
-            0, gate, ssd, x_low, gnorm, crow, stat,
-        )
-        columns = D // lax.axis_size("dp")
-        messages = blocks * (group - 1)
-        output, w_out_grad, low_xd, csums, dsums = call(
-            output_kernel,
-            [
-                ((T, own), bf16), ((inner, columns), f32), ((T, wide), bf16), ((8 * CONV + 8, width), f32),
-                ((16, LANES), f32),
-            ],
-            [
-                ((T, inner), bf16), ((inner, D), bf16), ((2, T, 2 * columns), bf16), ((T, inner), bf16),
-                ((T, inner), bf16), ((blocks, STATE, inner), bf16), ((T, inner), bf16), ((T, width), bf16),
-                ((T + 8, width), f32),
-                ((T, D), bf16), ((2, messages, BLOCK, own), bf16),
-                ((4, inner, columns), bf16), ((2, inner // 2, columns), bf16), ((2, inner, columns), bf16),
-                ((T, LANES), jnp.int32), ((T, LANES), jnp.int32), ((LANES, inner), bf16), ((T + 8, width), f32),
-                ((STATE, inner), f32), ((BLOCK, inner), bf16), ((BLOCK, inner), f32), ((BLOCK, BLOCK), f32),
-                ((BLOCK, BLOCK), f32),
-            ],
-            0, starts, tokens, gn, wout, cotangent, x_low, ssd, states, gs, slope, xin, bc_low, step, sgdt,
-            step_low, decay_low, taps, crow, dpar,
-            places="s" + "a" * 10 + "v" * 8,
-            sems=[(9,), (2,), (2, messages), (2, messages), (4,), (4,), (4,), (4,)],
-            collective=1,
-        )
-        size = lax.axis_size("dp")
-        input_grad, w_z_grad, dwxd_own, smalls = call(
-            input_kernel,
-            [((T, own), bf16), ((shard, inner), f32), ((shard, wide), f32), ((16, width), f32)],
-            [
-                ((T, D), bf16), ((T, D), bf16), ((T, inner), bf16), ((T, wide), bf16), ((D, inner), bf16),
-                ((D, wide), bf16), ((T, own), bf16),
-                ((T, D), bf16), ((2, messages, BLOCK, own), bf16), ((BLOCK, own), f32),
-                ((D, inner), bf16), ((4, shard, inner), bf16), ((2, shard // 2, inner), bf16), ((2, shard, inner), bf16),
-                ((D, wide), bf16), ((4, shard, wide), bf16), ((2, shard // 2, wide), bf16), ((2, shard, wide), bf16),
-                ((T, LANES), f32), ((8, T), f32), ((group - 1, 8, T), f32), ((8, D), f32),
-                ((size - 1, 16, width), f32), ((group - 1, 8, pair), f32), ((group - 1, 8, inner), f32),
-            ],
-            0, tokens, inverse, gain, normed, low_gate, low_xd, wz, wxd, cotangent, csums, sums, dsums,
-            places="avvaaaaaavvv",
-            sems=[
-                (7,), (2, messages), (2, messages), (4,), (4,), (4,), (4,), (4,), (4,), (4,), (4,),
-                (group - 1,), (group - 1,), (size - 1,), (size - 1,), (2 * group - 2,), (2 * group - 2,),
-            ],
-            collective=2,
-        )
-        bc = lax.dynamic_slice_in_dim(smalls[: CONV + 1, inner:], rank * (pair // group), pair // group, 1)
-        in_gain = lax.dynamic_slice_in_dim(smalls[8 : 8 + D // inner, :inner].reshape(D), rank * own, own, 0)
-        w_bc_grad = lax.psum_scatter(
-            dwxd_own[:, inner:width].astype(bf16), "mp", scatter_dimension=1, tiled=True
-        ).astype(f32)
-        return (
-            output, input_grad, w_z_grad, dwxd_own[:, :inner], w_bc_grad, dwxd_own[:, width : width + heads],
-            w_out_grad, smalls[:CONV, :inner], smalls[CONV, :inner], bc[:CONV], bc[CONV],
-            smalls[7, :heads], smalls[7, LANES : LANES + heads],
-            jnp.sum(smalls[6, :inner].reshape(heads, HEADDIM), axis=1), in_gain, smalls[5, :inner],
-        )
     branch, dwout, dwz, low_gate, gs, sums = call(
         functools.partial(middle_kernel, width=inner * group),
         [
@@ -1198,10 +1444,116 @@
     )
 
 
+def per_device(
+    tokens, cotangent, doc_lengths, w_z, w_x, w_bc, w_dt, w_out, conv_x, conv_x_bias, conv_bc,
+    conv_bc_bias, dt_bias, a_rate, d_skip, input_norm_gain, out_gain,
+):
+    group, size = lax.axis_size("mp"), lax.axis_size("dp")
+    T, D = tokens.shape
+    shard, inner = w_x.shape
+    heads, per = w_dt.shape[1], w_bc.shape[1]
+    pair = per * group
+    width = inner + pair
+    wide = width + LANES
+    own = D // group
+    columns = w_out.shape[1]
+    blocks = T // BLOCK
+    messages = blocks * (group - 1)
+
+    def row(v):
+        return v[None, :]
+
+    (
+        normed, xin, slope, x_low, ssd, states, wxd, wz, wout, gn, low_gate, gs,
+        bc_low, step, sgdt, step_low, decay_low, inverse, sums, taps, crow, dpar,
+    ) = call(
+        gather_kernel,
+        [
+            ((T, D), bf16), ((T + 8, width), f32), ((T, width), bf16), ((T, inner), bf16), ((T, inner), bf16),
+            ((blocks, STATE, inner), bf16), ((D, wide), bf16), ((D, inner), bf16), ((inner, D), bf16),
+            ((T, inner), bf16), ((T, inner), bf16), ((T, inner), bf16),
+            ((T, pair), bf16), ((T, LANES), f32), ((T, LANES), f32), ((T, LANES), bf16), ((T, LANES), bf16),
+            ((T, LANES), f32), ((16, inner), f32), ((8, width), f32), ((8, inner), f32), ((8, LANES), f32),
+        ],
+        [
+            ((T, D), bf16), ((shard, inner), f32), ((inner, columns), f32), ((T, D), bf16), ((T + 8, width), f32),
+            ((T, width), bf16), ((T, inner), bf16), ((T, inner), bf16), ((blocks, STATE, inner), bf16),
+            ((D, wide), bf16), ((D, inner), bf16), ((inner, D), bf16), ((T, inner), f32), ((T, inner), f32),
+            ((group, shard, LANES), bf16), ((group, 8, LANES), f32), ((group, 8, T), f32), ((shard, LANES), f32),
+            ((T, LANES), f32), ((LANES, BLOCK), f32),
+            ((T, LANES), jnp.int32), ((LANES, inner), bf16), ((T, LANES), f32), ((STATE, inner), f32),
+            ((BLOCK, inner), bf16), ((BLOCK, inner), f32), ((BLOCK, BLOCK), f32),
+        ],
+        0, doc_lengths, tokens, cotangent, w_x, w_z, w_out, w_bc, w_dt, conv_x, row(conv_x_bias), conv_bc,
+        row(conv_bc_bias), row(dt_bias), row(a_rate), row(d_skip), row(input_norm_gain), row(out_gain),
+        places="s" + "a" * 5 + "v" * 11,
+        sems=[(5,), (12,), (4, 4), (4, 4), (4, 4), (4, 4), (3 * group - 3,), (3 * group - 3,)],
+        collective=0,
+        far=12,
+    )
+    output, w_out_grad, low_xd, csums, dsums = call(
+        output_kernel,
+        [
+            ((T, own), bf16), ((inner, columns), f32), ((T, wide), bf16), ((8 * CONV + 8, width), f32),
+            ((16, LANES), f32),
+        ],
+        [
+            ((T, inner), bf16), ((inner, D), bf16), ((2, T, 2 * columns), bf16), ((T, inner), bf16),
+            ((T, inner), bf16), ((blocks, STATE, inner), bf16), ((T, inner), bf16), ((T, width), bf16),
+            ((T + 8, width), f32),
+            ((T, D), bf16), ((2, messages, BLOCK, own), bf16),
+            ((4, inner, columns), bf16), ((2, inner // 2, columns), bf16), ((2, inner, columns), bf16),
+            ((T, LANES), jnp.int32), ((T, LANES), jnp.int32), ((LANES, inner), bf16), ((T + 8, width), f32),
+            ((STATE, inner), f32), ((BLOCK, inner), bf16), ((BLOCK, inner), f32), ((BLOCK, BLOCK), f32),
+            ((BLOCK, BLOCK), f32),
+        ],
+        0, doc_lengths, tokens, gn, wout, cotangent, x_low, ssd, states, gs, slope, xin, bc_low, step, sgdt,
+        step_low, decay_low, taps, crow, dpar,
+        places="s" + "a" * 10 + "v" * 8,
+        sems=[(9,), (2,), (2, messages), (2, messages), (4,), (4,), (4,), (4,)],
+        collective=1,
+    )
+    (
+        input_grad, w_z_grad, w_x_grad, w_bc_grad, w_dt_grad, conv_x_grad, conv_x_bias_grad, conv_bc_grad,
+        conv_bc_bias_grad, dt_bias_grad, a_rate_grad, d_skip_grad, in_gain_grad, out_gain_grad,
+    ) = call(
+        input_kernel,
+        [
+            ((T, own), bf16), ((shard, inner), f32), ((shard, inner), f32), ((shard, per), f32),
+            ((shard, heads), f32), ((CONV, inner), f32), ((1, inner), f32), ((CONV, per), f32), ((1, per), f32),
+            ((1, heads), f32), ((1, heads), f32), ((1, heads), f32), ((1, own), f32), ((1, inner), f32),
+        ],
+        [
+            ((shard, wide), f32), ((16, width), f32), ((LANES, inner), bf16), ((pair // LANES, shard, LANES), bf16),
+            ((group - 1, shard, LANES), bf16),
+            ((T, D), bf16), ((T, D), bf16), ((T, inner), bf16), ((T, wide), bf16), ((D, inner), bf16),
+            ((D, wide), bf16), ((T, own), bf16),
+            ((T, D), bf16), ((2, messages, BLOCK, own), bf16), ((BLOCK, own), f32),
+            ((D, inner), bf16), ((4, shard, inner), bf16), ((2, shard // 2, inner), bf16), ((2, shard, inner), bf16),
+            ((D, wide), bf16), ((4, shard, wide), bf16), ((2, shard // 2, wide), bf16), ((2, shard, wide), bf16),
+            ((T, LANES), f32), ((8, T), f32), ((group - 1, 8, T), f32), ((8, D), f32),
+            ((size - 1, 16, width), f32), ((group - 1, 8, pair), f32), ((group - 1, 8, inner), f32),
+        ],
+        0, tokens, inverse, row(input_norm_gain), normed, low_gate, low_xd, wz, wxd, cotangent, csums, sums, dsums,
+        places="avvaaaaaavvv",
+        sems=[
+            (7,), (2, messages), (2, messages), (4,), (4,), (4,), (4,), (4,), (4,), (4,), (4,),
+            (group - 1,), (group - 1,), (size - 1,), (size - 1,), (2 * group - 2,), (2 * group - 2,),
+            (group - 1,), (group - 1,),
+        ],
+        collective=2,
+    )
+    return (
+        output, input_grad, w_z_grad, w_x_grad, w_bc_grad, w_dt_grad, w_out_grad,
+        conv_x_grad, conv_x_bias_grad[0], conv_bc_grad, conv_bc_bias_grad[0], dt_bias_grad[0], a_rate_grad[0],
+        d_skip_grad[0], in_gain_grad[0], out_gain_grad[0],
+    )
+
+
 def solution(mesh):
     row, block, column = P("dp", None), P("dp", "mp"), P("mp")
     return jax.shard_map(
-        per_device,
+        per_device if (mesh.shape["dp"], mesh.shape["mp"]) == (8, 4) else per_device_any,
         mesh=mesh,
         in_specs=(
             row, row, row, block, block, block, block, P("mp", "dp"), P(None, "mp"), column,

time: 396 us -> 283 us (0.71)
  waiting for transfers between devices: 72.4 us -> 0 us
  blocking collectives: 47.1 us -> 0 us
  Pallas kernels: 230 us -> 264 us
  between operations: 13.9 us -> 0.75 us
  other arithmetic: 8.43 us -> 0 us
  local copies, waits for them, and re-layouts: 24 us -> 17.6 us
    all_gather x3 -> x0, waiting for transfers between devices: 61.1 us -> none  [the longest x1 45.8 us: per_device(): wxd = lax.all_gather(wxd, 'dp', axis=0, tiled=True)]
    pallas_call x5 -> x3, Pallas kernels: 230 us -> 264 us  [call(): pl.pallas_call(kernel, out_shape=[jax.ShapeDtypeStruct(shape, kind) for s...]
    psum x1 -> x0, blocking collectives: 30.9 us -> none  [per_device(): stat = jnp.pad(lax.psum(stat[:, :8], 'mp'), ((0, 0), (0, LANES - 8)))]
    all_gather x1 -> x0, blocking collectives: 16.2 us -> none  [per_device(): packed = lax.all_gather(packed, 'mp', axis=1, tiled=True)]
    unnamed x5 -> x0, waiting for transfers between devices: 11.3 us -> none
    slice x9 -> x0, local copies, waits for them, and re-layouts: 8.42 us -> none  [the longest x1 2.39 us: per_device(): dwxd_own[:, :inner]]
    unnamed x37 -> x44, local copies, waits for them, and re-layouts: 10.1 us -> 17.6 us
    convert_element_type x4 -> x0, other arithmetic: 4.33 us -> none  [the longest x1 2.17 us: per_device(): wz = lax.all_gather(w_z.astype(bf16), 'dp', axis=0, tiled=True)]
  transfers between devices with their start and end apart: 4 -> 0, of which waited for: 3 -> 0; matrix products, arithmetic and copies ran while one was open for 4% -> 0% of each run, Pallas kernels for 10% -> 0%
where the time goes in v3:
time: 283 us; the launch traced here: 282 us
  Pallas kernels  264 us (93%)
  local copies, waits for them, and re-layouts  17.6 us (6%)
    pallas_call x3, Pallas kernels, call(): pl.pallas_call(kernel, out_shape=[jax.ShapeDtypeStruct(shape, kind) for s...  264 us
    unnamed x44, local copies, waits for them, and re-layouts  17.6 us

profile of v3, /device:TPU:0, one launch (start us, length us, event | category | flops | bytes accessed | tf_op | source)
XLA Modules:
  0.0 282.4 jit_solution(4605288662498461637)
XLA Ops:
  0.6 1.6 copy.33.w_bc
  2.2 1.5 copy.34.w_dt
  3.7 91.2 %shard_map.288 = (bf16[1024,2048]{1,0:T(8,128)(2,1)}, f32[1032,1280]{1,0:T(8,128)}, bf16[1024,1280]{1,0:T(8,128)(2,1)}, bf16[1024,1024]{1,0:T(8,128)(2,1)}, bf16...) custom-call(s32[1,5]{1,0:T(1,128)} %lengths.3, ...), custom_call_target="tpu_custom_call" | custom-call | tf_op jit(solution)/shard_map/pallas_call | solution.py:1318
  94.9 77.8 %shard_map.289 = (bf16[1024,512]{1,0:T(8,128)(2,1)}, f32[1024,256]{1,0:T(8,128)}, bf16[1024,1408]{1,0:T(8,128)(2,1)}, f32[40,1280]{1,0:T(8,128)}, f32[16,128]{1,0:T(8,128)}) custom-call(s32[1,5]{1,0:T(1,128)} %lengths.3, bf16[1024,2048]{1,0:T(8,128)(2,1)} %tok.5, bf16[1024,1024]{1,0:T(8,128)(2,1)} %get-tuple-element.57.gn, ...), custom_call_target="tpu_custom_call" | custom-call | tf_op jit(solution)/shard_map/pallas_call | solution.py:1318
  172.8 0.0 copy-start.1
  172.8 95.1 %shard_map.290 = (bf16[1024,512]{1,0:T(8,128)(2,1)}, f32[256,1024]{1,0:T(8,128)}, f32[256,1024]{1,0:T(8,128)}, f32[256,64]{1,0:T(8,128)}, f32[256,16]{1,0:T(8,12...) custom-call(bf16[1024,2048]{1,0:T(8,128)(2,1)} %tok.5, ...), custom_call_target="tpu_custom_call" | custom-call | tf_op jit(solution)/shard_map/pallas_call | solution.py:1318
  267.8 0.0 copy-start.2
  267.9 1.7 copy.36
  269.5 1.6 copy.35
  271.1 0.0 copy-done.1
  271.1 0.0 copy-start.3
  271.1 0.0 copy-start
  271.1 1.0 copy.51
  272.1 0.0 copy-start.4
  272.1 0.0 copy-start.6
  272.1 0.0 copy-start.8
  272.1 0.0 copy-start.12
  272.1 0.0 copy-start.11
  272.1 0.0 copy-start.10
  272.1 0.0 copy-start.9
  272.2 0.0 copy-start.7
  272.2 0.0 copy-start.5
  272.2 2.3 copy.52
  274.5 0.0 copy-done.3
  274.5 1.0 copy.53
  275.4 0.0 copy-done.2
  275.4 1.0 copy.54
  276.4 0.0 copy-done
  276.4 1.0 copy.55
  277.4 0.0 copy-done.4
  277.4 0.6 copy.56
  278.0 0.0 copy-done.6
  278.0 0.6 copy.57
  278.6 0.0 copy-done.8
  278.6 0.6 copy.58
  279.2 0.0 copy-done.12
  279.2 0.5 copy.59
  279.7 0.0 copy-done.11
  279.7 0.5 copy.60
  280.2 0.0 copy-done.10
  280.2 0.5 copy.61
  280.7 0.0 copy-done.9
  280.7 0.5 copy.62
  281.2 0.0 copy-done.7
  281.2 0.6 copy.63
  281.8 0.0 copy-done.5
  281.8 0.6 copy.64
Async XLA Ops:
  172.8 98.4 %copy-start.1 = (bf16[1024,512]{1,0:T(8,128)(2,1)S(1)}, bf16[1024,512]{1,0:T(8,128)(2,1)}, u32[]{:S(2)}) copy-start(bf16[1024,512]{1,0:T(8,128)(2,1)} %get-tuple-element.130) | copy-start | bytes 3145732
  267.8 7.6 %copy-start.2 = (f32[256,1024]{1,0:T(8,128)S(1)}, f32[256,1024]{1,0:T(8,128)}, u32[]{:S(2)}) copy-start(f32[256,1024]{1,0:T(8,128)} %get-tuple-element.133) | copy-start | bytes 3145732
  271.1 3.3 %copy-start.3 = (f32[256,1024]{1,0:T(8,128)S(1)}, f32[256,1024]{1,0:T(8,128)}, u32[]{:S(2)}) copy-start(f32[256,1024]{1,0:T(8,128)} %get-tuple-element.132) | copy-start | bytes 3145732
  271.1 5.3 %copy-start = (f32[1024,256]{1,0:T(8,128)S(1)}, f32[1024,256]{1,0:T(8,128)}, u32[]{:S(2)}) copy-start(f32[1024,256]{1,0:T(8,128)} %get-tuple-element.136) | copy-start | bytes 3145732
  272.1 5.3 %copy-start.4 = (f32[4,1024]{1,0:T(4,128)S(1)}, f32[4,1024]{1,0:T(4,128)}, u32[]{:S(2)}) copy-start(f32[4,1024]{1,0:T(4,128)} %get-tuple-element.137) | copy-start | bytes 49156
  272.1 5.9 %copy-start.6 = (f32[1,1024]{1,0:T(1,128)S(1)}, f32[1,1024]{1,0:T(1,128)}, u32[]{:S(2)}) copy-start(f32[1,1024]{1,0:T(1,128)} %get-tuple-element.90) | copy-start | bytes 12292
  272.1 6.5 %copy-start.8 = (f32[4,64]{1,0:T(4,128)S(1)}, f32[4,64]{1,0:T(4,128)}, u32[]{:S(2)}) copy-start(f32[4,64]{1,0:T(4,128)} %get-tuple-element.139) | copy-start | bytes 3076
  272.1 7.0 %copy-start.12 = (f32[1,64]{1,0:T(1,128)S(1)}, f32[1,64]{1,0:T(1,128)}, u32[]{:S(2)}) copy-start(f32[1,64]{1,0:T(1,128)} %get-tuple-element.92) | copy-start | bytes 772
  272.1 7.6 %copy-start.11 = (f32[1,16]{1,0:T(1,128)S(1)}, f32[1,16]{1,0:T(1,128)}, u32[]{:S(2)}) copy-start(f32[1,16]{1,0:T(1,128)} %get-tuple-element.93) | copy-start | bytes 196
  272.1 8.1 %copy-start.10 = (f32[1,16]{1,0:T(1,128)S(1)}, f32[1,16]{1,0:T(1,128)}, u32[]{:S(2)}) copy-start(f32[1,16]{1,0:T(1,128)} %get-tuple-element.94) | copy-start | bytes 196
  272.1 8.6 %copy-start.9 = (f32[1,16]{1,0:T(1,128)S(1)}, f32[1,16]{1,0:T(1,128)}, u32[]{:S(2)}) copy-start(f32[1,16]{1,0:T(1,128)} %get-tuple-element.95) | copy-start | bytes 196
  272.2 9.1 %copy-start.7 = (f32[1,512]{1,0:T(1,128)S(1)}, f32[1,512]{1,0:T(1,128)}, u32[]{:S(2)}) copy-start(f32[1,512]{1,0:T(1,128)} %get-tuple-element.96) | copy-start | bytes 6148
  272.2 9.6 %copy-start.5 = (f32[1,1024]{1,0:T(1,128)S(1)}, f32[1,1024]{1,0:T(1,128)}, u32[]{:S(2)}) copy-start(f32[1,1024]{1,0:T(1,128)} %get-tuple-element.97) | copy-start | bytes 12292

commit v4 on v3

--- a/solution.py
+++ b/solution.py
@@ -289,6 +289,54 @@
     lax.fori_loop(0, gate.shape[0] // step, body, 0)
 
 
+def gate_squares(gate, ssd, x_low, crow, gated, stat):
+    step, inner = 64, gate.shape[1]
+
+    def body(i, carry):
+        rows = pl.ds(pl.multiple_of(i * step, step), step)
+        squares = jnp.zeros((step, 256), f32)
+        for c in range(0, inner, 256):
+            cols = slice(c, c + 256)
+            g = gate[rows, cols]
+            mixed = ssd[rows, cols].astype(f32) + crow[1:2, cols] * x_low[rows, cols].astype(f32)
+            value = mixed * (g * logistic(g))
+            gated[rows, cols] = value
+            squares = squares + value * value
+        stat[rows, :] = jnp.broadcast_to(jnp.sum(squares, axis=1, keepdims=True), (step, LANES))
+        return carry
+
+    lax.fori_loop(0, gate.shape[0] // step, body, 0)
+
+
+def scale_rows(gated, inverse_out, crow, gn):
+    step, inner = 64, gated.shape[1]
+
+    def body(i, carry):
+        rows = pl.ds(pl.multiple_of(i * step, step), step)
+        inverse = inverse_out[rows, :1]
+        for c in range(0, inner, 256):
+            cols = slice(c, c + 256)
+            gn[rows, cols] = (gated[rows, cols] * inverse * crow[0:1, cols]).astype(bf16)
+        return carry
+
+    lax.fori_loop(0, gated.shape[0] // step, body, 0)
+
+
+def cross_sums(gnorm, gn, stat):
+    step, inner = 64, gn.shape[1]
+
+    def body(i, carry):
+        rows = pl.ds(pl.multiple_of(i * step, step), step)
+        total = jnp.zeros((step, 256), f32)
+        for c in range(0, inner, 256):
+            cols = slice(c, c + 256)
+            total = total + gnorm[rows, cols] * gn[rows, cols].astype(f32)
+        stat[rows, :] = jnp.broadcast_to(jnp.sum(total, axis=1, keepdims=True), (step, LANES))
+        return carry
+
+    lax.fori_loop(0, gn.shape[0] // step, body, 0)
+
+
 def forward_kernel(
     starts, tok, gain, wxd, wz, taps, dpar,
     normed, inverse, xin, slope, gate, x_low, bc_low, step, sgdt, step_low, decay_low, ssd, states,
@@ -309,14 +357,17 @@
     gate_sums(gate, ssd, x_low, gnorm, crow, stat)
 
 
-def gate_backward(gate, ssd, x_low, gnorm, crow, stat, width, gn, low_gate, gs, sums):
-    step, inner = 64, gate.shape[1]
+def gate_backward(gate, ssd, x_low, gnorm, crow, stat, width, gn, low_gate, gs, sums, known=None):
+    step, inner = 64, ssd.shape[1]
     sums[...] = jnp.zeros_like(sums)
 
     def body(i, carry):
         rows = pl.ds(pl.multiple_of(i * step, step), step)
-        inverse = lax.rsqrt(stat[rows, 0:1] / width + EPS)
-        mean = inverse * stat[rows, 1:2] / width
+        if known is None:
+            inverse = lax.rsqrt(stat[rows, 0:1] / width + EPS)
+            mean = inverse * stat[rows, 1:2] / width
+        else:
+            inverse, mean = known[rows, :1], stat[rows, :1]
         for c in range(0, inner, 256):
             cols = slice(c, c + 256)
             g = gate[rows, cols]
@@ -325,7 +376,8 @@
             sg = logistic(g)
             act = g * sg
             hat = mixed * act * inverse
-            gn[rows, cols] = (hat * crow[0:1, cols]).astype(bf16)
+            if gn is not None:
+                gn[rows, cols] = (hat * crow[0:1, cols]).astype(bf16)
             gnorm_here = gnorm[rows, cols]
             grad = inverse * (gnorm_here * crow[0:1, cols] - hat * mean)
             grad_mixed = grad * act
@@ -335,7 +387,7 @@
             sums[8:16, cols] += fold(grad_mixed * x)
         return carry
 
-    lax.fori_loop(0, gate.shape[0] // step, body, 0)
+    lax.fori_loop(0, ssd.shape[0] // step, body, 0)
 
 
 def middle_kernel(
@@ -426,14 +478,14 @@
     lax.fori_loop(0, blocks, body, 0)
 
 
-def convolve_back(xin, gpre, taps, pos, rpos, low_xd, csums):
+def convolve_back(xin, gpre, taps, pos, rpos, low_xd, csums, tick=None):
     width = gpre.shape[1]
     columns = width // LANES
     csums[...] = jnp.zeros_like(csums)
 
-    def body(i, carry):
-        at = pl.multiple_of((i // columns) * BLOCK, BLOCK)
-        cols = pl.ds(pl.multiple_of((i % columns) * LANES, LANES), LANES)
+    def body(b, j):
+        at = pl.multiple_of(b * BLOCK, BLOCK)
+        cols = pl.ds(pl.multiple_of(j * LANES, LANES), LANES)
         rows = pl.ds(at, BLOCK)
         x = xin[pl.ds(at, BLOCK + 8), cols]
         g = gpre[pl.ds(at, BLOCK + 8), cols]
@@ -450,9 +502,14 @@
             grad = grad + tap[k : k + 1] * jnp.where(ahead >= lag, later, 0.0)
             csums[pl.ds(8 * k, 8), cols] += fold(here * jnp.where(place >= lag, earlier, 0.0))
         low_xd[rows, cols] = grad.astype(bf16)
-        return carry
-
-    lax.fori_loop(0, (xin.shape[0] - 8) // BLOCK * columns, body, 0)
+
+    def block(b, carry):
+        lax.fori_loop(0, columns, lambda j, c: (body(b, j), c)[1], 0)
+        if tick is not None:
+            tick(b)
+        return carry
+
+    lax.fori_loop(0, (xin.shape[0] - 8) // BLOCK, block, 0)
 
 
 def backward_kernel(
@@ -637,6 +694,10 @@
         for side in range(2):
             @pl.when(self.place[side] == 0)
             def _():
+                @pl.when(jnp.int32(k) >= 2)
+                def _():
+                    self.copy(side, jnp.maximum(k - 2, 0))[0].wait_send()
+
                 self.copy(side, k)[0].start()
 
     def forward(self, k, hop):
@@ -660,7 +721,9 @@
     def drain(self):
         def body(k, carry):
             for side in range(2):
-                @pl.when(self.place[side] + k // self.blocks <= self.n - 2)
+                started = self.place[side] + k // self.blocks <= self.n - 2
+
+                @pl.when(started & ((self.place[side] > 0) | (k >= self.count - 2)))
                 def _():
                     self.copy(side, k)[0].wait_send()
             return carry
@@ -752,10 +815,12 @@
 def gather_kernel(
     lengths, tok, cot, w_x, w_z, w_out, w_bc, w_dt, conv_x, conv_x_bias, conv_bc, conv_bc_bias, dt_bias, a_rate,
     d_skip, gain, out_gain,
-    normed_o, xin_o, slope_o, x_low_o, ssd_o, states_o, wxd_o, wz_o, wout_o, gn_o, low_gate_o, gs_o,
-    bc_low, step, sgdt, step_low, decay_low, inverse, sums, taps, crow, dpar,
-    v_tc, stage_a, stage_b, normed, xin, slope, x_low, ssd, states, wxd, wz, wout, gate, gnorm,
-    bc_slots, tap_slots, row_slots, wide, stat, turned,
+    normed_o, xin_o, slope_o, x_low_o, ssd_o, states_o, wxd_o, wz_o, wout_o, gn_o, gate_o, gnorm_o,
+    bc_low_o, step_o, sgdt_o, step_low_o, decay_low_o, inverse_o, inverse_out_o,
+    taps, crow, dpar, rows,
+    v_tok, stage_a, stage_b, normed, xin, slope, x_low, ssd, states, wxd, wz, wout, gate, gated, gnorm,
+    bc_low, step, sgdt, step_low, decay_low, inverse, inverse_out,
+    bc_slots, tap_slots, row_slots, stat, turned,
     pos, spread, dtin, state, xs, yin, cbm,
     load_sems, store_sems, ring_send, ring_recv, core_send, core_recv, mp_send, mp_recv,
 ):
@@ -764,25 +829,25 @@
     length, features = normed.shape
     inner, width = gate.shape[1], xin.shape[1]
     shard, column_shard = stage_a.shape[0], stage_b.shape[1]
-    heads, per = w_dt.shape[1], w_bc.shape[1]
+    heads, per = w_dt.shape[0], w_bc.shape[0]
     loads, stores = Loads(load_sems), Loads(store_sems)
     load_x = loads.start(w_x, stage_a)
-    load_tok = loads.start(tok, v_tc)
+    load_tok = loads.start(tok, v_tok)
     load_out = loads.start(w_out, stage_b)
     starts = [jnp.int32(0)]
     for k in range(DOCS - 1):
         starts.append(starts[-1] + lengths[0, k])
 
-    wide[...] = jnp.zeros_like(wide)
-    wide[:, :per] = w_bc[...]
-    bc_slots[0] = wide[...].astype(bf16)
+    turned[...] = jnp.zeros_like(turned)
+    turned[:per, :] = w_bc[...]
+    bc_slots[0] = turned[...].T.astype(bf16)
     tap_slots[0] = jnp.zeros_like(tap_slots[0])
     tap_slots[0, :CONV, :per] = conv_bc[...]
     tap_slots[0, CONV : CONV + 1, :per] = conv_bc_bias[...]
-    wide[...] = jnp.zeros_like(wide)
-    wide[:, :heads] = w_dt[...]
+    turned[...] = jnp.zeros_like(turned)
+    turned[:heads, :] = w_dt[...]
     own_rows = pl.ds(pl.multiple_of(ring.me * shard, shard), shard)
-    wxd[own_rows, width:] = wide[...].astype(bf16)
+    wxd[own_rows, width:] = turned[...].T.astype(bf16)
     dpar[...] = jnp.zeros_like(dpar)
     dpar[0:1, :heads] = dt_bias[...]
     dpar[1:2, :heads] = a_rate[...]
@@ -822,9 +887,10 @@
     crow[0:1, :] = out_gain[...]
     crow[1:2, :] = expand(dpar[...], spread[...])[2:3]
     load_tok.wait()
-    normalize(tok=v_tc, gain=gain, normed=normed, stat=inverse)
-    load_cot = loads.start(cot, v_tc)
+    normalize(v_tok, gain, normed, inverse)
+    load_cot = loads.start(cot, v_tok)
     store_normed = stores.start(normed, normed_o)
+    stores.start(inverse, inverse_o)
     for k in range(2):
         for i in range(1, n):
             exchange(k, i).wait()
@@ -884,7 +950,10 @@
     convolve(xin, taps, pos, slope, x_low, bc_low)
     get_z.second()
     get_out.start()
-    for source, target in ((slope, slope_o), (x_low, x_low_o)):
+    for source, target in (
+        (slope, slope_o), (x_low, x_low_o), (bc_low, bc_low_o), (step, step_o), (sgdt, sgdt_o),
+        (step_low, step_low_o), (decay_low, decay_low_o),
+    ):
         stores.start(source, target)
 
     def scan_tick(b):
@@ -897,20 +966,28 @@
     )
     for source, target in ((ssd, ssd_o), (states, states_o)):
         stores.start(source, target)
-    get_out.second()
     for k in range(4):
         get_z.arrived(k)
     project_rows(normed, wz, gate)
     stores.start(wz, wz_o)
+    stores.start(gate, gate_o)
+    gate_squares(gate, ssd, x_low, crow, gated, stat)
+    for b in range(length // BLOCK):
+        columns = slice(b * BLOCK, (b + 1) * BLOCK)
+        row_slots[0, :, columns] = stat[columns, :].T[:8]
+    for i in range(1, n):
+        exchange(2, i).start()
+
     load_cot.wait()
 
     def back_chip(k, source):
         get_out.arrived(k)
         part = pl.ds(pl.multiple_of((source // 2) * 2 * column_shard, 2 * column_shard), 2 * column_shard)
+        stores.start(wout.at[:, part], wout_o.at[:, part])
 
         def body(i, carry):
             at = pl.ds(pl.multiple_of(i * 512, 512), 512)
-            left = v_tc[at, part]
+            left = v_tok[at, part]
             for c, w in tiles(inner, 512):
                 here = mm_nt(left, wout[c : c + w, part])
                 if k == 0:
@@ -922,45 +999,44 @@
         lax.fori_loop(0, length // 512, body, 0)
 
     back_chip(0, ring.me)
+    get_out.second()
+    for i in range(1, n):
+        exchange(2, i).wait()
+    for b in range(length // BLOCK):
+        columns = slice(b * BLOCK, (b + 1) * BLOCK)
+        total = functools.reduce(lambda p, q: p + q, [row_slots[i, 0:1, columns] for i in range(n)])
+        turned[...] = jnp.broadcast_to(lax.rsqrt(total / (inner * n) + EPS), turned.shape)
+        inverse_out[columns, :] = turned[...].T
+    store_normed.wait()
+    gn = normed.at[:, pl.ds(0, inner)]
+    scale_rows(gated, inverse_out, crow, gn)
+    stores.start(gn, gn_o)
+    stores.start(inverse_out, inverse_out_o)
     back_chip(1, ring.left)
     back_chip(2, ring.right)
     get_out.third()
     back_chip(3, ring.across)
-    stores.start(wout, wout_o)
-    gate_sums(gate, ssd, x_low, gnorm, crow, stat)
+    stores.start(gnorm, gnorm_o)
+    cross_sums(gnorm, gn, stat)
     for b in range(length // BLOCK):
         columns = slice(b * BLOCK, (b + 1) * BLOCK)
-        row_slots[0, :, columns] = stat[columns, :].T[:8]
-    for i in range(1, n):
-        exchange(2, i).start()
-    store_normed.wait()
-    turned[...] = jnp.zeros_like(turned)
-    for i in range(1, n):
-        exchange(2, i).wait()
-    for b in range(length // BLOCK):
-        columns = slice(b * BLOCK, (b + 1) * BLOCK)
-        turned[0:8, :] = functools.reduce(lambda p, q: p + q, [row_slots[i, :, columns] for i in range(n)])
-        stat[columns, :] = turned[...].T
-    gn = v_tc.at[:, pl.ds(0, inner)]
-    low_gate = v_tc.at[:, pl.ds(inner, inner)]
-    gs = normed.at[:, pl.ds(0, inner)]
-    gate_backward(gate, ssd, x_low, gnorm, crow, stat, inner * n, gn, low_gate, gs, sums)
-    for source, target in ((gn, gn_o), (low_gate, low_gate_o), (gs, gs_o)):
-        stores.start(source, target)
+        rows[:, columns] = stat[columns, :].T[:8]
     for each in (get_x, get_bd, get_z, get_out):
         each.drain()
-    for copy in stores.pairs[1:]:
-        copy.wait()
+    for copy in stores.pairs:
+        if copy is not store_normed:
+            copy.wait()
 
 
 def output_kernel(
-    lengths, tok, gn, wout, cot, x_low, ssd, states, gs, slope, xin, bc_low, step, sgdt, step_low, decay_low,
-    taps, crow, dpar,
-    out, dwout, low_xd, csums, dsums,
-    v_gn, v_wout, v_cot, v_x, v_ssd, v_states, v_gs, v_slope, v_xin,
-    part, slots, cores, parts, wholes,
-    pos, rpos, spread, gpre, dstate, xs, gx, cbm, acc,
-    load_sems, cot_sems, line_send, line_recv, core_send, core_recv, ring_send, ring_recv,
+    lengths, rows_own, tok, gn, wout, cot, gate, gnorm_o, x_low, ssd, states, slope, xin, bc_low, step, sgdt,
+    step_low, decay_low, inverse_out, taps, crow, dpar,
+    low_gate, low_xd, out, dwout_o, csums, dsums, sums,
+    v_gn, v_wout, v_cot, v_x, v_ssd, v_states, gs, v_slope, first_wide, second_wide, v_xd, dwout,
+    v_bc, v_step, v_sgdt, v_step_low, v_decay_low, v_inverse,
+    part, slots, cores, parts, wholes, row_slots, turned, stat,
+    pos, rpos, spread, dstate, xs, gx, cbm, acc,
+    load_sems, wout_sems, cot_sems, line_send, line_recv, core_send, core_recv, ring_send, ring_recv, mp_send, mp_recv,
 ):
     ring = Ring()
     starts = [jnp.int32(0)]
@@ -969,18 +1045,29 @@
     loads = Loads(load_sems)
     n = lax.axis_size("mp")
     z = lax.axis_index("mp")
+    length, inner = v_gn.shape
     own = part.shape[1] // n
-    load_gn = loads.start(gn, v_gn)
-    load_wout = loads.start(wout, v_wout)
-    later = [
-        loads.start(source, target)
-        for source, target in (
-            (x_low, v_x), (ssd, v_ssd), (states, v_states), (gs, v_gs), (slope, v_slope), (xin, v_xin),
-        )
-    ]
-    greet(ring, False)
+    v_gate = first_wide.at[pl.ds(0, length), pl.ds(0, inner)]
+    gnorm = second_wide.at[pl.ds(0, length), pl.ds(0, inner)]
     total = gx.at[:, pl.ds(0, own)]
     line = Line(part, slots, (line_send, line_recv), total)
+
+    def wout_copy(i):
+        columns = line.columns(line.order(i))
+        return pltpu.make_async_copy(wout.at[:, columns], v_wout.at[:, columns], wout_sems.at[i])
+
+    load_gn = loads.start(gn, v_gn)
+    wout_copy(0).start()
+    row_slots[0] = rows_own[...]
+    greet(ring, False)
+
+    def exchange(i):
+        return remote(
+            row_slots.at[0], row_slots.at[i], mp_send.at[i - 1], mp_recv.at[i - 1], mp=(z + i) % n
+        )
+
+    for i in range(1, n):
+        exchange(i).start()
     chunk = v_cot.shape[2]
     shard = dwout.shape[1]
 
@@ -989,16 +1076,28 @@
             cot.at[:, pl.ds(pl.multiple_of(j * chunk, chunk), chunk)], v_cot.at[j % 2], cot_sems.at[j % 2]
         )
 
+    load_gn.wait()
+    for i in range(1, n):
+        wout_copy(i).start()
     cot_copy(0).start()
-    fill_spread(spread)
-    fill_positions(starts, pos, rpos)
-    load_gn.wait()
-    load_wout.wait()
+    early = [
+        loads.start(source, target)
+        for source, target in (
+            (gate, v_gate), (gnorm_o, gnorm), (x_low, v_x), (ssd, v_ssd), (inverse_out, v_inverse),
+        )
+    ]
+    later = [
+        loads.start(source, target)
+        for source, target in (
+            (states, v_states), (slope, v_slope), (bc_low, v_bc), (step, v_step), (sgdt, v_sgdt),
+            (step_low, v_step_low), (decay_low, v_decay_low),
+        )
+    ]
 
     def quarter(i, carry):
-        q = line.order(i)
-        columns = line.columns(q)
-        for r in range(0, part.shape[0], 512):
+        columns = line.columns(line.order(i))
+        wout_copy(i).wait()
+        for r in range(0, length, 512):
             part[r : r + 512, columns] = mm(v_gn[r : r + 512, :], v_wout[:, columns]).astype(bf16)
 
         @pl.when(i == 0)
@@ -1006,11 +1105,10 @@
             line.inject(0)
             line.inject(1)
 
-        line.inject(i + 2)
         return carry
 
     lax.fori_loop(0, n, quarter, 0)
-
+    line.inject(2)
     grads = v_wout
     scatter = Scatter(
         ring, lambda r: grads.at[:, pl.ds(pl.multiple_of(r * shard, shard), shard)], cores, parts, wholes,
@@ -1024,66 +1122,91 @@
 
         cot_copy(j).wait()
         columns = pl.ds(pl.multiple_of(j * chunk, chunk), chunk)
-        for r in range(0, grads.shape[0], 256):
+        for r in range(0, inner, 256):
             grads[r : r + 256, columns] = mm_tn(v_gn[:, r : r + 256], v_cot[j % 2]).astype(bf16)
         scatter.start(j)
-
-        @pl.when(j == 2)
+        return carry
+
+    lax.fori_loop(0, 4, weight, 0)
+    line.inject(3)
+    line.forward(0, 1)
+    v_tok, v_out = v_cot.at[0], v_cot.at[1]
+    load_tok = loads.start(tok.at[:, pl.ds(pl.multiple_of(z * own, own), own)], v_tok)
+    fill_spread(spread)
+    fill_positions(starts, pos, rpos)
+    for copy in early:
+        copy.wait()
+    for i in range(1, n):
+        exchange(i).wait()
+    for b in range(length // BLOCK):
+        columns = slice(b * BLOCK, (b + 1) * BLOCK)
+        row = functools.reduce(lambda p, q: p + q, [row_slots[i, 0:1, columns] for i in range(n)])
+        turned[...] = jnp.broadcast_to(row / (inner * n), turned.shape)
+        stat[columns, :] = turned[...].T
+    gate_backward(
+        v_gate, v_ssd, v_x, gnorm, crow, stat, inner * n, None, v_gn, gs, sums, known=v_inverse
+    )
+    load_xin = loads.start(xin, second_wide)
+    store_gate = loads.start(v_gn, low_gate)
+    line.inject(4)
+    line.forward(1, 1)
+    line.forward(0, 2)
+    scatter.first()
+    for copy in later:
+        copy.wait()
+
+    def scan_tick(i):
+        line.inject(i + 5)
+        line.forward(i + 2, 1)
+
+        @pl.when(i < 3)
         def _():
-            line.forward(0, 1)
-            line.inject(6)
-
-        return carry
-
-    lax.fori_loop(0, 4, weight, 0)
-    v_tok = v_cot.at[0]
-    load_tok = loads.start(tok.at[:, pl.ds(pl.multiple_of(z * own, own), own)], v_tok)
-    for copy in later[:5]:
-        copy.wait()
-
-    def scan_tick(i):
-        @pl.when(i == 0)
-        def _():
-            scatter.first()
+            line.forward(i + 1, 2)
 
         @pl.when(i == 1)
         def _():
             scatter.second()
 
-        line.forward(i + 1, 1)
-        line.forward(i, 2)
-        line.inject(i + 7)
-
+    gpre = first_wide
     scan_backward(
-        starts, v_x, bc_low, step_low, decay_low, v_ssd, v_states, v_gs, v_slope, crow, step, sgdt, dpar,
-        gpre, low_xd, dsums, spread, dstate, xs, gx, cbm, acc, scan_tick,
-    )
+        starts, v_x, v_bc, v_step_low, v_decay_low, v_ssd, v_states, gs, v_slope, crow, v_step, v_sgdt, dpar,
+        gpre, v_xd, dsums, spread, dstate, xs, gx, cbm, acc, scan_tick,
+    )
+    scatter.finish(dwout)
+    store_dwout = loads.start(dwout, dwout_o)
+    load_xin.wait()
+
+    def conv_tick(b):
+        @pl.when(b % 2 == 1)
+        def _():
+            line.inject(9 + b // 2)
+            line.forward(6 + b // 2, 1)
+
+    convolve_back(second_wide, gpre, taps, pos, rpos, v_xd, csums, conv_tick)
     line.inject(11)
-    line.forward(5, 1)
-    scatter.finish(dwout)
-    later[5].wait()
-    convolve_back(v_xin, gpre, taps, pos, rpos, low_xd, csums)
-    line.forward(6, 1)
-    line.forward(7, 1)
+    store_xd = loads.start(v_xd, low_xd)
     load_tok.wait()
 
     def last(t, carry):
         line.finish(t)
-        out[line.rows(t), :] = (v_tok[line.rows(t), :].astype(f32) + total[...]).astype(bf16)
+        v_out[line.rows(t), :] = (v_tok[line.rows(t), :].astype(f32) + total[...]).astype(bf16)
         return carry
 
     lax.fori_loop(0, line.blocks, last, 0)
+    store_out = loads.start(v_out, out)
     line.drain()
+    for copy in (store_gate, store_dwout, store_xd, store_out):
+        copy.wait()
 
 
 def input_kernel(
     tok, inverse, gain, normed, low_gate, low_xd, wz, wxd, cot, csums, sums, dsums,
-    grad, dwz, dwx, dwbc, dwdt, conv_x, conv_x_bias, conv_bc, conv_bc_bias, dt_bias, a_rate, d_skip, in_gain, out_gain,
-    dwxd, smalls, spread, bc_own, bc_slots,
+    dwz_o, dwx_o, grad, dwbc, dwdt, conv_x, conv_x_bias, conv_bc, conv_bc_bias, dt_bias, a_rate, d_skip, in_gain, out_gain,
+    dwz, dwxd, smalls, spread, bc_own, bc_slots,
     v_tok, v_normed, v_gate, v_xd, v_wz, v_wxd, v_cot,
     part, slots, total, z_grads, z_cores, z_parts, z_wholes, x_grads, x_cores, x_parts, x_wholes,
     rowacc, rows_own, rows_in, colacc, dp_in, bc_in, gain_in,
-    load_sems, line_send, line_recv, z_core_send, z_core_recv, z_ring_send, z_ring_recv,
+    load_sems, quarter_sems, line_send, line_recv, z_core_send, z_core_recv, z_ring_send, z_ring_recv,
     x_core_send, x_core_recv, x_ring_send, x_ring_recv,
     rows_send, rows_recv, dp_send, dp_recv, mp_send, mp_recv, bc_send, bc_recv,
 ):
@@ -1095,25 +1218,41 @@
     length, features = part.shape
     inner = v_gate.shape[1]
     width = smalls.shape[1]
-    heads, per = dwdt.shape[1], dwbc.shape[1]
-    first = [
-        loads.start(source, target)
-        for source, target in ((low_gate, v_gate), (wz, v_wz), (low_xd, v_xd), (wxd, v_wxd), (tok, v_tok))
-    ]
+    heads, per = dwdt.shape[0], dwbc.shape[0]
     own = features // n
     own_columns = pl.ds(pl.multiple_of(z * own, own), own)
+    line = Line(part, slots, (line_send, line_recv), total)
+
+    def quarter_loads(i):
+        columns = line.columns(line.order(i))
+        return [
+            pltpu.make_async_copy(source, target, quarter_sems.at[i, k])
+            for k, (source, target) in enumerate((
+                (wz.at[columns, :], v_wz.at[columns, :]),
+                (wxd.at[columns, :], v_wxd.at[columns, :]),
+                (tok.at[:, columns], v_tok.at[:, columns]),
+            ))
+        ]
+
+    first = [loads.start(source, target) for source, target in ((low_gate, v_gate), (low_xd, v_xd))]
+    for copy in quarter_loads(0):
+        copy.start()
+    greet(ring, True)
+    rowacc[...] = jnp.zeros_like(rowacc)
+    for copy in first:
+        copy.wait()
+    for i in range(1, n):
+        for copy in quarter_loads(i):
+            copy.start()
     later = [
         loads.start(source, target)
         for source, target in ((normed, v_normed), (cot.at[:, own_columns], v_cot))
     ]
-    greet(ring, True)
-    line = Line(part, slots, (line_send, line_recv), total)
-    rowacc[...] = jnp.zeros_like(rowacc)
-    for copy in first:
-        copy.wait()
 
     def quarter(i, carry):
         columns = line.columns(line.order(i))
+        for copy in quarter_loads(i):
+            copy.wait()
         for r in range(0, length, 256):
             rows = slice(r, r + 256)
             here = mm_nt(v_gate[rows, :], v_wz[columns, :]) + mm_nt(v_xd[rows, :], v_wxd[columns, :])
@@ -1135,10 +1274,14 @@
             line.inject(0)
             line.inject(1)
 
-        line.inject(i + 2)
+        @pl.when(i == 2)
+        def _():
+            line.inject(2)
+
         return carry
 
     lax.fori_loop(0, n, quarter, 0)
+    line.inject(3)
     line.forward(0, 1)
 
     for b in range(length // BLOCK):
@@ -1202,15 +1345,11 @@
     def z_weight(j, carry):
         weight(j, v_gate, z_grads)
         z_scatter.start(j)
-
-        @pl.when(j % 2 == 1)
-        def _():
-            line.inject(6 + j // 2)
-            line.forward(1 + j // 2, 1)
-
         return carry
 
     lax.fori_loop(0, 4, z_weight, 0)
+    line.inject(4)
+    line.forward(1, 1)
     line.forward(0, 2)
 
     def x_weight(j, carry):
@@ -1223,17 +1362,18 @@
 
         @pl.when(j % 2 == 1)
         def _():
-            line.inject(8 + j // 2)
-            line.forward(3 + j // 2, 1)
-            line.forward(1 + j // 2, 2)
+            line.inject(5 + j // 2)
+            line.forward(2 + j // 2, 1)
 
         return carry
 
     lax.fori_loop(0, 4, x_weight, 0)
+    line.forward(1, 2)
+    x_scatter.first()
     z_scatter.second()
-    line.inject(10)
-    line.inject(11)
-    x_scatter.first()
+    line.inject(7)
+    line.forward(4, 1)
+    line.forward(2, 2)
 
     for i in range(1, size):
         dp_copy(i).wait()
@@ -1241,20 +1381,25 @@
     for i in range(1, n):
         bc_copy(i).start()
         gain_copy(i).start()
+    x_scatter.second()
+    line.inject(8)
     line.forward(5, 1)
     line.forward(3, 2)
     z_scatter.finish(dwz)
+    store_z = loads.start(dwz, dwz_o)
+    line.inject(9)
+    line.forward(6, 1)
     for i in range(1, n):
         rows_copy(i).wait()
     rows_own[...] += functools.reduce(lambda a, b: a + b, [rows_in[i] for i in range(n - 1)])
-    x_scatter.second()
-    line.forward(6, 1)
+    line.inject(10)
     line.forward(7, 1)
     for i in range(1, n):
         bc_copy(i).wait()
         gain_copy(i).wait()
     smalls[0:8, inner:] += functools.reduce(lambda a, b: a + b, [bc_in[i] for i in range(n - 1)])
     smalls[8:16, :inner] += functools.reduce(lambda a, b: a + b, [gain_in[i] for i in range(n - 1)])
+    line.inject(11)
     x_scatter.finish(dwxd)
     share = LANES // per
 
@@ -1274,8 +1419,8 @@
 
     for i in range(1, n):
         weight_copy(i).start()
-    cast_into(dwx, dwxd.at[:, pl.ds(0, inner)])
-    dwdt[...] = dwxd[:, width : width + heads]
+    store_x = loads.start(dwxd.at[:, pl.ds(0, inner)], dwx_o)
+    dwdt[...] = dwxd[:, width:].T[:heads]
     lanes = pl.ds(pl.multiple_of(inner + (z // share) * LANES, LANES), LANES)
     conv_x[...] = smalls[:CONV, :inner]
     conv_x_bias[...] = smalls[CONV : CONV + 1, :inner]
@@ -1292,7 +1437,7 @@
     for i in range(1, n):
         weight_copy(i).wait()
     here = functools.reduce(lambda a, b: a + b, [bc_slots[i].astype(f32) for i in range(n - 1)], dwxd[:, lanes])
-    dwbc[...] = mine(here)[:, :per]
+    dwbc[...] = mine(here).T[:per]
     later[1].wait()
 
     def last(t, carry):
@@ -1308,6 +1453,31 @@
 
     lax.fori_loop(0, line.blocks, last, 0)
     line.drain()
+    store_z.wait()
+    store_x.wait()
+
+
+def hand_on_kernel(*refs):
+    count = (len(refs) - 2) // 3
+    sources, targets, buffers = refs[:count], refs[count : 2 * count], refs[2 * count : 3 * count]
+    into, out = refs[-2:]
+    there = [pltpu.make_async_copy(sources[k], buffers[k], into.at[k]) for k in range(count)]
+    back = [pltpu.make_async_copy(buffers[k], targets[k], out.at[k]) for k in range(count)]
+    for copy in there:
+        copy.start()
+    for k in range(count):
+        there[k].wait()
+        back[k].start()
+    for copy in back:
+        copy.wait()
+
+
+def hand_on(*arrays):
+    kinds = [(v.shape, v.dtype) for v in arrays]
+    return call(
+        hand_on_kernel, kinds, kinds, 0, *arrays,
+        places="a" * len(arrays), sems=[(len(arrays),)] * 2, far=len(arrays),
+    )
 
 
 def call(kernel, outs, scratch, smem, *operands, places=None, sems=(), collective=None, far=0):
@@ -1464,68 +1634,74 @@
         return v[None, :]
 
     (
-        normed, xin, slope, x_low, ssd, states, wxd, wz, wout, gn, low_gate, gs,
-        bc_low, step, sgdt, step_low, decay_low, inverse, sums, taps, crow, dpar,
+        normed, xin, slope, x_low, ssd, states, wxd, wz, wout, gn, gate, gnorm,
+        bc_low, step, sgdt, step_low, decay_low, inverse, inverse_out, taps, crow, dpar, rows,
     ) = call(
         gather_kernel,
         [
             ((T, D), bf16), ((T + 8, width), f32), ((T, width), bf16), ((T, inner), bf16), ((T, inner), bf16),
             ((blocks, STATE, inner), bf16), ((D, wide), bf16), ((D, inner), bf16), ((inner, D), bf16),
-            ((T, inner), bf16), ((T, inner), bf16), ((T, inner), bf16),
+            ((T, inner), bf16), ((T, inner), f32), ((T, inner), f32),
             ((T, pair), bf16), ((T, LANES), f32), ((T, LANES), f32), ((T, LANES), bf16), ((T, LANES), bf16),
-            ((T, LANES), f32), ((16, inner), f32), ((8, width), f32), ((8, inner), f32), ((8, LANES), f32),
+            ((T, LANES), f32), ((T, LANES), f32),
+            ((8, width), f32), ((8, inner), f32), ((8, LANES), f32), ((8, T), f32),
         ],
         [
             ((T, D), bf16), ((shard, inner), f32), ((inner, columns), f32), ((T, D), bf16), ((T + 8, width), f32),
             ((T, width), bf16), ((T, inner), bf16), ((T, inner), bf16), ((blocks, STATE, inner), bf16),
             ((D, wide), bf16), ((D, inner), bf16), ((inner, D), bf16), ((T, inner), f32), ((T, inner), f32),
-            ((group, shard, LANES), bf16), ((group, 8, LANES), f32), ((group, 8, T), f32), ((shard, LANES), f32),
+            ((T, inner), f32),
+            ((T, pair), bf16), ((T, LANES), f32), ((T, LANES), f32), ((T, LANES), bf16), ((T, LANES), bf16),
+            ((T, LANES), f32), ((T, LANES), f32),
+            ((group, shard, LANES), bf16), ((group, 8, LANES), f32), ((group, 8, T), f32),
             ((T, LANES), f32), ((LANES, BLOCK), f32),
             ((T, LANES), jnp.int32), ((LANES, inner), bf16), ((T, LANES), f32), ((STATE, inner), f32),
             ((BLOCK, inner), bf16), ((BLOCK, inner), f32), ((BLOCK, BLOCK), f32),
         ],
-        0, doc_lengths, tokens, cotangent, w_x, w_z, w_out, w_bc, w_dt, conv_x, row(conv_x_bias), conv_bc,
+        0, doc_lengths, tokens, cotangent, w_x, w_z, w_out, w_bc.T, w_dt.T, conv_x, row(conv_x_bias), conv_bc,
         row(conv_bc_bias), row(dt_bias), row(a_rate), row(d_skip), row(input_norm_gain), row(out_gain),
         places="s" + "a" * 5 + "v" * 11,
-        sems=[(5,), (12,), (4, 4), (4, 4), (4, 4), (4, 4), (3 * group - 3,), (3 * group - 3,)],
+        sems=[(5,), (23,), (4, 4), (4, 4), (4, 4), (4, 4), (3 * group - 3,), (3 * group - 3,)],
         collective=0,
-        far=12,
-    )
-    output, w_out_grad, low_xd, csums, dsums = call(
+        far=19,
+    )
+    low_gate, low_xd, output, w_out_grad, csums, dsums, sums = call(
         output_kernel,
         [
-            ((T, own), bf16), ((inner, columns), f32), ((T, wide), bf16), ((8 * CONV + 8, width), f32),
-            ((16, LANES), f32),
+            ((T, inner), bf16), ((T, wide), bf16),
+            ((T, own), bf16), ((inner, columns), f32), ((8 * CONV + 8, width), f32), ((16, LANES), f32),
+            ((16, inner), f32),
         ],
         [
             ((T, inner), bf16), ((inner, D), bf16), ((2, T, 2 * columns), bf16), ((T, inner), bf16),
             ((T, inner), bf16), ((blocks, STATE, inner), bf16), ((T, inner), bf16), ((T, width), bf16),
-            ((T + 8, width), f32),
+            ((T + 8, width), f32), ((T + 8, width), f32), ((T, wide), bf16), ((inner, columns), f32),
+            ((T, pair), bf16), ((T, LANES), f32), ((T, LANES), f32), ((T, LANES), bf16), ((T, LANES), bf16),
+            ((T, LANES), f32),
             ((T, D), bf16), ((2, messages, BLOCK, own), bf16),
             ((4, inner, columns), bf16), ((2, inner // 2, columns), bf16), ((2, inner, columns), bf16),
-            ((T, LANES), jnp.int32), ((T, LANES), jnp.int32), ((LANES, inner), bf16), ((T + 8, width), f32),
+            ((group, 8, T), f32), ((LANES, BLOCK), f32), ((T, LANES), f32),
+            ((T, LANES), jnp.int32), ((T, LANES), jnp.int32), ((LANES, inner), bf16),
             ((STATE, inner), f32), ((BLOCK, inner), bf16), ((BLOCK, inner), f32), ((BLOCK, BLOCK), f32),
             ((BLOCK, BLOCK), f32),
         ],
-        0, doc_lengths, tokens, gn, wout, cotangent, x_low, ssd, states, gs, slope, xin, bc_low, step, sgdt,
-        step_low, decay_low, taps, crow, dpar,
-        places="s" + "a" * 10 + "v" * 8,
-        sems=[(9,), (2,), (2, messages), (2, messages), (4,), (4,), (4,), (4,)],
+        0, doc_lengths, rows, tokens, gn, wout, cotangent, gate, gnorm, x_low, ssd, states, slope, xin, bc_low,
+        step, sgdt, step_low, decay_low, inverse_out, taps, crow, dpar,
+        places="sv" + "a" * 17 + "v" * 3,
+        sems=[(19,), (group,), (2,), (2, messages), (2, messages), (4,), (4,), (4,), (4,), (group - 1,), (group - 1,)],
         collective=1,
-    )
-    (
-        input_grad, w_z_grad, w_x_grad, w_bc_grad, w_dt_grad, conv_x_grad, conv_x_bias_grad, conv_bc_grad,
-        conv_bc_bias_grad, dt_bias_grad, a_rate_grad, d_skip_grad, in_gain_grad, out_gain_grad,
-    ) = call(
+        far=4,
+    )
+    w_z_grad, w_x_grad, input_grad, w_bc_grad, w_dt_grad, *small_grads = call(
         input_kernel,
         [
-            ((T, own), bf16), ((shard, inner), f32), ((shard, inner), f32), ((shard, per), f32),
-            ((shard, heads), f32), ((CONV, inner), f32), ((1, inner), f32), ((CONV, per), f32), ((1, per), f32),
+            ((shard, inner), f32), ((shard, inner), f32), ((T, own), bf16), ((per, shard), f32),
+            ((heads, shard), f32), ((CONV, inner), f32), ((1, inner), f32), ((CONV, per), f32), ((1, per), f32),
             ((1, heads), f32), ((1, heads), f32), ((1, heads), f32), ((1, own), f32), ((1, inner), f32),
         ],
         [
-            ((shard, wide), f32), ((16, width), f32), ((LANES, inner), bf16), ((pair // LANES, shard, LANES), bf16),
-            ((group - 1, shard, LANES), bf16),
+            ((shard, inner), f32), ((shard, wide), f32), ((16, width), f32), ((LANES, inner), bf16),
+            ((pair // LANES, shard, LANES), bf16), ((group - 1, shard, LANES), bf16),
             ((T, D), bf16), ((T, D), bf16), ((T, inner), bf16), ((T, wide), bf16), ((D, inner), bf16),
             ((D, wide), bf16), ((T, own), bf16),
             ((T, D), bf16), ((2, messages, BLOCK, own), bf16), ((BLOCK, own), f32),
@@ -1537,14 +1713,19 @@
         0, tokens, inverse, row(input_norm_gain), normed, low_gate, low_xd, wz, wxd, cotangent, csums, sums, dsums,
         places="avvaaaaaavvv",
         sems=[
-            (7,), (2, messages), (2, messages), (4,), (4,), (4,), (4,), (4,), (4,), (4,), (4,),
+            (6,), (group, 3), (2, messages), (2, messages), (4,), (4,), (4,), (4,), (4,), (4,), (4,), (4,),
             (group - 1,), (group - 1,), (size - 1,), (size - 1,), (2 * group - 2,), (2 * group - 2,),
             (group - 1,), (group - 1,),
         ],
         collective=2,
-    )
+        far=2,
+    )
+    (
+        output, input_grad, w_z_grad, w_x_grad, w_bc_grad, w_dt_grad, w_out_grad, conv_x_grad, conv_x_bias_grad,
+        conv_bc_grad, conv_bc_bias_grad, dt_bias_grad, a_rate_grad, d_skip_grad, in_gain_grad, out_gain_grad,
+    ) = hand_on(output, input_grad, w_z_grad, w_x_grad, w_bc_grad, w_dt_grad, w_out_grad, *small_grads)
     return (
-        output, input_grad, w_z_grad, w_x_grad, w_bc_grad, w_dt_grad, w_out_grad,
+        output, input_grad, w_z_grad, w_x_grad, w_bc_grad.T, w_dt_grad.T, w_out_grad,
         conv_x_grad, conv_x_bias_grad[0], conv_bc_grad, conv_bc_bias_grad[0], dt_bias_grad[0], a_rate_grad[0],
         d_skip_grad[0], in_gain_grad[0], out_gain_grad[0],
     )

time: 283 us -> 247 us (0.87)
  Pallas kernels: 264 us -> 246 us
  local copies, waits for them, and re-layouts: 17.6 us -> 0 us
    pallas_call x3 -> x4, Pallas kernels: 264 us -> 246 us  [call(): pl.pallas_call(kernel, out_shape=[jax.ShapeDtypeStruct(shape, kind) for s...]
    unnamed x44 -> x0, local copies, waits for them, and re-layouts: 17.6 us -> none
where the time goes in v4:
time: 247 us
  Pallas kernels  246 us (100%)
    pallas_call x4, Pallas kernels, call(): pl.pallas_call(kernel, out_shape=[jax.ShapeDtypeStruct(shape, kind) for s...  246 us

profile of v4, /device:TPU:0, one launch (start us, length us, event | category | flops | bytes accessed | tf_op | source)
XLA Modules:
  0.0 247.1 jit_solution(8278399544344663020)
XLA Ops:
  0.7 77.0 %shard_map.288 = (bf16[1024,2048]{1,0:T(8,128)(2,1)}, f32[1032,1280]{1,0:T(8,128)}, bf16[1024,1280]{1,0:T(8,128)(2,1)}, bf16[1024,1024]{1,0:T(8,128)(2,1)}, bf16...) custom-call(s32[1,5]{1,0:T(1,128)} %lengths.3, ...), custom_call_target="tpu_custom_call" | custom-call | tf_op jit(solution)/shard_map/pallas_call | solution.py:1488
  77.6 75.3 %shard_map.289 = (bf16[1024,1024]{1,0:T(8,128)(2,1)}, bf16[1024,1408]{1,0:T(8,128)(2,1)}, bf16[1024,512]{1,0:T(8,128)(2,1)}, f32[1024,256]{1,0:T(8,128)}, f32[40...) custom-call(s32[1,5]{1,0:T(1,128)} %lengths.3, f32[8,1024]{1,0:T(8,128)} %get-tuple-element.76.rows_own, ...), custom_call_target="tpu_custom_call" | custom-call | tf_op jit(solution)/shard_map/pallas_call | solution.py:1488
  153.0 89.2 %shard_map.290 = (f32[256,1024]{1,0:T(8,128)}, f32[256,1024]{1,0:T(8,128)}, bf16[1024,512]{1,0:T(8,128)(2,1)}, f32[64,256]{1,0:T(8,128)}, f32[16,256]{1,0:T(8,12...) custom-call(bf16[1024,2048]{1,0:T(8,128)(2,1)} %tok.5, ...), custom_call_target="tpu_custom_call" | custom-call | tf_op jit(solution)/shard_map/pallas_call | solution.py:1488
  242.2 4.7 %shard_map.291 = (bf16[1024,512]{1,0:T(8,128)(2,1)}, bf16[1024,512]{1,0:T(8,128)(2,1)}, f32[256,1024]{1,0:T(8,128)}, f32[256,1024]{1,0:T(8,128)}, f32[64,256]{1,...) custom-call(bf16[1024,512]{1,0:T(8,128)(2,1)} %get-tuple-element.95., ...), custom_call_target="tpu_custom_call" | custom-call | tf_op jit(solution)/shard_map/pallas_call | solution.py:1488

commit v5 on v4

--- a/solution.py
+++ b/solution.py
@@ -16,7 +16,7 @@
 EPS = 1e-05
 f32 = jnp.float32
 bf16 = jnp.bfloat16
-VMEM_LIMIT = 62 * 2**20
+VMEM_LIMIT = 127 * 2**19
 
 
 def mm(a, b):
@@ -155,13 +155,18 @@
     lax.fori_loop(0, blocks * bcols, bc_body, 0)
 
 
+def softplus(v):
+    return jnp.maximum(v, 0.0) + jnp.log1p(jnp.exp(-jnp.abs(v)))
+
+
 def steps(dtin, dpar, step, sgdt, step_low, decay_low):
     def body(i, carry):
         rows = pl.ds(pl.multiple_of(i * BLOCK, BLOCK), BLOCK)
         v = dtin[rows, :] + dpar[0:1, :]
-        soft = jnp.maximum(v, 0.0) + jnp.log1p(jnp.exp(-jnp.abs(v)))
-        step[rows, :] = soft
-        sgdt[rows, :] = logistic(v)
+        soft = softplus(v)
+        if step is not None:
+            step[rows, :] = soft
+            sgdt[rows, :] = logistic(v)
         step_low[rows, :] = soft.astype(bf16)
         decay_low[rows, :] = (-dpar[1:2, :] * soft).astype(bf16)
         return carry
@@ -289,7 +294,7 @@
     lax.fori_loop(0, gate.shape[0] // step, body, 0)
 
 
-def gate_squares(gate, ssd, x_low, crow, gated, stat):
+def gate_squares(gate, ssd, x_low, crow, stat):
     step, inner = 64, gate.shape[1]
 
     def body(i, carry):
@@ -300,7 +305,6 @@
             g = gate[rows, cols]
             mixed = ssd[rows, cols].astype(f32) + crow[1:2, cols] * x_low[rows, cols].astype(f32)
             value = mixed * (g * logistic(g))
-            gated[rows, cols] = value
             squares = squares + value * value
         stat[rows, :] = jnp.broadcast_to(jnp.sum(squares, axis=1, keepdims=True), (step, LANES))
         return carry
@@ -308,18 +312,20 @@
     lax.fori_loop(0, gate.shape[0] // step, body, 0)
 
 
-def scale_rows(gated, inverse_out, crow, gn):
-    step, inner = 64, gated.shape[1]
+def gate_norm(gate, ssd, x_low, inverse_out, crow, gn):
+    step, inner = 64, gate.shape[1]
 
     def body(i, carry):
         rows = pl.ds(pl.multiple_of(i * step, step), step)
         inverse = inverse_out[rows, :1]
         for c in range(0, inner, 256):
             cols = slice(c, c + 256)
-            gn[rows, cols] = (gated[rows, cols] * inverse * crow[0:1, cols]).astype(bf16)
-        return carry
-
-    lax.fori_loop(0, gated.shape[0] // step, body, 0)
+            g = gate[rows, cols]
+            mixed = ssd[rows, cols].astype(f32) + crow[1:2, cols] * x_low[rows, cols].astype(f32)
+            gn[rows, cols] = (mixed * (g * logistic(g)) * inverse * crow[0:1, cols]).astype(bf16)
+        return carry
+
+    lax.fori_loop(0, gate.shape[0] // step, body, 0)
 
 
 def cross_sums(gnorm, gn, stat):
@@ -466,10 +472,15 @@
         later = mm(upper, high) + mm(upper, rest) + tail
         grad_decay = later.astype(bf16).astype(f32)
         total_step = grad_step - dpar[1:2, :] * grad_decay
-        grad_dt = total_step * sgdt[rows, :]
+        if sgdt is None:
+            before_step = step[rows, :] + dpar[0:1, :]
+            slope_here, step_here = logistic(before_step), softplus(before_step)
+        else:
+            slope_here, step_here = sgdt[rows, :], step[rows, :]
+        grad_dt = total_step * slope_here
         low_xd[rows, width:] = grad_dt.astype(bf16)
         dsums[0:8, :] += fold(grad_dt)
-        dsums[8:16, :] -= fold(grad_decay * step[rows, :])
+        dsums[8:16, :] -= fold(grad_decay * step_here)
         dstate[...] = kept_e * dstate[...] + mm_tn(cm, g_in)
         if tick is not None:
             tick(i)
@@ -666,29 +677,29 @@
 
 
 class Line:
-    def __init__(self, part, slots, sems, total):
-        self.part, self.slots, self.total = part, slots, total
+    def __init__(self, piece, slot, blocks, sems, total):
+        self.piece, self.slot, self.blocks, self.total = piece, slot, blocks, total
         self.send, self.recv = sems
         self.n, self.z = lax.axis_size("mp"), lax.axis_index("mp")
-        self.blocks = part.shape[0] // BLOCK
-        self.own = part.shape[1] // self.n
         self.place = (self.z, self.n - 1 - self.z)
-        self.count = self.blocks * (self.n - 1)
 
     def rows(self, t):
         return pl.ds(pl.multiple_of(t * BLOCK, BLOCK), BLOCK)
 
-    def columns(self, q):
-        return pl.ds(pl.multiple_of(q * self.own, self.own), self.own)
-
-    def copy(self, side, k):
+    def source(self, side, k):
         d = k // self.blocks
-        q = self.n - 1 - d if side == 0 else d
-        source = self.part.at[self.rows(k - d * self.blocks), self.columns(q)]
+        return self.piece(k - d * self.blocks, self.n - 1 - d if side == 0 else d)
+
+    def copy(self, side, place, k):
         return remote(
-            source, self.slots.at[side, k], self.send.at[side, k], self.recv.at[side, k],
+            self.source(side, k), self.slot(side, place + 1, k), self.send.at[side, k], self.recv.at[side, k],
             mp=self.z + 1 if side == 0 else self.z - 1,
-        ), source
+        )
+
+    def arrived(self, side, place, k):
+        target = self.slot(side, place, k)
+        remote(target, target, self.send.at[side, k], self.recv.at[side, k], mp=self.z).wait_recv()
+        return target
 
     def inject(self, k):
         for side in range(2):
@@ -696,39 +707,37 @@
             def _():
                 @pl.when(jnp.int32(k) >= 2)
                 def _():
-                    self.copy(side, jnp.maximum(k - 2, 0))[0].wait_send()
-
-                self.copy(side, k)[0].start()
+                    self.copy(side, 0, jnp.maximum(k - 2, 0)).wait_send()
+
+                self.copy(side, 0, k).start()
 
     def forward(self, k, hop):
         for side in range(2):
             @pl.when(self.place[side] == hop)
             def _():
-                copy, source = self.copy(side, k)
-                copy.wait_recv()
-                add_into(source, self.slots.at[side, k])
-                copy.start()
+                add_into(self.source(side, k), self.arrived(side, hop, k))
+                self.copy(side, hop, k).start()
 
     def finish(self, t):
-        self.total[...] = self.part[self.rows(t), self.columns(self.z)].astype(f32)
+        self.total[...] = self.piece(t, self.z)[...].astype(f32)
         for side in range(2):
-            @pl.when(self.place[side] >= 1)
-            def _():
-                k = (self.n - 1 - self.place[side]) * self.blocks + t
-                self.copy(side, k)[0].wait_recv()
-                self.total[...] += self.slots[side, k].astype(f32)
+            for place in range(1, self.n):
+                @pl.when(self.place[side] == place)
+                def _():
+                    self.total[...] += self.arrived(side, place, (self.n - 1 - place) * self.blocks + t)[...].astype(f32)
 
     def drain(self):
-        def body(k, carry):
-            for side in range(2):
-                started = self.place[side] + k // self.blocks <= self.n - 2
-
-                @pl.when(started & ((self.place[side] > 0) | (k >= self.count - 2)))
+        for side in range(2):
+            for place in range(self.n - 1):
+                count = (self.n - 1 - place) * self.blocks
+
+                @pl.when(self.place[side] == place)
                 def _():
-                    self.copy(side, k)[0].wait_send()
-            return carry
-
-        lax.fori_loop(0, self.count, body, 0)
+                    def body(k, carry):
+                        self.copy(side, place, k).wait_send()
+                        return carry
+
+                    lax.fori_loop(count - 2 if place == 0 else 0, count, body, 0)
 
     def order(self, i):
         z = self.z
@@ -812,22 +821,25 @@
     lax.fori_loop(0, target.shape[0] // rows, body, 0)
 
 
-def gather_kernel(
+def trunk_kernel(
     lengths, tok, cot, w_x, w_z, w_out, w_bc, w_dt, conv_x, conv_x_bias, conv_bc, conv_bc_bias, dt_bias, a_rate,
     d_skip, gain, out_gain,
-    normed_o, xin_o, slope_o, x_low_o, ssd_o, states_o, wxd_o, wz_o, wout_o, gn_o, gate_o, gnorm_o,
-    bc_low_o, step_o, sgdt_o, step_low_o, decay_low_o, inverse_o, inverse_out_o,
-    taps, crow, dpar, rows,
-    v_tok, stage_a, stage_b, normed, xin, slope, x_low, ssd, states, wxd, wz, wout, gate, gated, gnorm,
-    bc_low, step, sgdt, step_low, decay_low, inverse, inverse_out,
-    bc_slots, tap_slots, row_slots, stat, turned,
-    pos, spread, dtin, state, xs, yin, cbm,
-    load_sems, store_sems, ring_send, ring_recv, core_send, core_recv, mp_send, mp_recv,
+    normed_o, xin_o, wxd_o, wz_o, low_gate_o, low_xd_o, out_o, dwout_o, inverse_o,
+    csums, dsums, sums,
+    v_tok, stage_b, normed, xin, first_wide, slope, x_low, ssd, states, wxd, wz, wout,
+    bc_low, step_low, decay_low, inverse_out, taps, crow, dpar,
+    bc_slots, tap_slots, row_slots, cross_slots, stat, turned,
+    pos, rpos, spread, dtin, state, xs, wide, cbm, acc, near, cores, parts, wholes,
+    load_sems, store_sems, ring_send, ring_recv, core_send, core_recv, mp_send, mp_recv, line_send, line_recv,
+    scatter_core_send, scatter_core_recv, scatter_ring_send, scatter_ring_recv,
 ):
     ring = Ring()
     n, z = lax.axis_size("mp"), lax.axis_index("mp")
     length, features = normed.shape
-    inner, width = gate.shape[1], xin.shape[1]
+    stage_a = wide
+    inverse = inverse_out
+    inner, width = x_low.shape[1], xin.shape[1]
+    own = features // n
     shard, column_shard = stage_a.shape[0], stage_b.shape[1]
     heads, per = w_dt.shape[0], w_bc.shape[0]
     loads, stores = Loads(load_sems), Loads(store_sems)
@@ -856,7 +868,7 @@
     greet(ring, False)
 
     def exchange(k, i):
-        slots = (bc_slots, tap_slots, row_slots)[k]
+        slots = (bc_slots, tap_slots, row_slots, cross_slots)[k]
         at = k * (n - 1) + i - 1
         return remote(slots.at[0], slots.at[i], mp_send.at[at], mp_recv.at[at], mp=(z + i) % n)
 
@@ -883,14 +895,14 @@
             exchange(k, i).start()
     load_z = loads.start(w_z, stage_a)
     fill_spread(spread)
-    fill_positions(starts, pos, None)
+    fill_positions(starts, pos, rpos)
     crow[0:1, :] = out_gain[...]
     crow[1:2, :] = expand(dpar[...], spread[...])[2:3]
     load_tok.wait()
     normalize(v_tok, gain, normed, inverse)
     load_cot = loads.start(cot, v_tok)
     store_normed = stores.start(normed, normed_o)
-    stores.start(inverse, inverse_o)
+    store_inverse = stores.start(inverse, inverse_o)
     for k in range(2):
         for i in range(1, n):
             exchange(k, i).wait()
@@ -944,46 +956,53 @@
     get_x.third()
     get_bd.third()
     project_chip(3, ring.across)
-    for source, target in ((xin, xin_o), (wxd, wxd_o)):
-        stores.start(source, target)
-    steps(dtin, dpar, step, sgdt, step_low, decay_low)
+    store_xin = stores.start(xin, xin_o)
+    store_wxd = stores.start(wxd, wxd_o)
+    steps(dtin, dpar, None, None, step_low, decay_low)
     convolve(xin, taps, pos, slope, x_low, bc_low)
     get_z.second()
     get_out.start()
-    for source, target in (
-        (slope, slope_o), (x_low, x_low_o), (bc_low, bc_low_o), (step, step_o), (sgdt, sgdt_o),
-        (step_low, step_low_o), (decay_low, decay_low_o),
-    ):
-        stores.start(source, target)
-
-    def scan_tick(b):
+
+    def forward_tick(b):
         @pl.when(b == 1)
         def _():
             get_z.third()
 
     scan_forward(
-        starts, x_low, bc_low, step_low, decay_low, ssd, states, spread, state, xs, yin, cbm, scan_tick
-    )
-    for source, target in ((ssd, ssd_o), (states, states_o)):
-        stores.start(source, target)
+        starts, x_low, bc_low, step_low, decay_low, ssd, states, spread, state, xs, wide, cbm, forward_tick
+    )
     for k in range(4):
         get_z.arrived(k)
+    gate = first_wide.at[pl.ds(0, length), pl.ds(0, inner)]
+    gnorm = xin.at[pl.ds(0, length), pl.ds(0, inner)]
     project_rows(normed, wz, gate)
-    stores.start(wz, wz_o)
-    stores.start(gate, gate_o)
-    gate_squares(gate, ssd, x_low, crow, gated, stat)
-    for b in range(length // BLOCK):
-        columns = slice(b * BLOCK, (b + 1) * BLOCK)
-        row_slots[0, :, columns] = stat[columns, :].T[:8]
+    store_wz = stores.start(wz, wz_o)
+    gate_squares(gate, ssd, x_low, crow, stat)
+
+    def put_rows(slots):
+        for b in range(length // BLOCK):
+            columns = slice(b * BLOCK, (b + 1) * BLOCK)
+            slots[0, :, columns] = stat[columns, :].T[:8]
+
+    def sum_rows(slots, out, finish):
+        for b in range(length // BLOCK):
+            columns = slice(b * BLOCK, (b + 1) * BLOCK)
+            total = functools.reduce(lambda p, q: p + q, [slots[i, 0:1, columns] for i in range(n)])
+            turned[...] = jnp.broadcast_to(finish(total), turned.shape)
+            out[columns, :] = turned[...].T
+
+    put_rows(row_slots)
+    get_x.drain()
+    get_bd.drain()
+    store_wxd.wait()
     for i in range(1, n):
         exchange(2, i).start()
-
     load_cot.wait()
+    store_xin.wait()
 
     def back_chip(k, source):
         get_out.arrived(k)
         part = pl.ds(pl.multiple_of((source // 2) * 2 * column_shard, 2 * column_shard), 2 * column_shard)
-        stores.start(wout.at[:, part], wout_o.at[:, part])
 
         def body(i, carry):
             at = pl.ds(pl.multiple_of(i * 512, 512), 512)
@@ -1002,158 +1021,87 @@
     get_out.second()
     for i in range(1, n):
         exchange(2, i).wait()
-    for b in range(length // BLOCK):
-        columns = slice(b * BLOCK, (b + 1) * BLOCK)
-        total = functools.reduce(lambda p, q: p + q, [row_slots[i, 0:1, columns] for i in range(n)])
-        turned[...] = jnp.broadcast_to(lax.rsqrt(total / (inner * n) + EPS), turned.shape)
-        inverse_out[columns, :] = turned[...].T
+    store_inverse.wait()
+    sum_rows(row_slots, inverse_out, lambda total: lax.rsqrt(total / (inner * n) + EPS))
     store_normed.wait()
     gn = normed.at[:, pl.ds(0, inner)]
-    scale_rows(gated, inverse_out, crow, gn)
-    stores.start(gn, gn_o)
-    stores.start(inverse_out, inverse_out_o)
+    gs = normed.at[:, pl.ds(inner, inner)]
+    gate_norm(gate, ssd, x_low, inverse_out, crow, gn)
     back_chip(1, ring.left)
     back_chip(2, ring.right)
     get_out.third()
     back_chip(3, ring.across)
-    stores.start(gnorm, gnorm_o)
     cross_sums(gnorm, gn, stat)
-    for b in range(length // BLOCK):
-        columns = slice(b * BLOCK, (b + 1) * BLOCK)
-        rows[:, columns] = stat[columns, :].T[:8]
-    for each in (get_x, get_bd, get_z, get_out):
-        each.drain()
-    for copy in stores.pairs:
-        if copy is not store_normed:
-            copy.wait()
-
-
-def output_kernel(
-    lengths, rows_own, tok, gn, wout, cot, gate, gnorm_o, x_low, ssd, states, slope, xin, bc_low, step, sgdt,
-    step_low, decay_low, inverse_out, taps, crow, dpar,
-    low_gate, low_xd, out, dwout_o, csums, dsums, sums,
-    v_gn, v_wout, v_cot, v_x, v_ssd, v_states, gs, v_slope, first_wide, second_wide, v_xd, dwout,
-    v_bc, v_step, v_sgdt, v_step_low, v_decay_low, v_inverse,
-    part, slots, cores, parts, wholes, row_slots, turned, stat,
-    pos, rpos, spread, dstate, xs, gx, cbm, acc,
-    load_sems, wout_sems, cot_sems, line_send, line_recv, core_send, core_recv, ring_send, ring_recv, mp_send, mp_recv,
-):
-    ring = Ring()
-    starts = [jnp.int32(0)]
-    for k in range(DOCS - 1):
-        starts.append(starts[-1] + lengths[0, k])
-    loads = Loads(load_sems)
-    n = lax.axis_size("mp")
-    z = lax.axis_index("mp")
-    length, inner = v_gn.shape
-    own = part.shape[1] // n
-    v_gate = first_wide.at[pl.ds(0, length), pl.ds(0, inner)]
-    gnorm = second_wide.at[pl.ds(0, length), pl.ds(0, inner)]
-    total = gx.at[:, pl.ds(0, own)]
-    line = Line(part, slots, (line_send, line_recv), total)
-
-    def wout_copy(i):
-        columns = line.columns(line.order(i))
-        return pltpu.make_async_copy(wout.at[:, columns], v_wout.at[:, columns], wout_sems.at[i])
-
-    load_gn = loads.start(gn, v_gn)
-    wout_copy(0).start()
-    row_slots[0] = rows_own[...]
-    greet(ring, False)
-
-    def exchange(i):
-        return remote(
-            row_slots.at[0], row_slots.at[i], mp_send.at[i - 1], mp_recv.at[i - 1], mp=(z + i) % n
-        )
-
+    put_rows(cross_slots)
     for i in range(1, n):
-        exchange(i).start()
-    chunk = v_cot.shape[2]
-    shard = dwout.shape[1]
-
-    def cot_copy(j):
-        return pltpu.make_async_copy(
-            cot.at[:, pl.ds(pl.multiple_of(j * chunk, chunk), chunk)], v_cot.at[j % 2], cot_sems.at[j % 2]
-        )
-
-    load_gn.wait()
-    for i in range(1, n):
-        wout_copy(i).start()
-    cot_copy(0).start()
-    early = [
-        loads.start(source, target)
-        for source, target in (
-            (gate, v_gate), (gnorm_o, gnorm), (x_low, v_x), (ssd, v_ssd), (inverse_out, v_inverse),
-        )
-    ]
-    later = [
-        loads.start(source, target)
-        for source, target in (
-            (states, v_states), (slope, v_slope), (bc_low, v_bc), (step, v_step), (sgdt, v_sgdt),
-            (step_low, v_step_low), (decay_low, v_decay_low),
-        )
-    ]
+        exchange(3, i).start()
+    get_z.drain()
+    store_wz.wait()
+
+    fold_columns = inner // own
+
+    def piece(t, q):
+        row = pl.multiple_of((q // fold_columns) * length + t * BLOCK, BLOCK)
+        return wz.at[pl.ds(row, BLOCK), pl.ds(pl.multiple_of((q % fold_columns) * own, own), own)]
+
+    def slot(side, place, k):
+        if place == 2:
+            return near.at[k]
+        row = pl.multiple_of((k // fold_columns) * BLOCK, BLOCK)
+        return wxd.at[pl.ds(row, BLOCK), pl.ds(pl.multiple_of((k % fold_columns) * own, own), own)]
+
+    total = wide.at[:, pl.ds(0, own)]
+    line = Line(piece, slot, length // BLOCK, (line_send, line_recv), total)
 
     def quarter(i, carry):
-        columns = line.columns(line.order(i))
-        wout_copy(i).wait()
+        q = line.order(i)
+        columns = pl.ds(pl.multiple_of(q * own, own), own)
         for r in range(0, length, 512):
-            part[r : r + 512, columns] = mm(v_gn[r : r + 512, :], v_wout[:, columns]).astype(bf16)
-
-        @pl.when(i == 0)
-        def _():
-            line.inject(0)
-            line.inject(1)
+            at = pl.ds(pl.multiple_of((q // fold_columns) * length + r, 512), 512)
+            cols = pl.ds(pl.multiple_of((q % fold_columns) * own, own), own)
+            wz[at, cols] = mm(gn[r : r + 512, :], wout[:, columns]).astype(bf16)
+            if r == 0:
+                @pl.when(i == 0)
+                def _():
+                    line.inject(0)
+                    line.inject(1)
 
         return carry
 
     lax.fori_loop(0, n, quarter, 0)
     line.inject(2)
-    grads = v_wout
+    get_out.drain()
+    grads = wout
     scatter = Scatter(
-        ring, lambda r: grads.at[:, pl.ds(pl.multiple_of(r * shard, shard), shard)], cores, parts, wholes,
-        (core_send, core_recv, ring_send, ring_recv),
-    )
+        ring, lambda r: grads.at[:, pl.ds(pl.multiple_of(r * column_shard, column_shard), column_shard)],
+        cores, parts, wholes, (scatter_core_send, scatter_core_recv, scatter_ring_send, scatter_ring_recv),
+    )
+    chunk = 2 * column_shard
 
     def weight(j, carry):
-        @pl.when(j < 3)
-        def _():
-            cot_copy(j + 1).start()
-
-        cot_copy(j).wait()
         columns = pl.ds(pl.multiple_of(j * chunk, chunk), chunk)
         for r in range(0, inner, 256):
-            grads[r : r + 256, columns] = mm_tn(v_gn[:, r : r + 256], v_cot[j % 2]).astype(bf16)
+            grads[r : r + 256, columns] = mm_tn(gn[:, r : r + 256], v_tok[:, columns]).astype(bf16)
         scatter.start(j)
         return carry
 
     lax.fori_loop(0, 4, weight, 0)
     line.inject(3)
     line.forward(0, 1)
-    v_tok, v_out = v_cot.at[0], v_cot.at[1]
-    load_tok = loads.start(tok.at[:, pl.ds(pl.multiple_of(z * own, own), own)], v_tok)
-    fill_spread(spread)
-    fill_positions(starts, pos, rpos)
-    for copy in early:
-        copy.wait()
+    xd = v_tok.at[:, pl.ds(0, wxd.shape[1])]
+    token_own = v_tok.at[:, pl.ds(wxd.shape[1], own)]
+    load_own = loads.start(tok.at[:, pl.ds(pl.multiple_of(z * own, own), own)], token_own)
     for i in range(1, n):
-        exchange(i).wait()
-    for b in range(length // BLOCK):
-        columns = slice(b * BLOCK, (b + 1) * BLOCK)
-        row = functools.reduce(lambda p, q: p + q, [row_slots[i, 0:1, columns] for i in range(n)])
-        turned[...] = jnp.broadcast_to(row / (inner * n), turned.shape)
-        stat[columns, :] = turned[...].T
-    gate_backward(
-        v_gate, v_ssd, v_x, gnorm, crow, stat, inner * n, None, v_gn, gs, sums, known=v_inverse
-    )
-    load_xin = loads.start(xin, second_wide)
-    store_gate = loads.start(v_gn, low_gate)
+        exchange(3, i).wait()
+    sum_rows(cross_slots, stat, lambda total: total / (inner * n))
+    low_gate = gn
+    gate_backward(gate, ssd, x_low, gnorm, crow, stat, inner * n, None, low_gate, gs, sums, known=inverse_out)
+    load_xin = loads.start(xin_o, xin)
+    stores.start(low_gate, low_gate_o)
     line.inject(4)
     line.forward(1, 1)
     line.forward(0, 2)
     scatter.first()
-    for copy in later:
-        copy.wait()
 
     def scan_tick(i):
         line.inject(i + 5)
@@ -1169,11 +1117,11 @@
 
     gpre = first_wide
     scan_backward(
-        starts, v_x, v_bc, v_step_low, v_decay_low, v_ssd, v_states, gs, v_slope, crow, v_step, v_sgdt, dpar,
-        gpre, v_xd, dsums, spread, dstate, xs, gx, cbm, acc, scan_tick,
-    )
-    scatter.finish(dwout)
-    store_dwout = loads.start(dwout, dwout_o)
+        starts, x_low, bc_low, step_low, decay_low, ssd, states, gs, slope, crow, dtin, None, dpar,
+        gpre, xd, dsums, spread, state, xs, wide, cbm, acc, scan_tick,
+    )
+    scatter.finish(stage_b)
+    stores.start(stage_b, dwout_o)
     load_xin.wait()
 
     def conv_tick(b):
@@ -1182,21 +1130,23 @@
             line.inject(9 + b // 2)
             line.forward(6 + b // 2, 1)
 
-    convolve_back(second_wide, gpre, taps, pos, rpos, v_xd, csums, conv_tick)
+    convolve_back(xin, gpre, taps, pos, rpos, xd, csums, conv_tick)
     line.inject(11)
-    store_xd = loads.start(v_xd, low_xd)
-    load_tok.wait()
+    stores.start(xd, low_xd_o)
+    load_own.wait()
+    out = x_low.at[:, pl.ds(0, own)]
 
     def last(t, carry):
         line.finish(t)
-        v_out[line.rows(t), :] = (v_tok[line.rows(t), :].astype(f32) + total[...]).astype(bf16)
+        out[line.rows(t), :] = (token_own[line.rows(t), :].astype(f32) + total[...]).astype(bf16)
         return carry
 
     lax.fori_loop(0, line.blocks, last, 0)
-    store_out = loads.start(v_out, out)
+    stores.start(out, out_o)
     line.drain()
-    for copy in (store_gate, store_dwout, store_xd, store_out):
-        copy.wait()
+    for copy in stores.pairs:
+        if not any(copy is done for done in (store_normed, store_inverse, store_xin, store_wxd, store_wz)):
+            copy.wait()
 
 
 def input_kernel(
@@ -1221,10 +1171,17 @@
     heads, per = dwdt.shape[0], dwbc.shape[0]
     own = features // n
     own_columns = pl.ds(pl.multiple_of(z * own, own), own)
-    line = Line(part, slots, (line_send, line_recv), total)
+
+    def quarter_columns(q):
+        return pl.ds(pl.multiple_of(q * own, own), own)
+
+    line = Line(
+        lambda t, q: part.at[pl.ds(pl.multiple_of(t * BLOCK, BLOCK), BLOCK), quarter_columns(q)],
+        lambda side, place, k: slots.at[side, k], length // BLOCK, (line_send, line_recv), total,
+    )
 
     def quarter_loads(i):
-        columns = line.columns(line.order(i))
+        columns = quarter_columns(line.order(i))
         return [
             pltpu.make_async_copy(source, target, quarter_sems.at[i, k])
             for k, (source, target) in enumerate((
@@ -1250,13 +1207,18 @@
     ]
 
     def quarter(i, carry):
-        columns = line.columns(line.order(i))
+        columns = quarter_columns(line.order(i))
         for copy in quarter_loads(i):
             copy.wait()
         for r in range(0, length, 256):
             rows = slice(r, r + 256)
             here = mm_nt(v_gate[rows, :], v_wz[columns, :]) + mm_nt(v_xd[rows, :], v_wxd[columns, :])
             part[rows, columns] = here.astype(bf16)
+            if r < 512:
+                @pl.when(i == 0)
+                def _():
+                    line.inject(r // 256)
+
             along = here * (v_tok[rows, columns].astype(f32) * inverse[rows, :1])
             folded = fold(along)
             if r == 0:
@@ -1269,12 +1231,7 @@
                 sum_lanes = sum_lanes + along[:, c : c + LANES]
             rowacc[rows, :] += sum_lanes
 
-        @pl.when(i == 0)
-        def _():
-            line.inject(0)
-            line.inject(1)
-
-        @pl.when(i == 2)
+        @pl.when(i == 1)
         def _():
             line.inject(2)
 
@@ -1389,16 +1346,8 @@
     store_z = loads.start(dwz, dwz_o)
     line.inject(9)
     line.forward(6, 1)
-    for i in range(1, n):
-        rows_copy(i).wait()
-    rows_own[...] += functools.reduce(lambda a, b: a + b, [rows_in[i] for i in range(n - 1)])
     line.inject(10)
     line.forward(7, 1)
-    for i in range(1, n):
-        bc_copy(i).wait()
-        gain_copy(i).wait()
-    smalls[0:8, inner:] += functools.reduce(lambda a, b: a + b, [bc_in[i] for i in range(n - 1)])
-    smalls[8:16, :inner] += functools.reduce(lambda a, b: a + b, [gain_in[i] for i in range(n - 1)])
     line.inject(11)
     x_scatter.finish(dwxd)
     share = LANES // per
@@ -1419,6 +1368,13 @@
 
     for i in range(1, n):
         weight_copy(i).start()
+    for i in range(1, n):
+        rows_copy(i).wait()
+        bc_copy(i).wait()
+        gain_copy(i).wait()
+    rows_own[...] += functools.reduce(lambda a, b: a + b, [rows_in[i] for i in range(n - 1)])
+    smalls[0:8, inner:] += functools.reduce(lambda a, b: a + b, [bc_in[i] for i in range(n - 1)])
+    smalls[8:16, :inner] += functools.reduce(lambda a, b: a + b, [gain_in[i] for i in range(n - 1)])
     store_x = loads.start(dwxd.at[:, pl.ds(0, inner)], dwx_o)
     dwdt[...] = dwxd[:, width:].T[:heads]
     lanes = pl.ds(pl.multiple_of(inner + (z // share) * LANES, LANES), LANES)
@@ -1434,10 +1390,6 @@
     a_rate[...] = smalls[7:8, LANES : LANES + heads]
     fits = inner // own
     in_gain[...] = smalls[pl.ds(8 + z // fits, 1), pl.ds(pl.multiple_of((z % fits) * own, own), own)]
-    for i in range(1, n):
-        weight_copy(i).wait()
-    here = functools.reduce(lambda a, b: a + b, [bc_slots[i].astype(f32) for i in range(n - 1)], dwxd[:, lanes])
-    dwbc[...] = mine(here).T[:per]
     later[1].wait()
 
     def last(t, carry):
@@ -1452,6 +1404,10 @@
         return carry
 
     lax.fori_loop(0, line.blocks, last, 0)
+    for i in range(1, n):
+        weight_copy(i).wait()
+    here = functools.reduce(lambda a, b: a + b, [bc_slots[i].astype(f32) for i in range(n - 1)], dwxd[:, lanes])
+    dwbc[...] = mine(here).T[:per]
     line.drain()
     store_z.wait()
     store_x.wait()
@@ -1634,63 +1590,36 @@
         return v[None, :]
 
     (
-        normed, xin, slope, x_low, ssd, states, wxd, wz, wout, gn, gate, gnorm,
-        bc_low, step, sgdt, step_low, decay_low, inverse, inverse_out, taps, crow, dpar, rows,
+        normed, _, wxd, wz, low_gate, low_xd, output, w_out_grad, inverse, csums, dsums, sums,
     ) = call(
-        gather_kernel,
+        trunk_kernel,
         [
-            ((T, D), bf16), ((T + 8, width), f32), ((T, width), bf16), ((T, inner), bf16), ((T, inner), bf16),
-            ((blocks, STATE, inner), bf16), ((D, wide), bf16), ((D, inner), bf16), ((inner, D), bf16),
-            ((T, inner), bf16), ((T, inner), f32), ((T, inner), f32),
-            ((T, pair), bf16), ((T, LANES), f32), ((T, LANES), f32), ((T, LANES), bf16), ((T, LANES), bf16),
-            ((T, LANES), f32), ((T, LANES), f32),
-            ((8, width), f32), ((8, inner), f32), ((8, LANES), f32), ((8, T), f32),
+            ((T, D), bf16), ((T + 8, width), f32), ((D, wide), bf16), ((D, inner), bf16), ((T, inner), bf16),
+            ((T, wide), bf16), ((T, own), bf16), ((inner, columns), f32), ((T, LANES), f32),
+            ((8 * CONV + 8, width), f32), ((16, LANES), f32), ((16, inner), f32),
         ],
         [
-            ((T, D), bf16), ((shard, inner), f32), ((inner, columns), f32), ((T, D), bf16), ((T + 8, width), f32),
-            ((T, width), bf16), ((T, inner), bf16), ((T, inner), bf16), ((blocks, STATE, inner), bf16),
-            ((D, wide), bf16), ((D, inner), bf16), ((inner, D), bf16), ((T, inner), f32), ((T, inner), f32),
-            ((T, inner), f32),
-            ((T, pair), bf16), ((T, LANES), f32), ((T, LANES), f32), ((T, LANES), bf16), ((T, LANES), bf16),
-            ((T, LANES), f32), ((T, LANES), f32),
-            ((group, shard, LANES), bf16), ((group, 8, LANES), f32), ((group, 8, T), f32),
+            ((T, D), bf16), ((inner, columns), f32), ((T, D), bf16), ((T + 8, width), f32),
+            ((T + 8, width), f32), ((T, width), bf16), ((T, inner), bf16), ((T, inner), bf16),
+            ((blocks, STATE, inner), bf16), ((D, wide), bf16), ((D, inner), bf16), ((inner, D), bf16),
+            ((T, pair), bf16), ((T, LANES), bf16), ((T, LANES), bf16), ((T, LANES), f32),
+            ((8, width), f32), ((8, inner), f32), ((8, LANES), f32),
+            ((group, shard, LANES), bf16), ((group, 8, LANES), f32), ((group, 8, T), f32), ((group, 8, T), f32),
             ((T, LANES), f32), ((LANES, BLOCK), f32),
-            ((T, LANES), jnp.int32), ((LANES, inner), bf16), ((T, LANES), f32), ((STATE, inner), f32),
-            ((BLOCK, inner), bf16), ((BLOCK, inner), f32), ((BLOCK, BLOCK), f32),
+            ((T, LANES), jnp.int32), ((T, LANES), jnp.int32), ((LANES, inner), bf16), ((T, LANES), f32),
+            ((STATE, inner), f32), ((BLOCK, inner), bf16), ((BLOCK, inner), f32), ((BLOCK, BLOCK), f32),
+            ((BLOCK, BLOCK), f32), ((2 * blocks, BLOCK, own), bf16),
+            ((4, inner, columns), bf16), ((2, inner // 2, columns), bf16), ((2, inner, columns), bf16),
         ],
         0, doc_lengths, tokens, cotangent, w_x, w_z, w_out, w_bc.T, w_dt.T, conv_x, row(conv_x_bias), conv_bc,
         row(conv_bc_bias), row(dt_bias), row(a_rate), row(d_skip), row(input_norm_gain), row(out_gain),
         places="s" + "a" * 5 + "v" * 11,
-        sems=[(5,), (23,), (4, 4), (4, 4), (4, 4), (4, 4), (3 * group - 3,), (3 * group - 3,)],
+        sems=[
+            (7,), (9,), (4, 4), (4, 4), (4, 4), (4, 4), (4 * group - 4,), (4 * group - 4,),
+            (2, messages), (2, messages), (4,), (4,), (4,), (4,),
+        ],
         collective=0,
-        far=19,
-    )
-    low_gate, low_xd, output, w_out_grad, csums, dsums, sums = call(
-        output_kernel,
-        [
-            ((T, inner), bf16), ((T, wide), bf16),
-            ((T, own), bf16), ((inner, columns), f32), ((8 * CONV + 8, width), f32), ((16, LANES), f32),
-            ((16, inner), f32),
-        ],
-        [
-            ((T, inner), bf16), ((inner, D), bf16), ((2, T, 2 * columns), bf16), ((T, inner), bf16),
-            ((T, inner), bf16), ((blocks, STATE, inner), bf16), ((T, inner), bf16), ((T, width), bf16),
-            ((T + 8, width), f32), ((T + 8, width), f32), ((T, wide), bf16), ((inner, columns), f32),
-            ((T, pair), bf16), ((T, LANES), f32), ((T, LANES), f32), ((T, LANES), bf16), ((T, LANES), bf16),
-            ((T, LANES), f32),
-            ((T, D), bf16), ((2, messages, BLOCK, own), bf16),
-            ((4, inner, columns), bf16), ((2, inner // 2, columns), bf16), ((2, inner, columns), bf16),
-            ((group, 8, T), f32), ((LANES, BLOCK), f32), ((T, LANES), f32),
-            ((T, LANES), jnp.int32), ((T, LANES), jnp.int32), ((LANES, inner), bf16),
-            ((STATE, inner), f32), ((BLOCK, inner), bf16), ((BLOCK, inner), f32), ((BLOCK, BLOCK), f32),
-            ((BLOCK, BLOCK), f32),
-        ],
-        0, doc_lengths, rows, tokens, gn, wout, cotangent, gate, gnorm, x_low, ssd, states, slope, xin, bc_low,
-        step, sgdt, step_low, decay_low, inverse_out, taps, crow, dpar,
-        places="sv" + "a" * 17 + "v" * 3,
-        sems=[(19,), (group,), (2,), (2, messages), (2, messages), (4,), (4,), (4,), (4,), (group - 1,), (group - 1,)],
-        collective=1,
-        far=4,
+        far=9,
     )
     w_z_grad, w_x_grad, input_grad, w_bc_grad, w_dt_grad, *small_grads = call(
         input_kernel,

time: 247 us -> 240 us (0.972)
  Pallas kernels: 246 us -> 239 us
    pallas_call x4 -> x3, Pallas kernels: 246 us -> 239 us  [call(): pl.pallas_call(kernel, out_shape=[jax.ShapeDtypeStruct(shape, kind) for s...]
where the time goes in v5:
time: 240 us
  Pallas kernels  239 us (100%)
    pallas_call x3, Pallas kernels, call(): pl.pallas_call(kernel, out_shape=[jax.ShapeDtypeStruct(shape, kind) for s...  239 us

profile of v5, /device:TPU:0, one launch (start us, length us, event | category | flops | bytes accessed | tf_op | source)
XLA Modules:
  0.0 240.1 jit_solution(3854865677362124274)
XLA Ops:
  0.7 147.1 %shard_map.288 = (bf16[1024,2048]{1,0:T(8,128)(2,1)}, f32[1032,1280]{1,0:T(8,128)}, bf16[2048,1408]{1,0:T(8,128)(2,1)}, bf16[2048,1024]{1,0:T(8,128)(2,1)}, bf16...) custom-call(s32[1,5]{1,0:T(1,128)} %lengths.1, ...), custom_call_target="tpu_custom_call" | custom-call | tf_op jit(solution)/shard_map/pallas_call | solution.py:1444
  147.8 87.4 %shard_map.289 = (f32[256,1024]{1,0:T(8,128)}, f32[256,1024]{1,0:T(8,128)}, bf16[1024,512]{1,0:T(8,128)(2,1)}, f32[64,256]{1,0:T(8,128)}, f32[16,256]{1,0:T(8,12...) custom-call(bf16[1024,2048]{1,0:T(8,128)(2,1)} %tok.3, ...), custom_call_target="tpu_custom_call" | custom-call | tf_op jit(solution)/shard_map/pallas_call | solution.py:1444
  235.1 4.7 %shard_map.290 = (bf16[1024,512]{1,0:T(8,128)(2,1)}, bf16[1024,512]{1,0:T(8,128)(2,1)}, f32[256,1024]{1,0:T(8,128)}, f32[256,1024]{1,0:T(8,128)}, f32[64,256]{1,...) custom-call(bf16[1024,512]{1,0:T(8,128)(2,1)} %get-tuple-element.57., ...), custom_call_target="tpu_custom_call" | custom-call | tf_op jit(solution)/shard_map/pallas_call | solution.py:1444

commit v6 on v5

--- a/solution.py
+++ b/solution.py
@@ -306,7 +306,7 @@
             mixed = ssd[rows, cols].astype(f32) + crow[1:2, cols] * x_low[rows, cols].astype(f32)
             value = mixed * (g * logistic(g))
             squares = squares + value * value
-        stat[rows, :] = jnp.broadcast_to(jnp.sum(squares, axis=1, keepdims=True), (step, LANES))
+        stat[rows, :] = squares[:, :LANES] + squares[:, LANES:]
         return carry
 
     lax.fori_loop(0, gate.shape[0] // step, body, 0)
@@ -337,7 +337,7 @@
         for c in range(0, inner, 256):
             cols = slice(c, c + 256)
             total = total + gnorm[rows, cols] * gn[rows, cols].astype(f32)
-        stat[rows, :] = jnp.broadcast_to(jnp.sum(total, axis=1, keepdims=True), (step, LANES))
+        stat[rows, :] = total[:, :LANES] + total[:, LANES:]
         return carry
 
     lax.fori_loop(0, gn.shape[0] // step, body, 0)
@@ -603,7 +603,7 @@
         pl.semaphore_signal(barrier, inc=1, device_id={"dp": other}, device_id_type=MESH)
     for i in range(1, n):
         pl.semaphore_signal(barrier, inc=1, device_id={"mp": (z + i) % n}, device_id_type=MESH)
-    pl.semaphore_wait(barrier, len(close) + n - 1)
+    return lambda: pl.semaphore_wait(barrier, len(close) + n - 1)
 
 
 class Scatter:
@@ -677,8 +677,8 @@
 
 
 class Line:
-    def __init__(self, piece, slot, blocks, sems, total):
-        self.piece, self.slot, self.blocks, self.total = piece, slot, blocks, total
+    def __init__(self, piece, slot, blocks, sems, total, depth):
+        self.piece, self.slot, self.blocks, self.total, self.depth = piece, slot, blocks, total, depth
         self.send, self.recv = sems
         self.n, self.z = lax.axis_size("mp"), lax.axis_index("mp")
         self.place = (self.z, self.n - 1 - self.z)
@@ -705,9 +705,9 @@
         for side in range(2):
             @pl.when(self.place[side] == 0)
             def _():
-                @pl.when(jnp.int32(k) >= 2)
+                @pl.when(jnp.int32(k) >= self.depth)
                 def _():
-                    self.copy(side, 0, jnp.maximum(k - 2, 0)).wait_send()
+                    self.copy(side, 0, jnp.maximum(k - self.depth, 0)).wait_send()
 
                 self.copy(side, 0, k).start()
 
@@ -737,7 +737,7 @@
                         self.copy(side, place, k).wait_send()
                         return carry
 
-                    lax.fori_loop(count - 2 if place == 0 else 0, count, body, 0)
+                    lax.fori_loop(count - self.depth if place == 0 else 0, count, body, 0)
 
     def order(self, i):
         z = self.z
@@ -824,18 +824,20 @@
 def trunk_kernel(
     lengths, tok, cot, w_x, w_z, w_out, w_bc, w_dt, conv_x, conv_x_bias, conv_bc, conv_bc_bias, dt_bias, a_rate,
     d_skip, gain, out_gain,
-    normed_o, xin_o, wxd_o, wz_o, low_gate_o, low_xd_o, out_o, dwout_o, inverse_o,
-    csums, dsums, sums,
-    v_tok, stage_b, normed, xin, first_wide, slope, x_low, ssd, states, wxd, wz, wout,
+    normed_o, xin_o, wxd_o, wz_o, low_gate_o, low_xd_o, out_o, dwout_o, inverse_o, part_o,
+    csums, dsums, sums, rows_o, colacc,
+    v_tok, stage_b, normed, xin, first_wide, slope, both, states, wxd, wz, wout,
     bc_low, step_low, decay_low, inverse_out, taps, crow, dpar,
     bc_slots, tap_slots, row_slots, cross_slots, stat, turned,
     pos, rpos, spread, dtin, state, xs, wide, cbm, acc, near, cores, parts, wholes,
-    load_sems, store_sems, ring_send, ring_recv, core_send, core_recv, mp_send, mp_recv, line_send, line_recv,
+    load_sems, store_sems, token_sems, part_sems, ring_send, ring_recv, core_send, core_recv, mp_send, mp_recv, line_send, line_recv,
     scatter_core_send, scatter_core_recv, scatter_ring_send, scatter_ring_recv,
 ):
     ring = Ring()
+    met = greet(ring, False)
     n, z = lax.axis_size("mp"), lax.axis_index("mp")
     length, features = normed.shape
+    x_low, ssd = both.at[pl.ds(0, length), :], both.at[pl.ds(length, length), :]
     stage_a = wide
     inverse = inverse_out
     inner, width = x_low.shape[1], xin.shape[1]
@@ -850,6 +852,30 @@
     for k in range(DOCS - 1):
         starts.append(starts[-1] + lengths[0, k])
 
+    def exchange(k, i):
+        slots = (bc_slots, tap_slots, row_slots, cross_slots)[k]
+        at = k * (n - 1) + i - 1
+        return remote(slots.at[0], slots.at[i], mp_send.at[at], mp_recv.at[at], mp=(z + i) % n)
+
+    def rows_of(ref, low, high):
+        def shard_of(r):
+            return ref.at[pl.ds(pl.multiple_of(r * shard, shard), shard), pl.ds(low, high - low)]
+
+        return shard_of
+
+    def columns_of(r):
+        return wout.at[:, pl.ds(pl.multiple_of(r * column_shard, column_shard), column_shard)]
+
+    sems = [tuple(group.at[k] for group in (ring_send, ring_recv, core_send, core_recv)) for k in range(4)]
+    get_x = Gather(ring, rows_of(wxd, 0, inner), shard, sems[0])
+    get_bd = Gather(ring, rows_of(wxd, inner, wxd.shape[1]), shard, sems[1])
+    get_z = Gather(ring, rows_of(wz, 0, inner), shard, sems[2])
+    get_out = Gather(ring, columns_of, inner, sems[3])
+
+    load_x.wait()
+    cast_into(get_x.shard(ring.me), stage_a)
+    met()
+    get_x.start()
     turned[...] = jnp.zeros_like(turned)
     turned[:per, :] = w_bc[...]
     bc_slots[0] = turned[...].T.astype(bf16)
@@ -864,32 +890,6 @@
     dpar[0:1, :heads] = dt_bias[...]
     dpar[1:2, :heads] = a_rate[...]
     dpar[2:3, :heads] = d_skip[...]
-
-    greet(ring, False)
-
-    def exchange(k, i):
-        slots = (bc_slots, tap_slots, row_slots, cross_slots)[k]
-        at = k * (n - 1) + i - 1
-        return remote(slots.at[0], slots.at[i], mp_send.at[at], mp_recv.at[at], mp=(z + i) % n)
-
-    def rows_of(ref, low, high):
-        def shard_of(r):
-            return ref.at[pl.ds(pl.multiple_of(r * shard, shard), shard), pl.ds(low, high - low)]
-
-        return shard_of
-
-    def columns_of(r):
-        return wout.at[:, pl.ds(pl.multiple_of(r * column_shard, column_shard), column_shard)]
-
-    sems = [tuple(group.at[k] for group in (ring_send, ring_recv, core_send, core_recv)) for k in range(4)]
-    get_x = Gather(ring, rows_of(wxd, 0, inner), shard, sems[0])
-    get_bd = Gather(ring, rows_of(wxd, inner, wxd.shape[1]), shard, sems[1])
-    get_z = Gather(ring, rows_of(wz, 0, inner), shard, sems[2])
-    get_out = Gather(ring, columns_of, inner, sems[3])
-
-    load_x.wait()
-    cast_into(get_x.shard(ring.me), stage_a)
-    get_x.start()
     for k in range(2):
         for i in range(1, n):
             exchange(k, i).start()
@@ -979,19 +979,22 @@
     store_wz = stores.start(wz, wz_o)
     gate_squares(gate, ssd, x_low, crow, stat)
 
-    def put_rows(slots):
+    def put_rows(target):
         for b in range(length // BLOCK):
-            columns = slice(b * BLOCK, (b + 1) * BLOCK)
-            slots[0, :, columns] = stat[columns, :].T[:8]
+            line_sum = jnp.sum(stat[b * BLOCK : (b + 1) * BLOCK, :].T, axis=0, keepdims=True)
+            for j in range(BLOCK // LANES):
+                at = b * (BLOCK // LANES) + j
+                target[at : at + 1, :] = line_sum[:, j * LANES : (j + 1) * LANES]
 
     def sum_rows(slots, out, finish):
+        sums_here = finish(functools.reduce(lambda p, q: p + q, [slots[i] for i in range(n)]))
         for b in range(length // BLOCK):
-            columns = slice(b * BLOCK, (b + 1) * BLOCK)
-            total = functools.reduce(lambda p, q: p + q, [slots[i, 0:1, columns] for i in range(n)])
-            turned[...] = jnp.broadcast_to(finish(total), turned.shape)
-            out[columns, :] = turned[...].T
-
-    put_rows(row_slots)
+            at = b * (BLOCK // LANES)
+            row = jnp.concatenate([sums_here[at + j : at + j + 1] for j in range(BLOCK // LANES)], axis=1)
+            turned[...] = jnp.broadcast_to(row, turned.shape)
+            out[b * BLOCK : (b + 1) * BLOCK, :] = turned[...].T
+
+    put_rows(row_slots.at[0])
     get_x.drain()
     get_bd.drain()
     store_wxd.wait()
@@ -1017,22 +1020,22 @@
 
         lax.fori_loop(0, length // 512, body, 0)
 
+    get_out.second()
     back_chip(0, ring.me)
-    get_out.second()
+    back_chip(1, ring.left)
+    back_chip(2, ring.right)
     for i in range(1, n):
         exchange(2, i).wait()
     store_inverse.wait()
     sum_rows(row_slots, inverse_out, lambda total: lax.rsqrt(total / (inner * n) + EPS))
+    get_out.third()
     store_normed.wait()
     gn = normed.at[:, pl.ds(0, inner)]
     gs = normed.at[:, pl.ds(inner, inner)]
     gate_norm(gate, ssd, x_low, inverse_out, crow, gn)
-    back_chip(1, ring.left)
-    back_chip(2, ring.right)
-    get_out.third()
     back_chip(3, ring.across)
     cross_sums(gnorm, gn, stat)
-    put_rows(cross_slots)
+    put_rows(cross_slots.at[0])
     for i in range(1, n):
         exchange(3, i).start()
     get_z.drain()
@@ -1051,7 +1054,7 @@
         return wxd.at[pl.ds(row, BLOCK), pl.ds(pl.multiple_of((k % fold_columns) * own, own), own)]
 
     total = wide.at[:, pl.ds(0, own)]
-    line = Line(piece, slot, length // BLOCK, (line_send, line_recv), total)
+    line = Line(piece, slot, length // BLOCK, (line_send, line_recv), total, 4)
 
     def quarter(i, carry):
         q = line.order(i)
@@ -1070,6 +1073,7 @@
 
     lax.fori_loop(0, n, quarter, 0)
     line.inject(2)
+    line.inject(3)
     get_out.drain()
     grads = wout
     scatter = Scatter(
@@ -1086,7 +1090,7 @@
         return carry
 
     lax.fori_loop(0, 4, weight, 0)
-    line.inject(3)
+    line.inject(4)
     line.forward(0, 1)
     xd = v_tok.at[:, pl.ds(0, wxd.shape[1])]
     token_own = v_tok.at[:, pl.ds(wxd.shape[1], own)]
@@ -1098,7 +1102,6 @@
     gate_backward(gate, ssd, x_low, gnorm, crow, stat, inner * n, None, low_gate, gs, sums, known=inverse_out)
     load_xin = loads.start(xin_o, xin)
     stores.start(low_gate, low_gate_o)
-    line.inject(4)
     line.forward(1, 1)
     line.forward(0, 2)
     scatter.first()
@@ -1120,8 +1123,30 @@
         starts, x_low, bc_low, step_low, decay_low, ssd, states, gs, slope, crow, dtin, None, dpar,
         gpre, xd, dsums, spread, state, xs, wide, cbm, acc, scan_tick,
     )
+    bd = wxd.shape[1] - inner
+    weight_loads = [loads.start(wz_o, both)]
+    for h in range(2):
+        rows_here = pl.ds(h * length, length)
+        weight_loads.append(
+            loads.start(wxd_o.at[rows_here, pl.ds(inner, bd)], slope.at[:, pl.ds(h * bd, bd)])
+        )
+    inverse_in = dtin
+    weight_loads.append(loads.start(inverse_o, inverse_in))
+
+    def token_copy(i):
+        return pltpu.make_async_copy(
+            tok.at[:, pl.ds(pl.multiple_of(line.order(i) * own, own), own)],
+            normed.at[:, pl.ds(pl.multiple_of(inner + (i % 2) * own, own), own)], token_sems.at[i],
+        )
+
+    token_copy(0).start()
+    token_copy(1).start()
     scatter.finish(stage_b)
     stores.start(stage_b, dwout_o)
+    for h in range(2):
+        weight_loads.append(
+            loads.start(wxd_o.at[pl.ds(h * length, length), pl.ds(0, inner)], wout.at[:, pl.ds(h * inner, inner)])
+        )
     load_xin.wait()
 
     def conv_tick(b):
@@ -1131,95 +1156,41 @@
             line.forward(6 + b // 2, 1)
 
     convolve_back(xin, gpre, taps, pos, rpos, xd, csums, conv_tick)
-    line.inject(11)
     stores.start(xd, low_xd_o)
-    load_own.wait()
-    out = x_low.at[:, pl.ds(0, own)]
-
-    def last(t, carry):
-        line.finish(t)
-        out[line.rows(t), :] = (token_own[line.rows(t), :].astype(f32) + total[...]).astype(bf16)
-        return carry
-
-    lax.fori_loop(0, line.blocks, last, 0)
-    stores.start(out, out_o)
-    line.drain()
-    for copy in stores.pairs:
-        if not any(copy is done for done in (store_normed, store_inverse, store_xin, store_wxd, store_wz)):
-            copy.wait()
-
-
-def input_kernel(
-    tok, inverse, gain, normed, low_gate, low_xd, wz, wxd, cot, csums, sums, dsums,
-    dwz_o, dwx_o, grad, dwbc, dwdt, conv_x, conv_x_bias, conv_bc, conv_bc_bias, dt_bias, a_rate, d_skip, in_gain, out_gain,
-    dwz, dwxd, smalls, spread, bc_own, bc_slots,
-    v_tok, v_normed, v_gate, v_xd, v_wz, v_wxd, v_cot,
-    part, slots, total, z_grads, z_cores, z_parts, z_wholes, x_grads, x_cores, x_parts, x_wholes,
-    rowacc, rows_own, rows_in, colacc, dp_in, bc_in, gain_in,
-    load_sems, quarter_sems, line_send, line_recv, z_core_send, z_core_recv, z_ring_send, z_ring_recv,
-    x_core_send, x_core_recv, x_ring_send, x_ring_recv,
-    rows_send, rows_recv, dp_send, dp_recv, mp_send, mp_recv, bc_send, bc_recv,
-):
-    ring = Ring()
-    loads = Loads(load_sems)
-    n = lax.axis_size("mp")
-    z = lax.axis_index("mp")
-    size = lax.axis_size("dp")
-    length, features = part.shape
-    inner = v_gate.shape[1]
-    width = smalls.shape[1]
-    heads, per = dwdt.shape[0], dwbc.shape[0]
-    own = features // n
-    own_columns = pl.ds(pl.multiple_of(z * own, own), own)
-
-    def quarter_columns(q):
-        return pl.ds(pl.multiple_of(q * own, own), own)
-
-    line = Line(
-        lambda t, q: part.at[pl.ds(pl.multiple_of(t * BLOCK, BLOCK), BLOCK), quarter_columns(q)],
-        lambda side, place, k: slots.at[side, k], length // BLOCK, (line_send, line_recv), total,
-    )
-
-    def quarter_loads(i):
-        columns = quarter_columns(line.order(i))
-        return [
-            pltpu.make_async_copy(source, target, quarter_sems.at[i, k])
-            for k, (source, target) in enumerate((
-                (wz.at[columns, :], v_wz.at[columns, :]),
-                (wxd.at[columns, :], v_wxd.at[columns, :]),
-                (tok.at[:, columns], v_tok.at[:, columns]),
-            ))
-        ]
-
-    first = [loads.start(source, target) for source, target in ((low_gate, v_gate), (low_xd, v_xd))]
-    for copy in quarter_loads(0):
-        copy.start()
-    greet(ring, True)
-    rowacc[...] = jnp.zeros_like(rowacc)
-    for copy in first:
+    for copy in weight_loads:
         copy.wait()
-    for i in range(1, n):
-        for copy in quarter_loads(i):
-            copy.start()
-    later = [
-        loads.start(source, target)
-        for source, target in ((normed, v_normed), (cot.at[:, own_columns], v_cot))
-    ]
-
-    def quarter(i, carry):
-        columns = quarter_columns(line.order(i))
-        for copy in quarter_loads(i):
-            copy.wait()
+    stat[...] = jnp.zeros_like(stat)
+    half = own // 2
+
+    def part_copy(i, h):
+        column = pl.multiple_of(line.order(i) * own + h * half, half)
+        return pltpu.make_async_copy(
+            cores.at[(i % 2) * 2 + h], part_o.at[:, pl.ds(column, half)], part_sems.at[i, h]
+        )
+
+    def grad_quarter(i, carry):
+        q = line.order(i)
+        columns = pl.ds(pl.multiple_of(q * own, own), own)
+        low = pl.ds(pl.multiple_of((q % 2) * own, own), own)
+        high = q // 2
+        x_columns = pl.ds(pl.multiple_of(high * inner, inner), inner)
+        bd_columns = pl.ds(pl.multiple_of(high * bd, LANES), bd)
+        token_columns = pl.ds(pl.multiple_of(inner + (i % 2) * own, own), own)
+        token_copy(i).wait()
+
+        @pl.when(i >= 2)
+        def _():
+            for h in range(2):
+                part_copy(jnp.maximum(i - 2, 0), h).wait()
+
         for r in range(0, length, 256):
             rows = slice(r, r + 256)
-            here = mm_nt(v_gate[rows, :], v_wz[columns, :]) + mm_nt(v_xd[rows, :], v_wxd[columns, :])
-            part[rows, columns] = here.astype(bf16)
-            if r < 512:
-                @pl.when(i == 0)
-                def _():
-                    line.inject(r // 256)
-
-            along = here * (v_tok[rows, columns].astype(f32) * inverse[rows, :1])
+            here = mm_nt(low_gate[rows, :], both[columns, :])
+            here = here + mm_nt(xd[rows, :inner], wout[low, x_columns])
+            here = here + mm_nt(xd[rows, inner:], slope[low, bd_columns])
+            for h in range(2):
+                cores[(i % 2) * 2 + h, rows, :] = here[:, h * half : (h + 1) * half].astype(bf16)
+            along = here * (normed[rows, token_columns].astype(f32) * inverse_in[rows, :1])
             folded = fold(along)
             if r == 0:
                 colacc[:, columns] = folded
@@ -1229,59 +1200,137 @@
             sum_lanes = along[:, :LANES]
             for c in range(LANES, own, LANES):
                 sum_lanes = sum_lanes + along[:, c : c + LANES]
-            rowacc[rows, :] += sum_lanes
-
-        @pl.when(i == 1)
+            stat[rows, :] += sum_lanes
+        for h in range(2):
+            part_copy(i, h).start()
+
+        @pl.when(i < 2)
         def _():
-            line.inject(2)
-
-        return carry
-
-    lax.fori_loop(0, n, quarter, 0)
-    line.inject(3)
-    line.forward(0, 1)
-
-    for b in range(length // BLOCK):
-        columns = slice(b * BLOCK, (b + 1) * BLOCK)
-        line_sum = jnp.sum(rowacc[columns, :].T, axis=0, keepdims=True)
-        rows_own[:, columns] = jnp.broadcast_to(line_sum, (8, BLOCK))
+            token_copy(jnp.minimum(i + 2, n - 1)).start()
+
+        @pl.when(i == 0)
+        def _():
+            line.inject(11)
+
+        return carry
+
+    lax.fori_loop(0, n, grad_quarter, 0)
+    put_rows(rows_o)
+    load_own.wait()
+
+    def last(t, carry):
+        line.finish(t)
+        value = (token_own[line.rows(t), :].astype(f32) + total[...]).astype(bf16)
+        for h in range(2):
+            wholes[h, line.rows(t), :] = value[:, h * half : (h + 1) * half]
+        return carry
+
+    lax.fori_loop(0, line.blocks, last, 0)
+    for h in range(2):
+        stores.start(wholes.at[h], out_o.at[:, pl.ds(h * half, half)])
+    line.drain()
+    for i in range(2, n):
+        for h in range(2):
+            part_copy(i, h).wait()
+    for copy in stores.pairs:
+        if not any(copy is done for done in (store_normed, store_inverse, store_xin, store_wxd, store_wz)):
+            copy.wait()
+
+
+def input_kernel(
+    tok, inverse, gain, normed, low_gate, low_xd, part_o, cot, rows_o, colacc, csums, sums, dsums,
+    dwz_o, dwx_o, grad_o, dwbc, dwdt, conv_x, conv_x_bias, conv_bc, conv_bc_bias, dt_bias, a_rate, d_skip, in_gain,
+    out_gain,
+    dwz, dwxd, grad, smalls, spread, bc_turned, bc_own, bc_slots,
+    v_inverse, v_normed, v_gate, v_xd, v_cot, v_tok, v_colacc, v_csums, v_sums, v_dsums,
+    part, slots, total, z_grads, z_cores, z_parts, z_wholes, x_grads, x_cores, x_parts, x_wholes,
+    rows_slots, dp_in, mp_in, turned,
+    load_sems, part_sems, line_send, line_recv, z_core_send, z_core_recv, z_ring_send, z_ring_recv,
+    x_core_send, x_core_recv, x_ring_send, x_ring_recv,
+    rows_send, rows_recv, dp_send, dp_recv, mp_send, mp_recv, bc_send, bc_recv,
+):
+    ring = Ring()
+    met = greet(ring, True)
+    loads = Loads(load_sems)
+    n = lax.axis_size("mp")
+    z = lax.axis_index("mp")
+    size = lax.axis_size("dp")
+    length, features = part.shape
+    inner = v_gate.shape[1]
+    width = v_csums.shape[1]
+    heads, per = dwdt.shape[0], dwbc.shape[0]
+    own = features // n
+
+    def quarter_columns(q):
+        return pl.ds(pl.multiple_of(q * own, own), own)
+
+    line = Line(
+        lambda t, q: part.at[pl.ds(pl.multiple_of(t * BLOCK, BLOCK), BLOCK), quarter_columns(q)],
+        lambda side, place, k: slots.at[side, k], length // BLOCK, (line_send, line_recv), total, 2,
+    )
+
+    def part_copy(i):
+        columns = quarter_columns(line.order(i))
+        return pltpu.make_async_copy(part_o.at[:, columns], part.at[:, columns], part_sems.at[i])
+
+    load_rows = loads.start(rows_o, rows_slots.at[0])
+    part_copy(0).start()
 
     def rows_copy(i):
         return remote(
-            rows_own, rows_in.at[i - 1], rows_send.at[i - 1], rows_recv.at[i - 1], mp=(z + i) % n
+            rows_slots.at[0], rows_slots.at[i], rows_send.at[i - 1], rows_recv.at[i - 1], mp=(z + i) % n
         )
+
+    load_rows.wait()
+    met()
+    for i in range(1, n):
+        rows_copy(i).start()
+    part_copy(0).wait()
+    line.inject(0)
+    line.inject(1)
+    for i in range(1, n):
+        part_copy(i).start()
+    load_gate, load_normed, load_xd = [
+        loads.start(source, target) for source, target in ((low_gate, v_gate), (normed, v_normed), (low_xd, v_xd))
+    ]
+    load_sums = [
+        loads.start(source, target)
+        for source, target in ((colacc, v_colacc), (csums, v_csums), (sums, v_sums), (dsums, v_dsums))
+    ]
+    own_columns = quarter_columns(z)
+    later = [
+        loads.start(source, target)
+        for source, target in (
+            (cot.at[:, own_columns], v_cot), (tok.at[:, own_columns], v_tok), (inverse, v_inverse),
+        )
+    ]
+
+    gain_width = features // 8
 
     def dp_copy(i):
         return remote(
             smalls, dp_in.at[i - 1], dp_send.at[i - 1], dp_recv.at[i - 1], dp=(ring.me + i) % size
         )
 
-    def bc_copy(i):
+    def mp_copy(i):
         return remote(
-            smalls.at[pl.ds(0, 8), pl.ds(inner, width - inner)], bc_in.at[i - 1],
+            smalls.at[:, pl.ds(inner, width - inner + gain_width)], mp_in.at[i - 1],
             mp_send.at[i - 1], mp_recv.at[i - 1], mp=(z + i) % n,
         )
 
-    def gain_copy(i):
-        return remote(
-            smalls.at[pl.ds(8, 8), pl.ds(0, inner)], gain_in.at[i - 1],
-            mp_send.at[n + i - 2], mp_recv.at[n + i - 2], mp=(z + i) % n,
-        )
-
+    for copy in load_sums:
+        copy.wait()
     smalls[...] = jnp.zeros_like(smalls)
     for k in range(CONV + 1):
-        smalls[k : k + 1, :] = jnp.sum(csums[8 * k : 8 * k + 8, :], axis=0, keepdims=True)
+        smalls[k : k + 1, :width] = jnp.sum(v_csums[8 * k : 8 * k + 8, :], axis=0, keepdims=True)
     for k in range(2):
-        smalls[CONV + 1 + k : CONV + 2 + k, :inner] = jnp.sum(sums[8 * k : 8 * k + 8, :], axis=0, keepdims=True)
-        smalls[7:8, k * LANES : (k + 1) * LANES] = jnp.sum(dsums[8 * k : 8 * k + 8, :], axis=0, keepdims=True)
-    for k in range(features // inner):
-        smalls[8 + k : 9 + k, :inner] = jnp.sum(colacc[:, k * inner : (k + 1) * inner], axis=0, keepdims=True)
-    for i in range(1, n):
-        rows_copy(i).start()
+        smalls[CONV + 1 + k : CONV + 2 + k, :inner] = jnp.sum(v_sums[8 * k : 8 * k + 8, :], axis=0, keepdims=True)
+        smalls[7:8, k * LANES : (k + 1) * LANES] = jnp.sum(v_dsums[8 * k : 8 * k + 8, :], axis=0, keepdims=True)
+    for k in range(8):
+        columns = slice(k * gain_width, (k + 1) * gain_width)
+        smalls[k : k + 1, width:] = jnp.sum(v_colacc[:, columns], axis=0, keepdims=True)
     for i in range(1, size):
         dp_copy(i).start()
-
-    later[0].wait()
     shard = dwz.shape[0]
     z_scatter = Scatter(
         ring, lambda r: z_grads.at[pl.ds(pl.multiple_of(r * shard, shard), shard), :], z_cores, z_parts, z_wholes,
@@ -1299,15 +1348,20 @@
             for at, w in tiles(grads.shape[1], 512):
                 grads[rows, at : at + w] = mm_tn(left, right[:, at : at + w]).astype(bf16)
 
+    load_gate.wait()
+    load_normed.wait()
+
     def z_weight(j, carry):
         weight(j, v_gate, z_grads)
         z_scatter.start(j)
         return carry
 
     lax.fori_loop(0, 4, z_weight, 0)
-    line.inject(4)
-    line.forward(1, 1)
-    line.forward(0, 2)
+    for i in range(1, n):
+        part_copy(i).wait()
+    line.inject(2)
+    line.forward(0, 1)
+    load_xd.wait()
 
     def x_weight(j, carry):
         weight(j, v_xd, x_grads)
@@ -1319,37 +1373,58 @@
 
         @pl.when(j % 2 == 1)
         def _():
-            line.inject(5 + j // 2)
-            line.forward(2 + j // 2, 1)
+            line.inject(3 + j // 2)
+            line.forward(1 + j // 2, 1)
 
         return carry
 
     lax.fori_loop(0, 4, x_weight, 0)
+    line.forward(0, 2)
+    z_scatter.second()
+    line.inject(5)
+    line.forward(3, 1)
     line.forward(1, 2)
     x_scatter.first()
-    z_scatter.second()
-    line.inject(7)
+    line.inject(6)
     line.forward(4, 1)
     line.forward(2, 2)
-
     for i in range(1, size):
         dp_copy(i).wait()
     smalls[...] += functools.reduce(lambda a, b: a + b, [dp_in[i] for i in range(size - 1)])
     for i in range(1, n):
-        bc_copy(i).start()
-        gain_copy(i).start()
-    x_scatter.second()
-    line.inject(8)
+        mp_copy(i).start()
+    line.inject(7)
     line.forward(5, 1)
     line.forward(3, 2)
     z_scatter.finish(dwz)
     store_z = loads.start(dwz, dwz_o)
+    x_scatter.second()
+    line.inject(8)
+    line.forward(6, 1)
     line.inject(9)
-    line.forward(6, 1)
+    line.forward(7, 1)
+    x_scatter.finish(dwxd)
+
+    bc_turned[...] = dwxd[:, inner:width].T
+    bc_own[...] = bc_turned[...].astype(bf16)
+
+    def weight_copy(i):
+        other = (z + i) % n
+        return remote(
+            bc_own.at[pl.ds(pl.multiple_of(other * per, per), per), :], bc_slots.at[i - 1],
+            bc_send.at[i - 1], bc_recv.at[i - 1], mp=other,
+        )
+
+    for i in range(1, n):
+        weight_copy(i).start()
     line.inject(10)
-    line.forward(7, 1)
+    store_x = loads.start(dwxd.at[:, pl.ds(0, inner)], dwx_o)
+    dwdt[...] = dwxd[:, width:].T[:heads]
+    for i in range(1, n):
+        rows_copy(i).wait()
+        mp_copy(i).wait()
     line.inject(11)
-    x_scatter.finish(dwxd)
+    smalls[:, inner:] += functools.reduce(lambda a, b: a + b, [mp_in[i] for i in range(n - 1)])
     share = LANES // per
 
     def mine(v):
@@ -1357,26 +1432,6 @@
         which = jnp.full(v.shape, z % share, jnp.int32)
         return functools.reduce(lambda a, k: jnp.where(which == k, turns[k], a), range(1, share), turns[0])
 
-    for j in range((width - inner) // LANES):
-        bc_own[j] = dwxd[:, inner + j * LANES : inner + (j + 1) * LANES].astype(bf16)
-
-    def weight_copy(i):
-        other = (z + i) % n
-        return remote(
-            bc_own.at[other // share], bc_slots.at[i - 1], bc_send.at[i - 1], bc_recv.at[i - 1], mp=other
-        )
-
-    for i in range(1, n):
-        weight_copy(i).start()
-    for i in range(1, n):
-        rows_copy(i).wait()
-        bc_copy(i).wait()
-        gain_copy(i).wait()
-    rows_own[...] += functools.reduce(lambda a, b: a + b, [rows_in[i] for i in range(n - 1)])
-    smalls[0:8, inner:] += functools.reduce(lambda a, b: a + b, [bc_in[i] for i in range(n - 1)])
-    smalls[8:16, :inner] += functools.reduce(lambda a, b: a + b, [gain_in[i] for i in range(n - 1)])
-    store_x = loads.start(dwxd.at[:, pl.ds(0, inner)], dwx_o)
-    dwdt[...] = dwxd[:, width:].T[:heads]
     lanes = pl.ds(pl.multiple_of(inner + (z // share) * LANES, LANES), LANES)
     conv_x[...] = smalls[:CONV, :inner]
     conv_x_bias[...] = smalls[CONV : CONV + 1, :inner]
@@ -1388,29 +1443,42 @@
     d_skip[...] = gather_heads(smalls[0:8, :inner], spread[...])[6:7, :heads]
     dt_bias[...] = smalls[7:8, :heads]
     a_rate[...] = smalls[7:8, LANES : LANES + heads]
-    fits = inner // own
-    in_gain[...] = smalls[pl.ds(8 + z // fits, 1), pl.ds(pl.multiple_of((z % fits) * own, own), own)]
-    later[1].wait()
+    rows_own = own // gain_width
+    for k in range(rows_own):
+        in_gain[:, k * gain_width : (k + 1) * gain_width] = smalls[
+            pl.ds(z * rows_own + k, 1), width : width + gain_width
+        ]
+    for copy in later:
+        copy.wait()
+    means = functools.reduce(lambda a, b: a + b, [rows_slots[i] for i in range(n)]) / features
+    rows_slots[0] = means
 
     def last(t, carry):
         line.finish(t)
         rows = line.rows(t)
-        mean = jnp.broadcast_to(rows_own[0:1, rows] / features, (LANES, BLOCK)).T
+        lines = BLOCK // LANES
+        row = jnp.concatenate([rows_slots[0, pl.ds(t * lines + j, 1), :] for j in range(lines)], axis=1)
+        turned[...] = jnp.broadcast_to(row, turned.shape)
+        mean = turned[...].T
         for c in range(0, own, LANES):
-            columns = pl.ds(pl.multiple_of(z * own + c, LANES), LANES)
-            hat = v_tok[rows, columns].astype(f32) * inverse[rows, :]
-            change = inverse[rows, :] * (total[:, c : c + LANES] * gain[:, columns] - hat * mean)
-            grad[rows, c : c + LANES] = (v_cot[rows, c : c + LANES].astype(f32) + change).astype(bf16)
+            columns = slice(c, c + LANES)
+            hat = v_tok[rows, columns].astype(f32) * v_inverse[rows, :]
+            gain_here = gain[:, pl.ds(pl.multiple_of(z * own + c, LANES), LANES)]
+            change = v_inverse[rows, :] * (total[:, columns] * gain_here - hat * mean)
+            grad[rows, columns] = (v_cot[rows, columns].astype(f32) + change).astype(bf16)
         return carry
 
     lax.fori_loop(0, line.blocks, last, 0)
+    store_grad = loads.start(grad, grad_o)
     for i in range(1, n):
         weight_copy(i).wait()
-    here = functools.reduce(lambda a, b: a + b, [bc_slots[i].astype(f32) for i in range(n - 1)], dwxd[:, lanes])
-    dwbc[...] = mine(here).T[:per]
+    dwbc[...] = functools.reduce(
+        lambda a, b: a + b, [bc_slots[i].astype(f32) for i in range(n - 1)],
+        bc_turned[pl.ds(pl.multiple_of(z * per, per), per), :],
+    )
     line.drain()
-    store_z.wait()
-    store_x.wait()
+    for copy in (store_z, store_x, store_grad):
+        copy.wait()
 
 
 def hand_on_kernel(*refs):
@@ -1590,22 +1658,23 @@
         return v[None, :]
 
     (
-        normed, _, wxd, wz, low_gate, low_xd, output, w_out_grad, inverse, csums, dsums, sums,
+        normed, _, _, _, low_gate, low_xd, output, w_out_grad, inverse, part, csums, dsums, sums, rows, colacc,
     ) = call(
         trunk_kernel,
         [
             ((T, D), bf16), ((T + 8, width), f32), ((D, wide), bf16), ((D, inner), bf16), ((T, inner), bf16),
-            ((T, wide), bf16), ((T, own), bf16), ((inner, columns), f32), ((T, LANES), f32),
-            ((8 * CONV + 8, width), f32), ((16, LANES), f32), ((16, inner), f32),
+            ((T, wide), bf16), ((T, own), bf16), ((inner, columns), f32), ((T, LANES), f32), ((T, D), bf16),
+            ((8 * CONV + 8, width), f32), ((16, LANES), f32), ((16, inner), f32), ((T // LANES, LANES), f32),
+            ((8, D), f32),
         ],
         [
             ((T, D), bf16), ((inner, columns), f32), ((T, D), bf16), ((T + 8, width), f32),
-            ((T + 8, width), f32), ((T, width), bf16), ((T, inner), bf16), ((T, inner), bf16),
+            ((T + 8, width), f32), ((T, width), bf16), ((2 * T, inner), bf16),
             ((blocks, STATE, inner), bf16), ((D, wide), bf16), ((D, inner), bf16), ((inner, D), bf16),
             ((T, pair), bf16), ((T, LANES), bf16), ((T, LANES), bf16), ((T, LANES), f32),
             ((8, width), f32), ((8, inner), f32), ((8, LANES), f32),
-            ((group, shard, LANES), bf16), ((group, 8, LANES), f32), ((group, 8, T), f32), ((group, 8, T), f32),
-            ((T, LANES), f32), ((LANES, BLOCK), f32),
+            ((group, shard, LANES), bf16), ((group, 8, LANES), f32), ((group, T // LANES, LANES), f32),
+            ((group, T // LANES, LANES), f32), ((T, LANES), f32), ((LANES, BLOCK), f32),
             ((T, LANES), jnp.int32), ((T, LANES), jnp.int32), ((LANES, inner), bf16), ((T, LANES), f32),
             ((STATE, inner), f32), ((BLOCK, inner), bf16), ((BLOCK, inner), f32), ((BLOCK, BLOCK), f32),
             ((BLOCK, BLOCK), f32), ((2 * blocks, BLOCK, own), bf16),
@@ -1615,11 +1684,11 @@
         row(conv_bc_bias), row(dt_bias), row(a_rate), row(d_skip), row(input_norm_gain), row(out_gain),
         places="s" + "a" * 5 + "v" * 11,
         sems=[
-            (7,), (9,), (4, 4), (4, 4), (4, 4), (4, 4), (4 * group - 4,), (4 * group - 4,),
+            (13,), (10,), (group,), (group, 2), (4, 4), (4, 4), (4, 4), (4, 4), (4 * group - 4,), (4 * group - 4,),
             (2, messages), (2, messages), (4,), (4,), (4,), (4,),
         ],
         collective=0,
-        far=9,
+        far=10,
     )
     w_z_grad, w_x_grad, input_grad, w_bc_grad, w_dt_grad, *small_grads = call(
         input_kernel,
@@ -1629,25 +1698,26 @@
             ((1, heads), f32), ((1, heads), f32), ((1, heads), f32), ((1, own), f32), ((1, inner), f32),
         ],
         [
-            ((shard, inner), f32), ((shard, wide), f32), ((16, width), f32), ((LANES, inner), bf16),
-            ((pair // LANES, shard, LANES), bf16), ((group - 1, shard, LANES), bf16),
-            ((T, D), bf16), ((T, D), bf16), ((T, inner), bf16), ((T, wide), bf16), ((D, inner), bf16),
-            ((D, wide), bf16), ((T, own), bf16),
+            ((shard, inner), f32), ((shard, wide), f32), ((T, own), bf16), ((8, width + D // 8), f32),
+            ((LANES, inner), bf16), ((pair, shard), f32), ((pair, shard), bf16), ((group - 1, per, shard), bf16),
+            ((T, LANES), f32), ((T, D), bf16), ((T, inner), bf16), ((T, wide), bf16), ((T, own), bf16),
+            ((T, own), bf16), ((8, D), f32), ((8 * CONV + 8, width), f32), ((16, inner), f32), ((16, LANES), f32),
             ((T, D), bf16), ((2, messages, BLOCK, own), bf16), ((BLOCK, own), f32),
             ((D, inner), bf16), ((4, shard, inner), bf16), ((2, shard // 2, inner), bf16), ((2, shard, inner), bf16),
             ((D, wide), bf16), ((4, shard, wide), bf16), ((2, shard // 2, wide), bf16), ((2, shard, wide), bf16),
-            ((T, LANES), f32), ((8, T), f32), ((group - 1, 8, T), f32), ((8, D), f32),
-            ((size - 1, 16, width), f32), ((group - 1, 8, pair), f32), ((group - 1, 8, inner), f32),
+            ((group, T // LANES, LANES), f32), ((size - 1, 8, width + D // 8), f32),
+            ((group - 1, 8, pair + D // 8), f32), ((LANES, BLOCK), f32),
         ],
-        0, tokens, inverse, row(input_norm_gain), normed, low_gate, low_xd, wz, wxd, cotangent, csums, sums, dsums,
-        places="avvaaaaaavvv",
+        0, tokens, inverse, row(input_norm_gain), normed, low_gate, low_xd, part, cotangent, rows, colacc, csums,
+        sums, dsums,
+        places="aav" + "a" * 10,
         sems=[
-            (6,), (group, 3), (2, messages), (2, messages), (4,), (4,), (4,), (4,), (4,), (4,), (4,), (4,),
-            (group - 1,), (group - 1,), (size - 1,), (size - 1,), (2 * group - 2,), (2 * group - 2,),
+            (14,), (group,), (2, messages), (2, messages), (4,), (4,), (4,), (4,), (4,), (4,), (4,), (4,),
+            (group - 1,), (group - 1,), (size - 1,), (size - 1,), (group - 1,), (group - 1,),
             (group - 1,), (group - 1,),
         ],
         collective=2,
-        far=2,
+        far=3,
     )
     (
         output, input_grad, w_z_grad, w_x_grad, w_bc_grad, w_dt_grad, w_out_grad, conv_x_grad, conv_x_bias_grad,

time: 240 us -> 227 us (0.946)
  Pallas kernels: 239 us -> 224 us
    pallas_call x3, Pallas kernels: 239 us -> 224 us  [call(): pl.pallas_call(kernel, out_shape=[jax.ShapeDtypeStruct(shape, kind) for s...]
where the time goes in v6:
time: 227 us; the launch traced here: 225 us
  Pallas kernels  224 us (99%)
    pallas_call x3, Pallas kernels, call(): pl.pallas_call(kernel, out_shape=[jax.ShapeDtypeStruct(shape, kind) for s...  224 us

profile of v6, /device:TPU:0, one launch (start us, length us, event | category | flops | bytes accessed | tf_op | source)
XLA Modules:
  0.0 225.2 jit_solution(6168542975836610556)
XLA Ops:
  0.7 143.1 %shard_map.288 = (bf16[1024,2048]{1,0:T(8,128)(2,1)}, f32[1032,1280]{1,0:T(8,128)}, bf16[2048,1408]{1,0:T(8,128)(2,1)}, bf16[2048,1024]{1,0:T(8,128)(2,1)}, bf16...) custom-call(s32[1,5]{1,0:T(1,128)} %lengths.1, ...), custom_call_target="tpu_custom_call" | custom-call | tf_op jit(solution)/shard_map/pallas_call | solution.py:1512
  143.8 76.5 %shard_map.289 = (f32[256,1024]{1,0:T(8,128)}, f32[256,1024]{1,0:T(8,128)}, bf16[1024,512]{1,0:T(8,128)(2,1)}, f32[64,256]{1,0:T(8,128)}, f32[16,256]{1,0:T(8,12...) custom-call(bf16[1024,2048]{1,0:T(8,128)(2,1)} %tok.3, ...), custom_call_target="tpu_custom_call" | custom-call | tf_op jit(solution)/shard_map/pallas_call | solution.py:1512
  220.3 4.7 %shard_map.290 = (bf16[1024,512]{1,0:T(8,128)(2,1)}, bf16[1024,512]{1,0:T(8,128)(2,1)}, f32[256,1024]{1,0:T(8,128)}, f32[256,1024]{1,0:T(8,128)}, f32[64,256]{1,...) custom-call(bf16[1024,512]{1,0:T(8,128)(2,1)} %get-tuple-element.58., ...), custom_call_target="tpu_custom_call" | custom-call | tf_op jit(solution)/shard_map/pallas_call | solution.py:1512

commit v7 on v6

--- a/solution.py
+++ b/solution.py
@@ -766,9 +766,8 @@
 
     def ring_copy(self, k, source):
         ring = self.ring
-        piece = self.shard(source)
-        if k >= 2:
-            piece = piece.at[pl.ds((k - 2) * self.half, self.half), :]
+        half = (0, 1, 1, 0, 0, 1)[k]
+        piece = self.shard(source).at[pl.ds(half * self.half, self.half), :]
         return remote(
             piece, piece, self.ring_send.at[k], self.ring_recv.at[k], dp=(ring.right, ring.left)[k % 2]
         )
@@ -780,23 +779,28 @@
 
     def start(self):
         me = self.ring.me
-        self.ring_copy(0, me).start()
-        self.ring_copy(1, me).start()
+        for k in range(4):
+            self.ring_copy(k, me).start()
         self.core_copy(0, me).start()
 
     def second(self):
         left, right = self.ring.left, self.ring.right
         self.ring_copy(0, left).wait_recv()
-        self.ring_copy(2, left).start()
+        self.ring_copy(4, left).start()
+        self.ring_copy(1, right).wait_recv()
+        self.ring_copy(5, right).start()
+
+    def beside(self):
+        left, right = self.ring.left, self.ring.right
+        self.ring_copy(2, left).wait_recv()
         self.core_copy(1, left).start()
-        self.ring_copy(1, right).wait_recv()
-        self.ring_copy(3, right).start()
+        self.ring_copy(3, right).wait_recv()
         self.core_copy(2, right).start()
 
     def third(self):
         across = self.ring.across
-        self.ring_copy(2, across).wait_recv()
-        self.ring_copy(3, across).wait_recv()
+        self.ring_copy(4, across).wait_recv()
+        self.ring_copy(5, across).wait_recv()
         self.core_copy(3, across).start()
 
     def arrived(self, k):
@@ -806,7 +810,7 @@
 
     def drain(self):
         ring = self.ring
-        for k, source in enumerate((ring.me, ring.me, ring.left, ring.right)):
+        for k, source in enumerate((ring.me, ring.me, ring.me, ring.me, ring.left, ring.right)):
             self.ring_copy(k, source).wait_send()
         for k, source in enumerate((ring.me, ring.left, ring.right, ring.across)):
             self.core_copy(k, source).wait_send()
@@ -825,15 +829,17 @@
     lengths, tok, cot, w_x, w_z, w_out, w_bc, w_dt, conv_x, conv_x_bias, conv_bc, conv_bc_bias, dt_bias, a_rate,
     d_skip, gain, out_gain,
     normed_o, xin_o, wxd_o, wz_o, low_gate_o, low_xd_o, out_o, dwout_o, inverse_o, part_o,
-    csums, dsums, sums, rows_o, colacc,
-    v_tok, stage_b, normed, xin, first_wide, slope, both, states, wxd, wz, wout,
+    csums_o, dsums_o, sums_o, rows_o, colacc_o,
+    csums, dsums, sums, rows, colacc, v_tok, stage_b, normed, xin, first_wide, slope, both, states, wxd, wz, wout,
     bc_low, step_low, decay_low, inverse_out, taps, crow, dpar,
     bc_slots, tap_slots, row_slots, cross_slots, stat, turned,
     pos, rpos, spread, dtin, state, xs, wide, cbm, acc, near, cores, parts, wholes,
-    load_sems, store_sems, token_sems, part_sems, ring_send, ring_recv, core_send, core_recv, mp_send, mp_recv, line_send, line_recv,
+    load_sems, store_sems, token_sems, part_sems, out_sems, ring_send, ring_recv, core_send, core_recv, mp_send, mp_recv, line_send, line_recv,
     scatter_core_send, scatter_core_recv, scatter_ring_send, scatter_ring_recv,
 ):
     ring = Ring()
+    loads, stores = Loads(load_sems), Loads(store_sems)
+    load_x = loads.start(w_x, wide)
     met = greet(ring, False)
     n, z = lax.axis_size("mp"), lax.axis_index("mp")
     length, features = normed.shape
@@ -844,8 +850,6 @@
     own = features // n
     shard, column_shard = stage_a.shape[0], stage_b.shape[1]
     heads, per = w_dt.shape[0], w_bc.shape[0]
-    loads, stores = Loads(load_sems), Loads(store_sems)
-    load_x = loads.start(w_x, stage_a)
     load_tok = loads.start(tok, v_tok)
     load_out = loads.start(w_out, stage_b)
     starts = [jnp.int32(0)]
@@ -947,10 +951,12 @@
 
         lax.fori_loop(0, length // 512, body, 0)
 
+    get_x.second()
     project_chip(0, ring.me)
-    get_x.second()
+    get_x.beside()
     get_bd.second()
     get_z.start()
+    get_bd.beside()
     project_chip(1, ring.left)
     project_chip(2, ring.right)
     get_x.third()
@@ -964,7 +970,11 @@
     get_out.start()
 
     def forward_tick(b):
-        @pl.when(b == 1)
+        @pl.when(b == 0)
+        def _():
+            get_z.beside()
+
+        @pl.when(b == 3)
         def _():
             get_z.third()
 
@@ -977,6 +987,7 @@
     gnorm = xin.at[pl.ds(0, length), pl.ds(0, inner)]
     project_rows(normed, wz, gate)
     store_wz = stores.start(wz, wz_o)
+    get_out.second()
     gate_squares(gate, ssd, x_low, crow, stat)
 
     def put_rows(target):
@@ -1004,7 +1015,8 @@
     store_xin.wait()
 
     def back_chip(k, source):
-        get_out.arrived(k)
+        if k < 3:
+            get_out.arrived(k)
         part = pl.ds(pl.multiple_of((source // 2) * 2 * column_shard, 2 * column_shard), 2 * column_shard)
 
         def body(i, carry):
@@ -1020,8 +1032,8 @@
 
         lax.fori_loop(0, length // 512, body, 0)
 
-    get_out.second()
     back_chip(0, ring.me)
+    get_out.beside()
     back_chip(1, ring.left)
     back_chip(2, ring.right)
     for i in range(1, n):
@@ -1032,14 +1044,10 @@
     store_normed.wait()
     gn = normed.at[:, pl.ds(0, inner)]
     gs = normed.at[:, pl.ds(inner, inner)]
-    gate_norm(gate, ssd, x_low, inverse_out, crow, gn)
-    back_chip(3, ring.across)
-    cross_sums(gnorm, gn, stat)
-    put_rows(cross_slots.at[0])
-    for i in range(1, n):
-        exchange(3, i).start()
     get_z.drain()
     store_wz.wait()
+    gate_norm(gate, ssd, x_low, inverse_out, crow, gn)
+    get_out.arrived(3)
 
     fold_columns = inner // own
 
@@ -1071,8 +1079,14 @@
 
         return carry
 
-    lax.fori_loop(0, n, quarter, 0)
+    quarter(0, 0)
+    back_chip(3, ring.across)
+    cross_sums(gnorm, gn, stat)
+    put_rows(cross_slots.at[0])
+    for i in range(1, n):
+        exchange(3, i).start()
     line.inject(2)
+    lax.fori_loop(1, n, quarter, 0)
     line.inject(3)
     get_out.drain()
     grads = wout
@@ -1102,12 +1116,14 @@
     gate_backward(gate, ssd, x_low, gnorm, crow, stat, inner * n, None, low_gate, gs, sums, known=inverse_out)
     load_xin = loads.start(xin_o, xin)
     stores.start(low_gate, low_gate_o)
+    stores.start(sums, sums_o)
+    line.inject(5)
     line.forward(1, 1)
     line.forward(0, 2)
     scatter.first()
 
     def scan_tick(i):
-        line.inject(i + 5)
+        line.inject(i + 6)
         line.forward(i + 2, 1)
 
         @pl.when(i < 3)
@@ -1152,11 +1168,12 @@
     def conv_tick(b):
         @pl.when(b % 2 == 1)
         def _():
-            line.inject(9 + b // 2)
+            line.inject(10 + b // 2)
             line.forward(6 + b // 2, 1)
 
     convolve_back(xin, gpre, taps, pos, rpos, xd, csums, conv_tick)
-    stores.start(xd, low_xd_o)
+    for source, target in ((xd, low_xd_o), (csums, csums_o), (dsums, dsums_o)):
+        stores.start(source, target)
     for copy in weight_loads:
         copy.wait()
     stat[...] = jnp.zeros_like(stat)
@@ -1184,13 +1201,13 @@
                 part_copy(jnp.maximum(i - 2, 0), h).wait()
 
         for r in range(0, length, 256):
-            rows = slice(r, r + 256)
-            here = mm_nt(low_gate[rows, :], both[columns, :])
-            here = here + mm_nt(xd[rows, :inner], wout[low, x_columns])
-            here = here + mm_nt(xd[rows, inner:], slope[low, bd_columns])
+            at = slice(r, r + 256)
+            here = mm_nt(low_gate[at, :], both[columns, :])
+            here = here + mm_nt(xd[at, :inner], wout[low, x_columns])
+            here = here + mm_nt(xd[at, inner:], slope[low, bd_columns])
             for h in range(2):
-                cores[(i % 2) * 2 + h, rows, :] = here[:, h * half : (h + 1) * half].astype(bf16)
-            along = here * (normed[rows, token_columns].astype(f32) * inverse_in[rows, :1])
+                cores[(i % 2) * 2 + h, at, :] = here[:, h * half : (h + 1) * half].astype(bf16)
+            along = here * (normed[at, token_columns].astype(f32) * inverse_in[at, :1])
             folded = fold(along)
             if r == 0:
                 colacc[:, columns] = folded
@@ -1200,7 +1217,7 @@
             sum_lanes = along[:, :LANES]
             for c in range(LANES, own, LANES):
                 sum_lanes = sum_lanes + along[:, c : c + LANES]
-            stat[rows, :] += sum_lanes
+            stat[at, :] += sum_lanes
         for h in range(2):
             part_copy(i, h).start()
 
@@ -1208,14 +1225,12 @@
         def _():
             token_copy(jnp.minimum(i + 2, n - 1)).start()
 
-        @pl.when(i == 0)
-        def _():
-            line.inject(11)
-
         return carry
 
     lax.fori_loop(0, n, grad_quarter, 0)
-    put_rows(rows_o)
+    put_rows(rows)
+    stores.start(rows, rows_o)
+    stores.start(colacc, colacc_o)
     load_own.wait()
 
     def last(t, carry):
@@ -1223,12 +1238,19 @@
         value = (token_own[line.rows(t), :].astype(f32) + total[...]).astype(bf16)
         for h in range(2):
             wholes[h, line.rows(t), :] = value[:, h * half : (h + 1) * half]
-        return carry
+            out_copy(t, h).start()
+        return carry
+
+    def out_copy(t, h):
+        return pltpu.make_async_copy(
+            wholes.at[h, line.rows(t), :], out_o.at[line.rows(t), pl.ds(h * half, half)], out_sems.at[t, h]
+        )
 
     lax.fori_loop(0, line.blocks, last, 0)
-    for h in range(2):
-        stores.start(wholes.at[h], out_o.at[:, pl.ds(h * half, half)])
     line.drain()
+    for t in range(line.blocks):
+        for h in range(2):
+            out_copy(t, h).wait()
     for i in range(2, n):
         for h in range(2):
             part_copy(i, h).wait()
@@ -1245,7 +1267,7 @@
     v_inverse, v_normed, v_gate, v_xd, v_cot, v_tok, v_colacc, v_csums, v_sums, v_dsums,
     part, slots, total, z_grads, z_cores, z_parts, z_wholes, x_grads, x_cores, x_parts, x_wholes,
     rows_slots, dp_in, mp_in, turned,
-    load_sems, part_sems, line_send, line_recv, z_core_send, z_core_recv, z_ring_send, z_ring_recv,
+    load_sems, part_sems, grad_sems, line_send, line_recv, z_core_send, z_core_recv, z_ring_send, z_ring_recv,
     x_core_send, x_core_recv, x_ring_send, x_ring_recv,
     rows_send, rows_recv, dp_send, dp_recv, mp_send, mp_recv, bc_send, bc_recv,
 ):
@@ -1266,7 +1288,7 @@
 
     line = Line(
         lambda t, q: part.at[pl.ds(pl.multiple_of(t * BLOCK, BLOCK), BLOCK), quarter_columns(q)],
-        lambda side, place, k: slots.at[side, k], length // BLOCK, (line_send, line_recv), total, 2,
+        lambda side, place, k: slots.at[side, k], length // BLOCK, (line_send, line_recv), total, 3,
     )
 
     def part_copy(i):
@@ -1403,6 +1425,7 @@
     line.forward(6, 1)
     line.inject(9)
     line.forward(7, 1)
+    line.inject(10)
     x_scatter.finish(dwxd)
 
     bc_turned[...] = dwxd[:, inner:width].T
@@ -1417,13 +1440,12 @@
 
     for i in range(1, n):
         weight_copy(i).start()
-    line.inject(10)
+    line.inject(11)
     store_x = loads.start(dwxd.at[:, pl.ds(0, inner)], dwx_o)
     dwdt[...] = dwxd[:, width:].T[:heads]
     for i in range(1, n):
         rows_copy(i).wait()
         mp_copy(i).wait()
-    line.inject(11)
     smalls[:, inner:] += functools.reduce(lambda a, b: a + b, [mp_in[i] for i in range(n - 1)])
     share = LANES // per
 
@@ -1466,10 +1488,13 @@
             gain_here = gain[:, pl.ds(pl.multiple_of(z * own + c, LANES), LANES)]
             change = v_inverse[rows, :] * (total[:, columns] * gain_here - hat * mean)
             grad[rows, columns] = (v_cot[rows, columns].astype(f32) + change).astype(bf16)
-        return carry
+        grad_copy(t).start()
+        return carry
+
+    def grad_copy(t):
+        return pltpu.make_async_copy(grad.at[line.rows(t), :], grad_o.at[line.rows(t), :], grad_sems.at[t])
 
     lax.fori_loop(0, line.blocks, last, 0)
-    store_grad = loads.start(grad, grad_o)
     for i in range(1, n):
         weight_copy(i).wait()
     dwbc[...] = functools.reduce(
@@ -1477,8 +1502,10 @@
         bc_turned[pl.ds(pl.multiple_of(z * per, per), per), :],
     )
     line.drain()
-    for copy in (store_z, store_x, store_grad):
+    for copy in (store_z, store_x):
         copy.wait()
+    for t in range(line.blocks):
+        grad_copy(t).wait()
 
 
 def hand_on_kernel(*refs):
@@ -1498,9 +1525,10 @@
 
 def hand_on(*arrays):
     kinds = [(v.shape, v.dtype) for v in arrays]
+    count = len(arrays)
     return call(
         hand_on_kernel, kinds, kinds, 0, *arrays,
-        places="a" * len(arrays), sems=[(len(arrays),)] * 2, far=len(arrays),
+        places="a" * len(arrays), sems=[(count,)] * 2, far=len(arrays),
     )
 
 
@@ -1668,6 +1696,8 @@
             ((8, D), f32),
         ],
         [
+            ((8 * CONV + 8, width), f32), ((16, LANES), f32), ((16, inner), f32), ((T // LANES, LANES), f32),
+            ((8, D), f32),
             ((T, D), bf16), ((inner, columns), f32), ((T, D), bf16), ((T + 8, width), f32),
             ((T + 8, width), f32), ((T, width), bf16), ((2 * T, inner), bf16),
             ((blocks, STATE, inner), bf16), ((D, wide), bf16), ((D, inner), bf16), ((inner, D), bf16),
@@ -1684,11 +1714,11 @@
         row(conv_bc_bias), row(dt_bias), row(a_rate), row(d_skip), row(input_norm_gain), row(out_gain),
         places="s" + "a" * 5 + "v" * 11,
         sems=[
-            (13,), (10,), (group,), (group, 2), (4, 4), (4, 4), (4, 4), (4, 4), (4 * group - 4,), (4 * group - 4,),
+            (13,), (13,), (group,), (group, 2), (blocks, 2), (4, 6), (4, 6), (4, 4), (4, 4), (4 * group - 4,), (4 * group - 4,),
             (2, messages), (2, messages), (4,), (4,), (4,), (4,),
         ],
         collective=0,
-        far=10,
+        far=15,
     )
     w_z_grad, w_x_grad, input_grad, w_bc_grad, w_dt_grad, *small_grads = call(
         input_kernel,
@@ -1712,7 +1742,7 @@
         sums, dsums,
         places="aav" + "a" * 10,
         sems=[
-            (14,), (group,), (2, messages), (2, messages), (4,), (4,), (4,), (4,), (4,), (4,), (4,), (4,),
+            (13,), (group,), (blocks,), (2, messages), (2, messages), (4,), (4,), (4,), (4,), (4,), (4,), (4,), (4,),
             (group - 1,), (group - 1,), (size - 1,), (size - 1,), (group - 1,), (group - 1,),
             (group - 1,), (group - 1,),
         ],

time: 227 us -> 222 us (0.978)
  Pallas kernels: 224 us -> 221 us
    pallas_call x3, Pallas kernels: 224 us -> 221 us  [call(): pl.pallas_call(kernel, out_shape=[jax.ShapeDtypeStruct(shape, kind) for s...]
where the time goes in v7:
time: 222 us
  Pallas kernels  221 us (100%)
    pallas_call x3, Pallas kernels, call(): pl.pallas_call(kernel, out_shape=[jax.ShapeDtypeStruct(shape, kind) for s...  221 us

profile of v7, /device:TPU:0, one launch (start us, length us, event | category | flops | bytes accessed | tf_op | source)
XLA Modules:
  0.0 221.6 jit_solution(950406112142832027)
XLA Ops:
  0.7 139.2 %shard_map.288 = (bf16[1024,2048]{1,0:T(8,128)(2,1)}, f32[1032,1280]{1,0:T(8,128)}, bf16[2048,1408]{1,0:T(8,128)(2,1)}, bf16[2048,1024]{1,0:T(8,128)(2,1)}, bf16...) custom-call(s32[1,5]{1,0:T(1,128)} %lengths.1, ...), custom_call_target="tpu_custom_call" | custom-call | tf_op jit(solution)/shard_map/pallas_call | solution.py:1540
  139.9 76.8 %shard_map.289 = (f32[256,1024]{1,0:T(8,128)}, f32[256,1024]{1,0:T(8,128)}, bf16[1024,512]{1,0:T(8,128)(2,1)}, f32[64,256]{1,0:T(8,128)}, f32[16,256]{1,0:T(8,12...) custom-call(bf16[1024,2048]{1,0:T(8,128)(2,1)} %tok.3, ...), custom_call_target="tpu_custom_call" | custom-call | tf_op jit(solution)/shard_map/pallas_call | solution.py:1540
  216.7 4.7 %shard_map.290 = (bf16[1024,512]{1,0:T(8,128)(2,1)}, bf16[1024,512]{1,0:T(8,128)(2,1)}, f32[256,1024]{1,0:T(8,128)}, f32[256,1024]{1,0:T(8,128)}, f32[64,256]{1,...) custom-call(bf16[1024,512]{1,0:T(8,128)(2,1)} %get-tuple-element.58., ...), custom_call_target="tpu_custom_call" | custom-call | tf_op jit(solution)/shard_map/pallas_call | solution.py:1540

commit v8 on v7

--- a/solution.py
+++ b/solution.py
@@ -828,9 +828,9 @@
 def trunk_kernel(
     lengths, tok, cot, w_x, w_z, w_out, w_bc, w_dt, conv_x, conv_x_bias, conv_bc, conv_bc_bias, dt_bias, a_rate,
     d_skip, gain, out_gain,
-    normed_o, xin_o, wxd_o, wz_o, low_gate_o, low_xd_o, out_o, dwout_o, inverse_o, part_o,
+    normed_o, xin_o, wx_o, wz_o, low_gate_o, low_xd_o, out_o, dwout_o, inverse_o, part_o,
     csums_o, dsums_o, sums_o, rows_o, colacc_o,
-    csums, dsums, sums, rows, colacc, v_tok, stage_b, normed, xin, first_wide, slope, both, states, wxd, wz, wout,
+    csums, dsums, sums, rows, colacc, v_tok, stage_b, normed, xin, first_wide, slope, both, states, wx, wbd, wz, wout,
     bc_low, step_low, decay_low, inverse_out, taps, crow, dpar,
     bc_slots, tap_slots, row_slots, cross_slots, stat, turned,
     pos, rpos, spread, dtin, state, xs, wide, cbm, acc, near, cores, parts, wholes,
@@ -848,6 +848,8 @@
     inverse = inverse_out
     inner, width = x_low.shape[1], xin.shape[1]
     own = features // n
+    pair = width - inner
+    bd_rows = pair + 32
     shard, column_shard = stage_a.shape[0], stage_b.shape[1]
     heads, per = w_dt.shape[0], w_bc.shape[0]
     load_tok = loads.start(tok, v_tok)
@@ -871,8 +873,10 @@
         return wout.at[:, pl.ds(pl.multiple_of(r * column_shard, column_shard), column_shard)]
 
     sems = [tuple(group.at[k] for group in (ring_send, ring_recv, core_send, core_recv)) for k in range(4)]
-    get_x = Gather(ring, rows_of(wxd, 0, inner), shard, sems[0])
-    get_bd = Gather(ring, rows_of(wxd, inner, wxd.shape[1]), shard, sems[1])
+    get_x = Gather(ring, rows_of(wx, 0, inner), shard, sems[0])
+    get_bd = Gather(
+        ring, lambda r: wbd.at[pl.ds(0, bd_rows), pl.ds(pl.multiple_of(r * shard, shard), shard)], bd_rows, sems[1]
+    )
     get_z = Gather(ring, rows_of(wz, 0, inner), shard, sems[2])
     get_out = Gather(ring, columns_of, inner, sems[3])
 
@@ -880,16 +884,14 @@
     cast_into(get_x.shard(ring.me), stage_a)
     met()
     get_x.start()
-    turned[...] = jnp.zeros_like(turned)
-    turned[:per, :] = w_bc[...]
-    bc_slots[0] = turned[...].T.astype(bf16)
+    bc_slots[0] = w_bc[...].astype(bf16)
     tap_slots[0] = jnp.zeros_like(tap_slots[0])
     tap_slots[0, :CONV, :per] = conv_bc[...]
     tap_slots[0, CONV : CONV + 1, :per] = conv_bc_bias[...]
-    turned[...] = jnp.zeros_like(turned)
-    turned[:heads, :] = w_dt[...]
-    own_rows = pl.ds(pl.multiple_of(ring.me * shard, shard), shard)
-    wxd[own_rows, width:] = turned[...].T.astype(bf16)
+    my_columns = pl.ds(pl.multiple_of(ring.me * shard, shard), shard)
+    wbd[pair : pair + heads, my_columns] = w_dt[...].astype(bf16)
+    wbd[pair + heads : bd_rows, my_columns] = jnp.zeros((bd_rows - pair - heads, shard), bf16)
+    wbd[bd_rows:, :] = jnp.zeros((wbd.shape[0] - bd_rows, features), bf16)
     dpar[...] = jnp.zeros_like(dpar)
     dpar[0:1, :heads] = dt_bias[...]
     dpar[1:2, :heads] = a_rate[...]
@@ -910,14 +912,14 @@
     for k in range(2):
         for i in range(1, n):
             exchange(k, i).wait()
-    first = lax.broadcasted_iota(jnp.int32, (shard, LANES), 1) < per
-    for j in range((width - inner) // LANES):
+    for m in range(n):
+        wbd[m * per : (m + 1) * per, my_columns] = bc_slots[(z - m + n) % n]
+    get_bd.start()
+    first = lax.broadcasted_iota(jnp.int32, (8, LANES), 1) < per
+    for j in range(pair // LANES):
         low, high = (z - 2 * j + n) % n, (z - 2 * j - 1 + n) % n
         columns = slice(inner + j * LANES, inner + (j + 1) * LANES)
-        pair = jnp.where(first, bc_slots[low].astype(f32), pltpu.roll(bc_slots[high].astype(f32), per, 1))
-        wxd[own_rows, columns] = pair.astype(bf16)
-        taps[:, columns] = jnp.where(first[:8], tap_slots[low], pltpu.roll(tap_slots[high], per, 1))
-    get_bd.start()
+        taps[:, columns] = jnp.where(first, tap_slots[low], pltpu.roll(tap_slots[high], per, 1))
     taps[:, :inner] = jnp.zeros((8, inner), f32)
     taps[:CONV, :inner] = conv_x[...]
     taps[CONV : CONV + 1, :inner] = conv_x_bias[...]
@@ -929,27 +931,27 @@
 
     def project_chip(k, source):
         get_x.arrived(k)
-        get_bd.arrived(k)
         part = pl.ds(pl.multiple_of((source // 2) * 2 * shard, 2 * shard), 2 * shard)
 
         def body(i, carry):
             at = pl.multiple_of(i * 512, 512)
             left = normed[pl.ds(at, 512), part]
-            for c, w in tiles(wxd.shape[1], 512):
-                here = mm(left, wxd[part, c : c + w])
-                w_x_part = min(w, width - c)
+            for c, w in tiles(inner, 512):
+                here = mm(left, wx[part, c : c + w])
                 if k == 0:
-                    xin[pl.ds(at + 8, 512), c : c + w_x_part] = here[:, :w_x_part]
+                    xin[pl.ds(at + 8, 512), c : c + w] = here
                 else:
-                    xin[pl.ds(at + 8, 512), c : c + w_x_part] += here[:, :w_x_part]
-                if w_x_part < w:
-                    if k == 0:
-                        dtin[pl.ds(at, 512), :] = here[:, w_x_part:]
-                    else:
-                        dtin[pl.ds(at, 512), :] += here[:, w_x_part:]
+                    xin[pl.ds(at + 8, 512), c : c + w] += here
             return carry
 
         lax.fori_loop(0, length // 512, body, 0)
+
+    def project_bd(i, carry):
+        at = pl.multiple_of(i * 512, 512)
+        here = mm_nt(normed[pl.ds(at, 512), :], wbd[...])
+        xin[pl.ds(at + 8, 512), inner:] = here[:, :pair]
+        dtin[pl.ds(at, 512), :] = here[:, pair:]
+        return carry
 
     get_x.second()
     project_chip(0, ring.me)
@@ -962,8 +964,11 @@
     get_x.third()
     get_bd.third()
     project_chip(3, ring.across)
+    store_wx = stores.start(wx, wx_o)
+    for i in range(4):
+        get_bd.arrived(i)
+    lax.fori_loop(0, length // 512, project_bd, 0)
     store_xin = stores.start(xin, xin_o)
-    store_wxd = stores.start(wxd, wxd_o)
     steps(dtin, dpar, None, None, step_low, decay_low)
     convolve(xin, taps, pos, slope, x_low, bc_low)
     get_z.second()
@@ -1008,7 +1013,7 @@
     put_rows(row_slots.at[0])
     get_x.drain()
     get_bd.drain()
-    store_wxd.wait()
+    store_wx.wait()
     for i in range(1, n):
         exchange(2, i).start()
     load_cot.wait()
@@ -1059,7 +1064,7 @@
         if place == 2:
             return near.at[k]
         row = pl.multiple_of((k // fold_columns) * BLOCK, BLOCK)
-        return wxd.at[pl.ds(row, BLOCK), pl.ds(pl.multiple_of((k % fold_columns) * own, own), own)]
+        return wx.at[pl.ds(row, BLOCK), pl.ds(pl.multiple_of((k % fold_columns) * own, own), own)]
 
     total = wide.at[:, pl.ds(0, own)]
     line = Line(piece, slot, length // BLOCK, (line_send, line_recv), total, 4)
@@ -1106,8 +1111,8 @@
     lax.fori_loop(0, 4, weight, 0)
     line.inject(4)
     line.forward(0, 1)
-    xd = v_tok.at[:, pl.ds(0, wxd.shape[1])]
-    token_own = v_tok.at[:, pl.ds(wxd.shape[1], own)]
+    xd = v_tok.at[:, pl.ds(0, width + LANES)]
+    token_own = v_tok.at[:, pl.ds(width + LANES, own)]
     load_own = loads.start(tok.at[:, pl.ds(pl.multiple_of(z * own, own), own)], token_own)
     for i in range(1, n):
         exchange(3, i).wait()
@@ -1139,13 +1144,7 @@
         starts, x_low, bc_low, step_low, decay_low, ssd, states, gs, slope, crow, dtin, None, dpar,
         gpre, xd, dsums, spread, state, xs, wide, cbm, acc, scan_tick,
     )
-    bd = wxd.shape[1] - inner
     weight_loads = [loads.start(wz_o, both)]
-    for h in range(2):
-        rows_here = pl.ds(h * length, length)
-        weight_loads.append(
-            loads.start(wxd_o.at[rows_here, pl.ds(inner, bd)], slope.at[:, pl.ds(h * bd, bd)])
-        )
     inverse_in = dtin
     weight_loads.append(loads.start(inverse_o, inverse_in))
 
@@ -1161,7 +1160,7 @@
     stores.start(stage_b, dwout_o)
     for h in range(2):
         weight_loads.append(
-            loads.start(wxd_o.at[pl.ds(h * length, length), pl.ds(0, inner)], wout.at[:, pl.ds(h * inner, inner)])
+            loads.start(wx_o.at[pl.ds(h * length, length), :], wout.at[:, pl.ds(h * inner, inner)])
         )
     load_xin.wait()
 
@@ -1191,7 +1190,6 @@
         low = pl.ds(pl.multiple_of((q % 2) * own, own), own)
         high = q // 2
         x_columns = pl.ds(pl.multiple_of(high * inner, inner), inner)
-        bd_columns = pl.ds(pl.multiple_of(high * bd, LANES), bd)
         token_columns = pl.ds(pl.multiple_of(inner + (i % 2) * own, own), own)
         token_copy(i).wait()
 
@@ -1204,7 +1202,7 @@
             at = slice(r, r + 256)
             here = mm_nt(low_gate[at, :], both[columns, :])
             here = here + mm_nt(xd[at, :inner], wout[low, x_columns])
-            here = here + mm_nt(xd[at, inner:], slope[low, bd_columns])
+            here = here + mm(xd[at, inner:], wbd[:, columns])
             for h in range(2):
                 cores[(i % 2) * 2 + h, at, :] = here[:, h * half : (h + 1) * half].astype(bf16)
             along = here * (normed[at, token_columns].astype(f32) * inverse_in[at, :1])
@@ -1255,14 +1253,15 @@
         for h in range(2):
             part_copy(i, h).wait()
     for copy in stores.pairs:
-        if not any(copy is done for done in (store_normed, store_inverse, store_xin, store_wxd, store_wz)):
+        if not any(copy is done for done in (store_normed, store_inverse, store_xin, store_wx, store_wz)):
             copy.wait()
 
 
 def input_kernel(
     tok, inverse, gain, normed, low_gate, low_xd, part_o, cot, rows_o, colacc, csums, sums, dsums,
-    dwz_o, dwx_o, grad_o, dwbc, dwdt, conv_x, conv_x_bias, conv_bc, conv_bc_bias, dt_bias, a_rate, d_skip, in_gain,
-    out_gain,
+    dwz_o, dwx_o, grad_o, dwbc_o, dwdt_o, conv_x_o, conv_x_bias_o, conv_bc_o, conv_bc_bias_o, dt_bias_o, a_rate_o,
+    d_skip_o, in_gain_o, out_gain_o,
+    dwbc, dwdt, conv_x, conv_x_bias, conv_bc, conv_bc_bias, dt_bias, a_rate, d_skip, in_gain, out_gain,
     dwz, dwxd, grad, smalls, spread, bc_turned, bc_own, bc_slots,
     v_inverse, v_normed, v_gate, v_xd, v_cot, v_tok, v_colacc, v_csums, v_sums, v_dsums,
     part, slots, total, z_grads, z_cores, z_parts, z_wholes, x_grads, x_cores, x_parts, x_wholes,
@@ -1470,6 +1469,20 @@
         in_gain[:, k * gain_width : (k + 1) * gain_width] = smalls[
             pl.ds(z * rows_own + k, 1), width : width + gain_width
         ]
+    for i in range(1, n):
+        weight_copy(i).wait()
+    dwbc[...] = functools.reduce(
+        lambda a, b: a + b, [bc_slots[i].astype(f32) for i in range(n - 1)],
+        bc_turned[pl.ds(pl.multiple_of(z * per, per), per), :],
+    )
+    small = [
+        loads.start(source, target)
+        for source, target in (
+            (dwbc, dwbc_o), (dwdt, dwdt_o), (conv_x, conv_x_o), (conv_x_bias, conv_x_bias_o), (conv_bc, conv_bc_o),
+            (conv_bc_bias, conv_bc_bias_o), (dt_bias, dt_bias_o), (a_rate, a_rate_o), (d_skip, d_skip_o),
+            (in_gain, in_gain_o), (out_gain, out_gain_o),
+        )
+    ]
     for copy in later:
         copy.wait()
     means = functools.reduce(lambda a, b: a + b, [rows_slots[i] for i in range(n)]) / features
@@ -1495,14 +1508,8 @@
         return pltpu.make_async_copy(grad.at[line.rows(t), :], grad_o.at[line.rows(t), :], grad_sems.at[t])
 
     lax.fori_loop(0, line.blocks, last, 0)
-    for i in range(1, n):
-        weight_copy(i).wait()
-    dwbc[...] = functools.reduce(
-        lambda a, b: a + b, [bc_slots[i].astype(f32) for i in range(n - 1)],
-        bc_turned[pl.ds(pl.multiple_of(z * per, per), per), :],
-    )
     line.drain()
-    for copy in (store_z, store_x):
+    for copy in (store_z, store_x, *small):
         copy.wait()
     for t in range(line.blocks):
         grad_copy(t).wait()
@@ -1690,7 +1697,7 @@
     ) = call(
         trunk_kernel,
         [
-            ((T, D), bf16), ((T + 8, width), f32), ((D, wide), bf16), ((D, inner), bf16), ((T, inner), bf16),
+            ((T, D), bf16), ((T + 8, width), f32), ((D, inner), bf16), ((D, inner), bf16), ((T, inner), bf16),
             ((T, wide), bf16), ((T, own), bf16), ((inner, columns), f32), ((T, LANES), f32), ((T, D), bf16),
             ((8 * CONV + 8, width), f32), ((16, LANES), f32), ((16, inner), f32), ((T // LANES, LANES), f32),
             ((8, D), f32),
@@ -1700,10 +1707,11 @@
             ((8, D), f32),
             ((T, D), bf16), ((inner, columns), f32), ((T, D), bf16), ((T + 8, width), f32),
             ((T + 8, width), f32), ((T, width), bf16), ((2 * T, inner), bf16),
-            ((blocks, STATE, inner), bf16), ((D, wide), bf16), ((D, inner), bf16), ((inner, D), bf16),
+            ((blocks, STATE, inner), bf16), ((D, inner), bf16), ((pair + LANES, D), bf16),
+            ((D, inner), bf16), ((inner, D), bf16),
             ((T, pair), bf16), ((T, LANES), bf16), ((T, LANES), bf16), ((T, LANES), f32),
             ((8, width), f32), ((8, inner), f32), ((8, LANES), f32),
-            ((group, shard, LANES), bf16), ((group, 8, LANES), f32), ((group, T // LANES, LANES), f32),
+            ((group, per, shard), bf16), ((group, 8, LANES), f32), ((group, T // LANES, LANES), f32),
             ((group, T // LANES, LANES), f32), ((T, LANES), f32), ((LANES, BLOCK), f32),
             ((T, LANES), jnp.int32), ((T, LANES), jnp.int32), ((LANES, inner), bf16), ((T, LANES), f32),
             ((STATE, inner), f32), ((BLOCK, inner), bf16), ((BLOCK, inner), f32), ((BLOCK, BLOCK), f32),
@@ -1728,6 +1736,9 @@
             ((1, heads), f32), ((1, heads), f32), ((1, heads), f32), ((1, own), f32), ((1, inner), f32),
         ],
         [
+            ((per, shard), f32), ((heads, shard), f32), ((CONV, inner), f32), ((1, inner), f32), ((CONV, per), f32),
+            ((1, per), f32), ((1, heads), f32), ((1, heads), f32), ((1, heads), f32), ((1, own), f32),
+            ((1, inner), f32),
             ((shard, inner), f32), ((shard, wide), f32), ((T, own), bf16), ((8, width + D // 8), f32),
             ((LANES, inner), bf16), ((pair, shard), f32), ((pair, shard), bf16), ((group - 1, per, shard), bf16),
             ((T, LANES), f32), ((T, D), bf16), ((T, inner), bf16), ((T, wide), bf16), ((T, own), bf16),
@@ -1742,12 +1753,12 @@
         sums, dsums,
         places="aav" + "a" * 10,
         sems=[
-            (13,), (group,), (blocks,), (2, messages), (2, messages), (4,), (4,), (4,), (4,), (4,), (4,), (4,), (4,),
+            (24,), (group,), (blocks,), (2, messages), (2, messages), (4,), (4,), (4,), (4,), (4,), (4,), (4,), (4,),
             (group - 1,), (group - 1,), (size - 1,), (size - 1,), (group - 1,), (group - 1,),
             (group - 1,), (group - 1,),
         ],
         collective=2,
-        far=3,
+        far=14,
     )
     (
         output, input_grad, w_z_grad, w_x_grad, w_bc_grad, w_dt_grad, w_out_grad, conv_x_grad, conv_x_bias_grad,

time: 222 us -> 221 us (level)
  no operation moved by 1% of the time
where the time goes in v8:
time: 221 us
  Pallas kernels  220 us (100%)
    pallas_call x3, Pallas kernels, call(): pl.pallas_call(kernel, out_shape=[jax.ShapeDtypeStruct(shape, kind) for s...  220 us

profile of v8, /device:TPU:0, one launch (start us, length us, event | category | flops | bytes accessed | tf_op | source)
XLA Modules:
  0.0 220.5 jit_solution(7468241333506914746)
XLA Ops:
  0.7 139.3 %shard_map.288 = (bf16[1024,2048]{1,0:T(8,128)(2,1)}, f32[1032,1280]{1,0:T(8,128)}, bf16[2048,1024]{1,0:T(8,128)(2,1)}, bf16[2048,1024]{1,0:T(8,128)(2,1)}, bf16...) custom-call(s32[1,5]{1,0:T(1,128)} %lengths.1, ...), custom_call_target="tpu_custom_call" | custom-call | tf_op jit(solution)/shard_map/pallas_call | solution.py:1547
  139.9 75.6 %shard_map.289 = (f32[256,1024]{1,0:T(8,128)}, f32[256,1024]{1,0:T(8,128)}, bf16[1024,512]{1,0:T(8,128)(2,1)}, f32[64,256]{1,0:T(8,128)}, f32[16,256]{1,0:T(8,12...) custom-call(bf16[1024,2048]{1,0:T(8,128)(2,1)} %tok.3, ...), custom_call_target="tpu_custom_call" | custom-call | tf_op jit(solution)/shard_map/pallas_call | solution.py:1547
  215.6 4.7 %shard_map.290 = (bf16[1024,512]{1,0:T(8,128)(2,1)}, bf16[1024,512]{1,0:T(8,128)(2,1)}, f32[256,1024]{1,0:T(8,128)}, f32[256,1024]{1,0:T(8,128)}, f32[64,256]{1,...) custom-call(bf16[1024,512]{1,0:T(8,128)(2,1)} %get-tuple-element.58., ...), custom_call_target="tpu_custom_call" | custom-call | tf_op jit(solution)/shard_map/pallas_call | solution.py:1547

commit v9 on v8

--- a/solution.py
+++ b/solution.py
@@ -1069,22 +1069,20 @@
     total = wide.at[:, pl.ds(0, own)]
     line = Line(piece, slot, length // BLOCK, (line_send, line_recv), total, 4)
 
-    def quarter(i, carry):
+    def quarter(i, carry, first_quarter=False):
         q = line.order(i)
         columns = pl.ds(pl.multiple_of(q * own, own), own)
-        for r in range(0, length, 512):
-            at = pl.ds(pl.multiple_of((q // fold_columns) * length + r, 512), 512)
+        tall = 256 if first_quarter else 512
+        for r in range(0, length, tall):
+            at = pl.ds(pl.multiple_of((q // fold_columns) * length + r, tall), tall)
             cols = pl.ds(pl.multiple_of((q % fold_columns) * own, own), own)
-            wz[at, cols] = mm(gn[r : r + 512, :], wout[:, columns]).astype(bf16)
-            if r == 0:
-                @pl.when(i == 0)
-                def _():
-                    line.inject(0)
-                    line.inject(1)
-
-        return carry
-
-    quarter(0, 0)
+            wz[at, cols] = mm(gn[r : r + tall, :], wout[:, columns]).astype(bf16)
+            if first_quarter and r < 512:
+                line.inject(r // 256)
+
+        return carry
+
+    quarter(0, 0, True)
     back_chip(3, ring.across)
     cross_sums(gnorm, gn, stat)
     put_rows(cross_slots.at[0])

time: 221 us -> 221 us (level)
  no operation moved by 1% of the time
where the time goes in v9:
time: 221 us; the launch traced here: 220 us
  Pallas kernels  219 us (99%)
    pallas_call x3, Pallas kernels, call(): pl.pallas_call(kernel, out_shape=[jax.ShapeDtypeStruct(shape, kind) for s...  219 us

profile of v9, /device:TPU:0, one launch (start us, length us, event | category | flops | bytes accessed | tf_op | source)
XLA Modules:
  0.0 220.2 jit_solution(5615720656071049299)
XLA Ops:
  0.7 139.0 %shard_map.288 = (bf16[1024,2048]{1,0:T(8,128)(2,1)}, f32[1032,1280]{1,0:T(8,128)}, bf16[2048,1024]{1,0:T(8,128)(2,1)}, bf16[2048,1024]{1,0:T(8,128)(2,1)}, bf16...) custom-call(s32[1,5]{1,0:T(1,128)} %lengths.1, ...), custom_call_target="tpu_custom_call" | custom-call | tf_op jit(solution)/shard_map/pallas_call | solution.py:1545
  139.7 75.6 %shard_map.289 = (f32[256,1024]{1,0:T(8,128)}, f32[256,1024]{1,0:T(8,128)}, bf16[1024,512]{1,0:T(8,128)(2,1)}, f32[64,256]{1,0:T(8,128)}, f32[16,256]{1,0:T(8,12...) custom-call(bf16[1024,2048]{1,0:T(8,128)(2,1)} %tok.3, ...), custom_call_target="tpu_custom_call" | custom-call | tf_op jit(solution)/shard_map/pallas_call | solution.py:1545
  215.3 4.7 %shard_map.290 = (bf16[1024,512]{1,0:T(8,128)(2,1)}, bf16[1024,512]{1,0:T(8,128)(2,1)}, f32[256,1024]{1,0:T(8,128)}, f32[256,1024]{1,0:T(8,128)}, f32[64,256]{1,...) custom-call(bf16[1024,512]{1,0:T(8,128)(2,1)} %get-tuple-element.58., ...), custom_call_target="tpu_custom_call" | custom-call | tf_op jit(solution)/shard_map/pallas_call | solution.py:1545
